TPU v7x, 256 devices: a whole 4x4x8 slice. The times are simulated.
256 devices in a mesh: kblk: 64 (over y, z, core), amp: 4 (over x).
Axes of the slice: x: 4, y: 4, z: 8, core: 2. Of those that a mesh axis runs over, the one named last changes fastest.
Arguments:
- integrals: bfloat16 [32768, 16384], P(('kblk', 'amp')), may hold values from -0.046875 to 0.046875
- row_owner: int32 [32768, 1], P(('kblk', 'amp')), may hold values from 0 to 63; in each aligned block of 128 rows (0 to 127, 128 to 255, ...) at most 4 rows name the same one
- lambda_amps: bfloat16 [64, 512, 16384], P('kblk', 'amp'), may hold values from -6 to 6
Outputs:
- ladder: float32 [32768, 512], P(('kblk', 'amp'))
Inputs may be any that keep to these rules, and one draw needn't show every extreme that they name: Among the 128 rows of one device (aligned blocks of row_owner), at most 4 name the same k-triple, and some k-triple is named by exactly 4 of them.
All inputs are finite; a program needn't handle non-finite values.
Results may differ from a plain program's by a relative error of at most 0.0003.
Values may be sent and summed in bfloat16 or wider, within the bound.
No kernel may reach another device: no remote copies, remote signals or barrier semaphores. Data moves between devices by JAX's collectives and lax.ppermute only.
A program may use at most 128 MiB of HBM per device.

v0:
```python
import jax
import jax.numpy as jnp
from jax import lax
from jax.sharding import PartitionSpec as P


def body(integrals, row_owner, lambda_amps):
    peers = lax.axis_size("kblk")
    rows_here = integrals.shape[0]
    capacity = 2 * rows_here // peers
    owner = row_owner[:, 0]
    onehot = (owner[:, None] == jnp.arange(peers, dtype=jnp.int32)[None, :]).astype(jnp.int32)
    earlier = jnp.cumsum(onehot, axis=0) - onehot
    slot_index = jnp.sum(earlier * onehot, axis=1)
    position = owner * capacity + slot_index
    source_row = (
        jnp.zeros((peers * capacity,), jnp.int32)
        .at[position]
        .set(jnp.arange(rows_here, dtype=jnp.int32))
    )
    occupied = jnp.zeros((peers * capacity,), jnp.int32).at[position].set(1) > 0
    picked = jnp.where(occupied[:, None], integrals[source_row], jnp.zeros((), jnp.bfloat16))
    outgoing = picked.reshape(peers, capacity, integrals.shape[1])
    whole_lambda = lax.all_gather(lambda_amps, "amp", axis=1, tiled=True)[0]
    arrived = lax.all_to_all(outgoing, "kblk", split_axis=0, concat_axis=0, tiled=True)
    flat = arrived.reshape(-1, arrived.shape[-1])
    values = lax.dot_general(
        flat, whole_lambda, (((1,), (1,)), ((), ())), preferred_element_type=jnp.float32
    )
    returned = lax.all_to_all(
        values.reshape(arrived.shape[0], arrived.shape[1], whole_lambda.shape[0]),
        "kblk",
        split_axis=0,
        concat_axis=0,
        tiled=True,
    )
    return returned.reshape(peers * capacity, whole_lambda.shape[0])[position]


def solution(mesh):
    placed = (P(("kblk", "amp"), None), P(("kblk", "amp"), None), P("kblk", "amp", None))
    return jax.shard_map(
        body, mesh=mesh, in_specs=placed, out_specs=P(("kblk", "amp"), None), check_vma=False
    )
```

profile of v0, /device:TPU:1, one launch (start us, length us, event | category | flops | bytes accessed | tf_op | source)
XLA Modules:
  0.0 308.3 jit_solution(13061345254896272995)
XLA Ops:
  6.5 0.0 all-gather.2.cloned.1.call-start
  6.5 0.7 all-gather.2.cloned.1.call-update
  7.3 0.7 fusion.3
  8.0 0.2 reduce_window_sum.11
  8.2 0.8 select_reduce_fusion
  9.0 0.7 fusion.4
  9.7 1.0 scatter_custom_fusion.1
  10.7 20.3 %gather_fusion = bf16[256,16384]{1,0:T(8,128)(2,1)} fusion(bf16[128,16384]{1,0:T(8,128)(2,1)} %param.3, s32[1024]{0:T(1024)S(1)} %pad_clamp_fusion.1), kind=kCustom, calls=%fused_computation | custom fusion | bytes 16778240 | tf_op jit(solution)/shard_map/gather | solution.py:22
  30.9 13.3 %gather.9 = bf16[64,4,16384]{2,1,0:T(4,128)(2,1)} reshape(bf16[256,16384]{1,0:T(8,128)(2,1)} %gather_fusion) | data formatting | bytes 16777216 | tf_op jit(solution)/shard_map/gather | solution.py:22
  44.3 1.0 scatter_custom_fusion
  45.3 0.1 broadcast_in_dim.26
  45.4 6.0 %broadcast_select_fusion = bf16[64,4,16384]{2,1,0:T(4,128)(2,1)S(1)} fusion(bf16[64,4,16384]{2,1,0:T(4,128)(2,1)} %gather.9, pred[64,4]{1,0:T(8,128)(4,1)S(1)} %broadcast_in_dim.26), kind=kLoop, calls=%fused_computation.7 | loop fusion | flops 4194304 | bytes 16777472 | tf_op jit(solution)/shard_map/jit(_where)/select_n | solution.py:22
  51.4 198.5 %all_to_all.10 = bf16[64,4,16384]{2,1,0:T(4,128)(2,1)} all-to-all(bf16[64,4,16384]{2,1,0:T(4,128)(2,1)S(1)} %broadcast_select_fusion), channel_id=1, replica_groups=mesh['kblk'=64,'amp'=4] {'kblk'}, dimensions={0} | all-to-all | bytes 16777216 | tf_op jit(solution)/shard_map/all_to_all | solution.py:25
  249.9 0.0 all-gather.2.cloned.1.call-done
  249.9 25.7 %fusion = f32[64,4,512]{2,0,1:T(8,128)S(1)} fusion(bf16[1,512,16384]{2,1,0:T(8,128)(2,1)} %all-gather.2.cloned.1.call-done, bf16[64,4,16384]{2,1,0:T(4,128)(2,1)} %all_to_all.10), kind=kOutput, calls=%fused_computation.4 | convolution fusion | flops 4294967296 | bytes 25690112 | tf_op jit(solution)/shard_map/dot_general | solution.py:27
  275.6 1.1 copy.8
  276.7 5.8 %all-to-all-start.1 = ((f32[64,4,512]{2,1,0:T(4,128)}), f32[64,4,512]{2,1,0:T(4,128)S(1)}, u32[]{:S(2)}, u32[]{:S(2)}) async-start(f32[64,4,512]{2,1,0:T(4,128)} %copy.8), calls=%async_computation.1 | async-start | bytes 1048576 | tf_op jit(solution)/shard_map/all_to_all | solution.py:30
  282.5 17.3 %all-to-all-done.1 = f32[64,4,512]{2,1,0:T(4,128)S(1)} async-done(((f32[64,4,512]{2,1,0:T(4,128)}), f32[64,4,512]{2,1,0:T(4,128)S(1)}, u32[]{:S(2)}, u32[]{:S(2)}) %all-to-all-start.1) | async-done | bytes 524320 | tf_op jit(solution)/shard_map/all_to_all | solution.py:30
  299.8 0.2 reshape.16
  300.0 1.5 gather_fusion.1
  (6 shorter events, 0.0 us)
Async XLA Ops:
  6.5 243.3 %all-gather.2.cloned.1.call-start = ((), (), s32[]{:S(2)}) async-start(), calls=%async_computation.2 | async-start | bytes 20971520 | tf_op jit(solution)/shard_map/all_gather | solution.py:24
  276.7 23.1 %all-to-all-start.1 = ((f32[64,4,512]{2,1,0:T(4,128)}), f32[64,4,512]{2,1,0:T(4,128)S(1)}, u32[]{:S(2)}, u32[]{:S(2)}) async-start(f32[64,4,512]{2,1,0:T(4,128)} %copy.8), calls=%async_computation.1 | async-start | bytes 1048576 | tf_op jit(solution)/shard_map/all_to_all | solution.py:30
Sparse Core Ops, SparseCore 0:
  9.2 160.4 all-gather.1
where the time goes:
time: 309 us; the launch traced here: 308 us
  blocking collectives  198 us (64%)
  local copies, waits for them, and re-layouts  38.4 us (12%)
  matrix products  25.7 us (8%)
  waiting for transfers between devices  18 us (6%)
  between operations  13.5 us (4%)
  other arithmetic  8.41 us (3%)
  starting transfers between devices  5.82 us (2%)
    all_to_all x1, blocking collectives, body(): lax.all_to_all(outgoing, 'kblk', split_axis=0, concat_axis=0, tiled=True)  198 us
    gather x2, local copies, waits for them, and re-layouts, body(): integrals[source_row]  33.6 us
    dot_general x1, matrix products, body(): lax.dot_general(flat, whole_lambda, (((1,), (1,)), ((), ())), preferred_e...  25.7 us
    all_to_all x1, waiting for transfers between devices, body(): lax.all_to_all(values.reshape(arrived.shape[0], arrived.shape[1], whole_l...  17.3 us
  transfers between devices with their start and end apart: 2, of which 1 were waited for; matrix products, arithmetic and copies ran while one was open for 14% of the time, Pallas kernels for 0%

commit v1 on v0

v1 whole, which is shorter than its diff:
```python
import jax
import jax.numpy as jnp
from jax import lax
from jax.experimental import pallas as pl
from jax.experimental.pallas import tpu as pltpu
from jax.sharding import PartitionSpec as P

CAP = 4
BLOCK = 2 * CAP
CHIPS = 32
VMEM = 48 * 1024 * 1024
SIBLING = [(k, k ^ 1) for k in range(2 * CHIPS)]
SAME_CORE = [[2 * chip + core for chip in range(CHIPS)] for core in range(2)]


def place_kernel(line_ref, mine_ref, theirs_ref, out_ref):
    lines = out_ref.shape[0]
    number = lax.broadcasted_iota(jnp.int32, (lines, line_ref.shape[1]), 0)
    pick = (number == line_ref[...]).astype(jnp.bfloat16)
    both = jnp.concatenate([mine_ref[...], theirs_ref[...]], axis=0)
    out_ref[...] = jnp.dot(pick, both, preferred_element_type=jnp.float32).astype(jnp.bfloat16)


def place(line, mine, theirs):
    rows, cols = mine.shape
    lines, block = CHIPS * BLOCK, min(2048, cols)
    return pl.pallas_call(
        place_kernel,
        grid=(cols // block,),
        in_specs=[
            pl.BlockSpec((1, 2 * rows), lambda i: (0, 0)),
            pl.BlockSpec((rows, block), lambda i: (0, i)),
            pl.BlockSpec((rows, block), lambda i: (0, i)),
        ],
        out_specs=pl.BlockSpec((lines, block), lambda i: (0, i)),
        out_shape=jax.ShapeDtypeStruct((lines, cols), jnp.bfloat16),
        compiler_params=pltpu.CompilerParams(vmem_limit_bytes=VMEM),
        cost_estimate=pl.CostEstimate(
            flops=4 * lines * rows * cols,
            bytes_accessed=2 * (2 * rows + lines) * cols,
            transcendentals=0,
        ),
        name="place",
    )(line, mine, theirs)


def multiply_kernel(rows_ref, amps_ref, out_ref):
    @pl.when(pl.program_id(0) == 0)
    def _():
        out_ref[...] = jnp.zeros_like(out_ref)

    out_ref[...] += lax.dot_general(
        rows_ref[...], amps_ref[...], (((1,), (1,)), ((), ())), preferred_element_type=jnp.float32
    )


def multiply(rows, amps):
    lines, cols = rows.shape
    pairs, block = amps.shape[0], min(2048, cols)
    return pl.pallas_call(
        multiply_kernel,
        grid=(cols // block,),
        in_specs=[
            pl.BlockSpec((lines, block), lambda i: (0, i)),
            pl.BlockSpec((pairs, block), lambda i: (0, i)),
        ],
        out_specs=pl.BlockSpec((lines, pairs), lambda i: (0, 0)),
        out_shape=jax.ShapeDtypeStruct((lines, pairs), jnp.float32),
        compiler_params=pltpu.CompilerParams(vmem_limit_bytes=VMEM),
        cost_estimate=pl.CostEstimate(
            flops=2 * lines * pairs * cols,
            bytes_accessed=2 * (lines + pairs) * cols + 4 * lines * pairs,
            transcendentals=0,
        ),
        name="multiply",
    )(rows, amps)


def body(integrals, row_owner, lambda_amps):
    peers = lax.axis_size("kblk")
    core = lax.axis_index("kblk") % 2
    rows_here, cols = integrals.shape
    theirs = lax.ppermute(integrals, "kblk", SIBLING)

    owner = row_owner[:, 0]
    number = jnp.arange(rows_here, dtype=jnp.int32)
    earlier = (owner[:, None] == owner[None, :]) & (number[None, :] < number[:, None])
    slot = jnp.sum(earlier.astype(jnp.int32), axis=1)
    line = (owner // 2) * BLOCK + core * CAP + slot
    stays = owner % 2 == core
    sent = lax.ppermute(jnp.where(stays, -1, line)[None, :], "kblk", SIBLING)
    lines = jnp.concatenate([jnp.where(stays, line, -1)[None, :], sent], axis=1)

    whole_lambda = lax.all_gather(lambda_amps, "amp", axis=1, tiled=True)[0]
    pairs = whole_lambda.shape[0]

    placed = place(lines, integrals, theirs)
    arrived = lax.all_to_all(
        placed.reshape(CHIPS, BLOCK, cols),
        "kblk",
        split_axis=0,
        concat_axis=0,
        axis_index_groups=SAME_CORE,
        tiled=True,
    )
    values = multiply(arrived.reshape(CHIPS * BLOCK, cols), whole_lambda)
    returned = lax.all_to_all(
        values.reshape(peers, CAP, pairs), "kblk", split_axis=0, concat_axis=0, tiled=True
    )
    return returned.reshape(peers * CAP, pairs)[owner * CAP + slot]


def solution(mesh):
    placed = (P(("kblk", "amp"), None), P(("kblk", "amp"), None), P("kblk", "amp", None))
    return jax.shard_map(
        body, mesh=mesh, in_specs=placed, out_specs=P(("kblk", "amp"), None), check_vma=False
    )
```

time: 309 us -> 270 us (0.87)
  local copies, waits for them, and re-layouts: 38.4 us -> 4.76 us
  matrix products: 25.7 us -> 0 us
  Pallas kernels: 0 us -> 21.4 us
  starting transfers between devices: 5.82 us -> 13 us
  other arithmetic: 8.41 us -> 2.26 us
  blocking collectives: 198 us -> 192 us
  waiting for transfers between devices: 18 us -> 22.8 us
    gather x3 -> x1, local copies, waits for them, and re-layouts: 35 us -> 1.45 us  [body(): return returned.reshape(peers * CAP, pairs)[owner * CAP + slot]]
    dot_general x1 -> x0, matrix products: 25.7 us -> none  [body(): lax.dot_general(flat, whole_lambda, (((1,), (1,)), ((), ())), preferred_e...]
    pallas_call x0 -> x2, Pallas kernels: none -> 21.4 us  [the longest x1 12.2 us: multiply(): pl.pallas_call(multiply_kernel, grid=(cols // block,), in_specs=[pl.Block...]
    all_to_all x1, blocking collectives: 198 us -> 192 us  [body(): lax.all_to_all(placed.reshape(CHIPS, BLOCK, cols), 'kblk', split_axis=0,...]
    select_n x3, other arithmetic: 6.66 us -> 1.35 us  [the longest x1 0.68 us: body(): lines = jnp.concatenate([jnp.where(stays, line, -1)[None, :], sent], axis=1)]
    ppermute x0 -> x2, waiting for transfers between devices: none -> 4.85 us  [the longest x1 4.51 us: body(): sent = lax.ppermute(jnp.where(stays, -1, line)[None, :], 'kblk', SIBLING)]
    all_to_all x1, starting transfers between devices: 5.81 us -> 9.63 us  [body(): lax.all_to_all(values.reshape(peers, CAP, pairs), 'kblk', split_axis=0, c...]
    ppermute x0 -> x2, starting transfers between devices: none -> 3.36 us  [the longest x1 3.33 us: body(): theirs = lax.ppermute(integrals, 'kblk', SIBLING)]
  transfers between devices with their start and end apart: 2 -> 4, of which waited for: 1 -> 3; matrix products, arithmetic and copies ran while one was open for 14% -> 1% of each run, Pallas kernels for 0% -> 3%
where the time goes in v1:
time: 270 us
  blocking collectives  192 us (71%)
  waiting for transfers between devices  22.8 us (8%)
  Pallas kernels  21.4 us (8%)
  between operations  13.4 us (5%)
  starting transfers between devices  13 us (5%)
  local copies, waits for them, and re-layouts  4.76 us (2%)
    all_to_all x1, blocking collectives, body(): lax.all_to_all(placed.reshape(CHIPS, BLOCK, cols), 'kblk', split_axis=0,...  192 us
    all_to_all x1, waiting for transfers between devices, body(): lax.all_to_all(values.reshape(peers, CAP, pairs), 'kblk', split_axis=0, c...  17.3 us
    pallas_call x1, Pallas kernels, multiply(): pl.pallas_call(multiply_kernel, grid=(cols // block,), in_specs=[pl.Block...  12.2 us
    all_to_all x1, starting transfers between devices, body(): lax.all_to_all(values.reshape(peers, CAP, pairs), 'kblk', split_axis=0, c...  9.63 us
    pallas_call x1, Pallas kernels, place(): pl.pallas_call(place_kernel, grid=(cols // block,), in_specs=[pl.BlockSpe...  9.13 us
  transfers between devices with their start and end apart: 4, of which 3 were waited for; matrix products, arithmetic and copies ran while one was open for 1% of the time, Pallas kernels for 3%

profile of v1, /device:TPU:1, one launch (start us, length us, event | category | flops | bytes accessed | tf_op | source)
XLA Modules:
  0.0 269.7 jit_solution(14332525261274829522)
XLA Ops:
  6.5 0.0 all-gather.2.cloned.1.call-start
  6.5 0.7 all-gather.2.cloned.1.call-update
  7.3 3.3 %collective-permute-start.1 = (bf16[128,16384]{1,0:T(8,128)(2,1)}, bf16[128,16384]{1,0:T(8,128)(2,1)}, u32[]{:S(2)}, u32[]{:S(2)}) collective-permute-start(bf16[128,16384]{1,0:T(8,128)(2,1)} %mine_ref.1), channel_id=1, source_target_pairs={{0,4},{4,0},{8,12},{12,8},{16,20},{20,16},{24,28},{28,24},{32,36},... | collective-permute-start | bytes 12582920 | tf_op jit(solution)/shard_map/ppermute | solution.py:83
  10.6 0.9 convert_reduce_fusion
  11.5 0.7 compare_select_fusion.5
  12.2 0.7 compare_select_fusion.4
  12.8 0.0 collective-permute-start
  12.9 4.5 %collective-permute-done = s32[1,128]{1,0:T(1,128)S(1)} collective-permute-done((s32[1,128]{1,0:T(1,128)S(1)}, s32[1,128]{1,0:T(1,128)S(1)}, u32[]{:S(2)}, u32[]{:S(2)}) %collective-permute-start) | collective-permute-done | bytes 544 | tf_op jit(solution)/shard_map/ppermute | solution.py:91
  17.4 0.3 collective-permute-done.1.theirs_ref
  17.7 0.0 copy-start
  17.7 2.2 copy-done
  19.9 9.1 %place.1 = bf16[256,16384]{1,0:T(8,128)(2,1)} custom-call(s32[1,256]{1,0:T(1,128)S(1)} %pad_add_fusion.line_ref, bf16[128,16384]{1,0:T(8,128)(2,1)S(1)} %copy-done, bf16[128,16384]{1,0:T(8,128)(2,1)} %collective-permute-done.1.theirs_ref), custom_call_target="tpu_custom_call" | custom-call | flops 2147483648 | bytes 16777216 | tf_op jit(solution)/shard_map/place/pallas_call | solution.py:27
  29.0 192.1 %all_to_all.10 = bf16[32,8,16384]{2,1,0:T(8,128)(2,1)} all-to-all(bf16[32,8,16384]{2,1,0:T(8,128)(2,1)} %bitcast.34), channel_id=1, replica_groups={{0,8,16,24,32,40,48,56,64,72,80,88,96,104,112,120,128,136,144,152,160,1..., dimensions={0} | all-to-all | bytes 16777216 | tf_op jit(solution)/shard_map/all_to_all | solution.py:98
  221.1 0.0 all-gather.2.cloned.1.call-done
  221.1 0.0 copy-start.1
  221.1 12.2 %multiply.1 = f32[256,512]{1,0:T(8,128)S(1)} custom-call(bf16[256,16384]{1,0:T(8,128)(2,1)} %bitcast.33, bf16[512,16384]{1,0:T(8,128)(2,1)} %bitcast.35), custom_call_target="tpu_custom_call" | custom-call | flops 4294967296 | bytes 25690112 | tf_op jit(solution)/shard_map/multiply/pallas_call | solution.py:60
  233.3 0.9 reshape.153
  234.3 9.6 %all-to-all-start.1 = ((f32[64,4,512]{2,1,0:T(4,128)}), f32[64,4,512]{2,1,0:T(4,128)S(1)}, u32[]{:S(2)}, u32[]{:S(2)}) async-start(f32[64,4,512]{2,1,0:T(4,128)} %reshape.153), calls=%async_computation.1 | async-start | bytes 1048576 | tf_op jit(solution)/shard_map/all_to_all | solution.py:107
  243.9 0.0 copy-done.1
  243.9 17.3 %all-to-all-done.1 = f32[64,4,512]{2,1,0:T(4,128)S(1)} async-done(((f32[64,4,512]{2,1,0:T(4,128)}), f32[64,4,512]{2,1,0:T(4,128)S(1)}, u32[]{:S(2)}, u32[]{:S(2)}) %all-to-all-start.1) | async-done | bytes 524320 | tf_op jit(solution)/shard_map/all_to_all | solution.py:107
  261.2 0.2 reshape.154
  261.4 1.5 gather_fusion
  (3 shorter events, 0.0 us)
Async XLA Ops:
  6.5 214.5 %all-gather.2.cloned.1.call-start = ((), (), s32[]{:S(2)}) async-start(), calls=%async_computation.2 | async-start | bytes 20971520 | tf_op jit(solution)/shard_map/all_gather | solution.py:94
  7.3 10.5 %collective-permute-start.1 = (bf16[128,16384]{1,0:T(8,128)(2,1)}, bf16[128,16384]{1,0:T(8,128)(2,1)}, u32[]{:S(2)}, u32[]{:S(2)}) collective-permute-start(bf16[128,16384]{1,0:T(8,128)(2,1)} %mine_ref.1), channel_id=1, source_target_pairs={{0,4},{4,0},{8,12},{12,8},{16,20},{20,16},{24,28},{28,24},{32,36},... | collective-permute-start | bytes 12582920 | tf_op jit(solution)/shard_map/ppermute | solution.py:83
  12.8 4.5 %collective-permute-start = (s32[1,128]{1,0:T(1,128)S(1)}, s32[1,128]{1,0:T(1,128)S(1)}, u32[]{:S(2)}, u32[]{:S(2)}) collective-permute-start(s32[1,128]{1,0:T(1,128)S(1)} %compare_select_fusion.4), channel_id=1, source_target_pairs={{0,4},{4,0},{8,12},{12,8},{16,20},{20,16},{24,28},{28,24},{32,36},... | collective-permute-start | bytes 1544 | tf_op jit(solution)/shard_map/ppermute | solution.py:91
  17.7 2.2 copy-start
  221.1 22.8 %copy-start.1 = (s32[128,1]{0,1:T(1,128)S(1)}, s32[128,1]{0,1:T(1,128)}, u32[]{:S(2)}) copy-start(s32[128,1]{0,1:T(1,128)} %param.4) | copy-start | bytes 1540
  234.3 27.0 %all-to-all-start.1 = ((f32[64,4,512]{2,1,0:T(4,128)}), f32[64,4,512]{2,1,0:T(4,128)S(1)}, u32[]{:S(2)}, u32[]{:S(2)}) async-start(f32[64,4,512]{2,1,0:T(4,128)} %reshape.153), calls=%async_computation.1 | async-start | bytes 1048576 | tf_op jit(solution)/shard_map/all_to_all | solution.py:107
Sparse Core Ops, SparseCore 0:
  9.2 160.4 all-gather.1

commit v2 on v0

v2 whole, which is shorter than its diff:
```python
import jax
import jax.numpy as jnp
from jax import lax
from jax.experimental import pallas as pl
from jax.experimental.pallas import tpu as pltpu
from jax.sharding import PartitionSpec as P

CAP = 4
BLOCK = 2 * CAP
SHIFTS = (0, 1, 3, 2)
VMEM = 48 * 1024 * 1024


def place_kernel(owner_ref, low_ref, high_ref, out_ref, pick_ref):
    lines, rows = out_ref.shape[0], low_ref.shape[0]

    @pl.when(pl.program_id(0) == 0)
    def _():
        owner = owner_ref[...]
        across = jnp.broadcast_to(owner.astype(jnp.float32), (rows, rows))
        down = across.T
        first = lax.broadcasted_iota(jnp.int32, (rows, rows), 0)
        second = lax.broadcasted_iota(jnp.int32, (rows, rows), 1)
        earlier = jnp.where((across == down) & (first < second), 1, 0)
        line = owner * BLOCK + jnp.sum(earlier, axis=0, keepdims=True)
        number = lax.broadcasted_iota(jnp.int32, (lines, rows), 0)
        pick_ref[:, :rows] = jnp.where(number == line, 1.0, 0.0).astype(jnp.bfloat16)
        pick_ref[:, rows:] = jnp.where(number == line + CAP, 1.0, 0.0).astype(jnp.bfloat16)

    both = jnp.concatenate([low_ref[...], high_ref[...]], axis=0)
    out_ref[...] = jnp.dot(
        pick_ref[...], both, preferred_element_type=jnp.float32
    ).astype(jnp.bfloat16)


def place(owner, integrals, peers):
    rows, cols = integrals.shape
    lines, width = peers * BLOCK, cols // 2
    block = min(1024, width)
    steps = width // block
    return pl.pallas_call(
        place_kernel,
        grid=(steps,),
        in_specs=[
            pl.BlockSpec((1, rows), lambda i: (0, 0)),
            pl.BlockSpec((rows, block), lambda i: (0, i)),
            pl.BlockSpec((rows, block), lambda i: (0, steps + i)),
        ],
        out_specs=pl.BlockSpec((lines, block), lambda i: (0, i)),
        out_shape=jax.ShapeDtypeStruct((lines, width), jnp.bfloat16),
        scratch_shapes=[pltpu.VMEM((lines, 2 * rows), jnp.bfloat16)],
        compiler_params=pltpu.CompilerParams(vmem_limit_bytes=VMEM),
        cost_estimate=pl.CostEstimate(
            flops=4 * lines * rows * width,
            bytes_accessed=2 * (2 * rows + lines) * width,
            transcendentals=0,
        ),
        name="place",
    )(owner, integrals, integrals)


def multiply_kernel(amp_ref, rows_ref, *refs):
    amp_refs, out_ref, total_ref = refs[:-2], refs[-2], refs[-1]
    step, last = pl.program_id(0), pl.num_programs(0) - 1

    @pl.when(step == 0)
    def _():
        total_ref[...] = jnp.zeros_like(total_ref)

    rows = rows_ref[...]
    half = lax.broadcasted_iota(jnp.int32, rows.shape, 0) // CAP % 2
    zero = jnp.zeros_like(rows)
    wide = jnp.concatenate(
        [jnp.where(half == 0, rows, zero), jnp.where(half == 1, rows, zero)], axis=1
    )
    count = len(amp_refs) // 2
    low = jnp.concatenate([ref[...] for ref in amp_refs[:count]], axis=0)
    high = jnp.concatenate([ref[...] for ref in amp_refs[count:]], axis=0)
    amps = jnp.concatenate([low, high], axis=1)
    total_ref[...] += lax.dot_general(
        wide, amps, (((1,), (1,)), ((), ())), preferred_element_type=jnp.float32
    )

    @pl.when(step == last)
    def _():
        pairs = amp_refs[0].shape[0]
        for i, shift in enumerate(SHIFTS):
            at = (amp_ref[0] + len(SHIFTS) - shift) % len(SHIFTS)
            there = pl.ds(pl.multiple_of(at * pairs, pairs), pairs)
            here = slice(i * pairs, (i + 1) * pairs)
            for source in range(out_ref.shape[0]):
                start = source * BLOCK
                out_ref[source, :, there] = (
                    total_ref[start : start + CAP, here]
                    + total_ref[start + CAP : start + BLOCK, here]
                )


def multiply(amp, rows, shards, peers):
    lines, width = rows.shape
    pairs, block = shards[0].shape[0], min(1024, width)
    steps, count = width // block, len(shards)
    return pl.pallas_call(
        multiply_kernel,
        grid=(steps,),
        in_specs=[
            pl.BlockSpec(memory_space=pltpu.SMEM),
            pl.BlockSpec((lines, block), lambda i: (0, i)),
        ]
        + [pl.BlockSpec((pairs, block), lambda i: (0, i))] * count
        + [pl.BlockSpec((pairs, block), lambda i: (0, steps + i))] * count,
        out_specs=pl.BlockSpec((peers, CAP, count * pairs), lambda i: (0, 0, 0)),
        out_shape=jax.ShapeDtypeStruct((peers, CAP, count * pairs), jnp.float32),
        scratch_shapes=[pltpu.VMEM((lines, count * pairs), jnp.float32)],
        compiler_params=pltpu.CompilerParams(vmem_limit_bytes=VMEM),
        cost_estimate=pl.CostEstimate(
            flops=4 * lines * count * pairs * width,
            bytes_accessed=2 * (lines + 2 * count * pairs) * width,
            transcendentals=0,
        ),
        name="multiply",
    )(amp, rows, *shards, *shards)


def body(integrals, row_owner, lambda_amps):
    peers, amps = lax.axis_size("kblk"), lax.axis_size("amp")
    amp = lax.axis_index("amp").astype(jnp.int32)
    mine = lambda_amps[0]
    shards = [mine] + [
        lax.ppermute(mine, "amp", [(i, (i + shift) % amps) for i in range(amps)])
        for shift in SHIFTS[1:]
    ]

    rows_here = integrals.shape[0]
    owner = row_owner[:, 0]
    placed = place(owner[None, :], integrals, peers)
    width = placed.shape[1]
    arrived = lax.all_to_all(
        placed.reshape(peers, BLOCK, width), "kblk", split_axis=0, concat_axis=0, tiled=True
    )
    values = multiply(amp[None], arrived.reshape(peers * BLOCK, width), shards, peers)
    returned = lax.all_to_all(values, "kblk", split_axis=0, concat_axis=0, tiled=True)

    number = jnp.arange(rows_here, dtype=jnp.int32)
    earlier = (owner[:, None] == owner[None, :]) & (number[None, :] < number[:, None])
    slot = jnp.sum(earlier.astype(jnp.int32), axis=1)
    return returned.reshape(peers * CAP, values.shape[2])[owner * CAP + slot]


def solution(mesh):
    placed = (P(("kblk", "amp"), None), P(("kblk", "amp"), None), P("kblk", "amp", None))
    return jax.shard_map(
        body, mesh=mesh, in_specs=placed, out_specs=P(("kblk", "amp"), None), check_vma=False
    )
```

time: 309 us -> 255 us (0.83)
  blocking collectives: 198 us -> 0 us
  waiting for transfers between devices: 18 us -> 199 us
  local copies, waits for them, and re-layouts: 38.4 us -> 6.67 us
  matrix products: 25.7 us -> 0 us
  starting transfers between devices: 5.82 us -> 27.3 us
  Pallas kernels: 0 us -> 21.3 us
  between operations: 13.5 us -> 0.06 us
  other arithmetic: 8.41 us -> 0.18 us
    all_to_all x1 -> x0, blocking collectives: 198 us -> none  [body(): lax.all_to_all(outgoing, 'kblk', split_axis=0, concat_axis=0, tiled=True)]
    ppermute x0 -> x3, waiting for transfers between devices: none -> 180 us  [body(): lax.ppermute(mine, 'amp', [(i, (i + shift) % amps) for i in range(amps)])]
    gather x3 -> x1, local copies, waits for them, and re-layouts: 35 us -> 1.45 us  [body(): return returned.reshape(peers * CAP, values.shape[2])[owner * CAP + slot]]
    dot_general x1 -> x0, matrix products: 25.7 us -> none  [body(): lax.dot_general(flat, whole_lambda, (((1,), (1,)), ((), ())), preferred_e...]
    pallas_call x0 -> x2, Pallas kernels: none -> 21.3 us  [the longest x1 14.5 us: multiply(): pl.pallas_call(multiply_kernel, grid=(steps,), in_specs=[pl.BlockSpec(mem...]
    all_to_all x1 -> x2, starting transfers between devices: 5.81 us -> 23 us  [the longest x1 13.3 us: body(): lax.all_to_all(placed.reshape(peers, BLOCK, width), 'kblk', split_axis=0,...]
    select_n x3 -> x1, other arithmetic: 6.66 us -> 0.01 us  [body(): return returned.reshape(peers * CAP, values.shape[2])[owner * CAP + slot]]
    unnamed x0 -> x8, local copies, waits for them, and re-layouts: none -> 5.03 us
  transfers between devices with their start and end apart: 2 -> 5, of which waited for: 1 -> 4; matrix products, arithmetic and copies ran while one was open for 14% -> 0% of each run, Pallas kernels for 0% -> 0%
where the time goes in v2:
time: 255 us; the launch traced here: 254 us
  waiting for transfers between devices  199 us (78%)
  starting transfers between devices  27.3 us (11%)
  Pallas kernels  21.3 us (8%)
  local copies, waits for them, and re-layouts  6.67 us (3%)
    ppermute x3, waiting for transfers between devices, body(): lax.ppermute(mine, 'amp', [(i, (i + shift) % amps) for i in range(amps)])  180 us
    all_to_all x1, waiting for transfers between devices, body(): lax.all_to_all(values, 'kblk', split_axis=0, concat_axis=0, tiled=True)  17.1 us
    pallas_call x1, Pallas kernels, multiply(): pl.pallas_call(multiply_kernel, grid=(steps,), in_specs=[pl.BlockSpec(mem...  14.5 us
    all_to_all x1, starting transfers between devices, body(): lax.all_to_all(placed.reshape(peers, BLOCK, width), 'kblk', split_axis=0,...  13.3 us
    all_to_all x1, starting transfers between devices, body(): lax.all_to_all(values, 'kblk', split_axis=0, concat_axis=0, tiled=True)  9.67 us
    pallas_call x1, Pallas kernels, place(): pl.pallas_call(place_kernel, grid=(steps,), in_specs=[pl.BlockSpec((1, ro...  6.76 us
  transfers between devices with their start and end apart: 5, of which 4 were waited for; matrix products, arithmetic and copies ran while one was open for 0% of the time, Pallas kernels for 0%

profile of v2, /device:TPU:1, one launch (start us, length us, event | category | flops | bytes accessed | tf_op | source)
XLA Modules:
  0.0 254.1 jit_solution(9757577678814963888)
XLA Ops:
  0.0 0.0 copy-start
  0.0 2.2 copy-done
  2.2 0.0 copy-start.2
  2.2 0.7 copy-done.2
  2.8 6.8 %place.1 = bf16[512,8192]{1,0:T(8,128)(2,1)} custom-call(s32[1,128]{1,0:T(1,128)S(1)} %bitcast.17, bf16[128,16384]{1,0:T(8,128)(2,1)S(1)} %copy-done, bf16[128,16384]{1,0:T(8,128)(2,1)S(1)} %copy-done), custom_call_target="tpu_custom_call" | custom-call | flops 2147483648 | bytes 12582912 | tf_op jit(solution)/shard_map/place/pallas_call | solution.py:41
  9.6 13.3 %all-to-all-start = ((bf16[64,8,8192]{2,1,0:T(8,128)(2,1)}), bf16[64,8,8192]{2,1,0:T(8,128)(2,1)}, u32[]{:S(2)}, u32[]{:S(2)}) async-start(bf16[64,8,8192]{2,1,0:T(8,128)(2,1)} %bitcast.19), calls=%async_computation | async-start | bytes 16777216 | tf_op jit(solution)/shard_map/all_to_all | solution.py:138
  23.0 1.3 collective-permute-start
  24.2 1.5 collective-permute-start.1
  25.7 1.5 collective-permute-start.2
  27.2 88.9 %collective-permute-done.refs_1_.refs_5_ = bf16[128,16384]{1,0:T(8,128)(2,1)} collective-permute-done((bf16[128,16384]{1,0:T(8,128)(2,1)}, bf16[128,16384]{1,0:T(8,128)(2,1)}, u32[]{:S(2)}, u32[]{:S(2)}) %collective-permute-start) | collective-permute-done | bytes 4194336 | tf_op jit(solution)/shard_map/ppermute | solution.py:130
  116.2 0.0 collective-permute-done.1.refs_2_.refs_6_
  116.2 90.9 %collective-permute-done.2.refs_3_.refs_7_ = bf16[128,16384]{1,0:T(8,128)(2,1)} collective-permute-done((bf16[128,16384]{1,0:T(8,128)(2,1)}, bf16[128,16384]{1,0:T(8,128)(2,1)}, u32[]{:S(2)}, u32[]{:S(2)}) %collective-permute-start.2) | collective-permute-done | bytes 4194336 | tf_op jit(solution)/shard_map/ppermute | solution.py:130
  207.0 1.7 all-to-all-done
  208.7 0.0 copy-start.1
  208.7 2.2 copy-done.1
  210.9 0.0 copy-start.3
  210.9 14.5 %multiply.1 = f32[64,4,512]{2,1,0:T(4,128)} custom-call(s32[1]{0:T(128)} %bitcast.amp_ref, bf16[512,8192]{1,0:T(8,128)(2,1)} %bitcast.3.rows_ref, bf16[128,16384]{1,0:T(8,128)(2,1)S(1)} %bitcast.15, bf16[128,16384]{1,0:T(8,128)(2,1)} %collective-permute-done.refs_1_.refs_5_, bf16[128,16384]{1,0:T(8,128)(2,1)} %collective-permute-done.1.refs_2_.refs_6_, ...), custom_call_target="tpu_custom_call" | custom-call | flops 8589934592 | bytes 25165824 | tf_op jit(solution)/shard_map/multiply/pallas_call | solution.py:103
  225.4 9.7 %all-to-all-start.1 = ((f32[64,4,512]{2,1,0:T(4,128)}), f32[64,4,512]{2,1,0:T(4,128)S(1)}, u32[]{:S(2)}, u32[]{:S(2)}) async-start(f32[64,4,512]{2,1,0:T(4,128)} %multiply.1), calls=%async_computation.1 | async-start | bytes 1048576 | tf_op jit(solution)/shard_map/all_to_all | solution.py:142
  235.1 0.0 copy-done.3
  235.1 0.2 convert_reduce_fusion
  235.3 17.1 %all-to-all-done.1 = f32[64,4,512]{2,1,0:T(4,128)S(1)} async-done(((f32[64,4,512]{2,1,0:T(4,128)}), f32[64,4,512]{2,1,0:T(4,128)S(1)}, u32[]{:S(2)}, u32[]{:S(2)}) %all-to-all-start.1) | async-done | bytes 524320 | tf_op jit(solution)/shard_map/all_to_all | solution.py:142
  252.4 0.2 reshape.13
  252.6 1.5 gather_fusion
  (2 shorter events, 0.0 us)
Async XLA Ops:
  0.0 2.2 copy-start
  2.2 0.7 copy-start.2
  9.6 199.1 %all-to-all-start = ((bf16[64,8,8192]{2,1,0:T(8,128)(2,1)}), bf16[64,8,8192]{2,1,0:T(8,128)(2,1)}, u32[]{:S(2)}, u32[]{:S(2)}) async-start(bf16[64,8,8192]{2,1,0:T(8,128)(2,1)} %bitcast.19), calls=%async_computation | async-start | bytes 16777216 | tf_op jit(solution)/shard_map/all_to_all | solution.py:138
  23.0 93.2 %collective-permute-start = (bf16[128,16384]{1,0:T(8,128)(2,1)}, bf16[128,16384]{1,0:T(8,128)(2,1)}, u32[]{:S(2)}, u32[]{:S(2)}) collective-permute-start(bf16[128,16384]{1,0:T(8,128)(2,1)} %bitcast.12), channel_id=1, source_target_pairs={{0,1},{1,2},{2,3},{3,0},{4,5},{5,6},{6,7},{7,4},{8,9},{9,10},{10,1... | collective-permute-start | bytes 12582920 | tf_op jit(solution)/shard_map/ppermute | solution.py:130
  24.2 91.9 %collective-permute-start.1 = (bf16[128,16384]{1,0:T(8,128)(2,1)}, bf16[128,16384]{1,0:T(8,128)(2,1)}, u32[]{:S(2)}, u32[]{:S(2)}) collective-permute-start(bf16[128,16384]{1,0:T(8,128)(2,1)} %bitcast.13), channel_id=1, source_target_pairs={{0,3},{1,0},{2,1},{3,2},{4,7},{5,4},{6,5},{7,6},{8,11},{9,8},{10,9... | collective-permute-start | bytes 12582920 | tf_op jit(solution)/shard_map/ppermute | solution.py:130
  25.7 181.3 %collective-permute-start.2 = (bf16[128,16384]{1,0:T(8,128)(2,1)}, bf16[128,16384]{1,0:T(8,128)(2,1)}, u32[]{:S(2)}, u32[]{:S(2)}) collective-permute-start(bf16[128,16384]{1,0:T(8,128)(2,1)} %bitcast.14), channel_id=1, source_target_pairs={{0,2},{1,3},{2,0},{3,1},{4,6},{5,7},{6,4},{7,5},{8,10},{9,11},{10,... | collective-permute-start | bytes 12582920 | tf_op jit(solution)/shard_map/ppermute | solution.py:130
  208.7 2.2 copy-start.1
  210.9 24.2 %copy-start.3 = (s32[128,1]{0,1:T(1,128)S(1)}, s32[128,1]{0,1:T(1,128)}, u32[]{:S(2)}) copy-start(s32[128,1]{0,1:T(1,128)} %param.4) | copy-start | bytes 1540
  225.4 27.0 %all-to-all-start.1 = ((f32[64,4,512]{2,1,0:T(4,128)}), f32[64,4,512]{2,1,0:T(4,128)S(1)}, u32[]{:S(2)}, u32[]{:S(2)}) async-start(f32[64,4,512]{2,1,0:T(4,128)} %multiply.1), calls=%async_computation.1 | async-start | bytes 1048576 | tf_op jit(solution)/shard_map/all_to_all | solution.py:142

commit v3 on v0

v3 whole, which is shorter than its diff:
```python
import jax
import jax.numpy as jnp
from jax import lax
from jax.experimental import pallas as pl
from jax.experimental.pallas import tpu as pltpu
from jax.sharding import PartitionSpec as P

CAP = 4
BLOCK = 2 * CAP
PLACE_STEPS = 8
MULTIPLY_STEPS = 8


def whole_in(space):
    return pl.BlockSpec(memory_space=space)


def place_kernel(swap_ref, owner_ref, integrals_ref, out_ref, both_ref, placed_ref, pick_ref, sem):
    rows, (lines, width) = integrals_ref.shape[0], out_ref.shape
    block = width // PLACE_STEPS
    fetches = [
        [
            pltpu.make_async_copy(
                integrals_ref.at[:, pl.ds(half * width + i * block, block)],
                both_ref.at[pl.ds(half * rows, rows), pl.ds(i * block, block)],
                sem.at[i, half],
            )
            for half in range(2)
        ]
        for i in range(PLACE_STEPS)
    ]
    for pair in fetches:
        for copy in pair:
            copy.start()

    owner = owner_ref[...]
    across = jnp.broadcast_to(owner.astype(jnp.float32), (rows, rows))
    down = across.T
    first = lax.broadcasted_iota(jnp.int32, (rows, rows), 0)
    second = lax.broadcasted_iota(jnp.int32, (rows, rows), 1)
    earlier = jnp.where((across == down) & (first < second), 1, 0)
    line = owner * BLOCK + jnp.sum(earlier, axis=0, keepdims=True)
    number = lax.broadcasted_iota(jnp.int32, (lines, rows), 0)
    swap = swap_ref[0] * CAP
    pick_ref[:, :rows] = jnp.where(number == line + swap, 1.0, 0.0).astype(jnp.bfloat16)
    pick_ref[:, rows:] = jnp.where(number == line + (CAP - swap), 1.0, 0.0).astype(jnp.bfloat16)

    writes = []
    for i, pair in enumerate(fetches):
        for copy in pair:
            copy.wait()
        here = pl.ds(i * block, block)
        placed_ref[:, here] = jnp.dot(
            pick_ref[...], both_ref[:, here], preferred_element_type=jnp.float32
        ).astype(jnp.bfloat16)
        write = pltpu.make_async_copy(placed_ref.at[:, here], out_ref.at[:, here], sem.at[i, 2])
        write.start()
        writes.append(write)
    for write in writes:
        write.wait()


def place(swap, owner, integrals, peers):
    rows, cols = integrals.shape
    lines, width = peers * BLOCK, cols // 2
    return pl.pallas_call(
        place_kernel,
        in_specs=[whole_in(pltpu.SMEM), whole_in(pltpu.VMEM), whole_in(pl.ANY)],
        out_specs=whole_in(pl.ANY),
        out_shape=pltpu.HBM((lines, width), jnp.bfloat16),
        scratch_shapes=[
            pltpu.VMEM((2 * rows, width), jnp.bfloat16),
            pltpu.VMEM((lines, width), jnp.bfloat16),
            pltpu.VMEM((lines, 2 * rows), jnp.bfloat16),
            pltpu.SemaphoreType.DMA((PLACE_STEPS, 3)),
        ],
        compiler_params=pltpu.CompilerParams(vmem_limit_bytes=24 * 1024 * 1024),
        cost_estimate=pl.CostEstimate(
            flops=4 * lines * rows * width,
            bytes_accessed=2 * (2 * rows + lines) * width,
            transcendentals=0,
        ),
        name="place",
    )(swap, owner, pltpu.with_memory_space_constraint(integrals, pltpu.HBM))


def multiply_kernel(
    amp_ref, rows_ref, mine_ref, left_ref, right_ref, top_ref, bottom_ref,
    out_ref, near_ref, amps_ref, low_ref, high_ref, sem,
):
    lines, width = rows_ref.shape
    upper = lines // 2
    block = width // MULTIPLY_STEPS
    pairs = mine_ref.shape[0]
    count = amps_ref.shape[0] // pairs
    shards = (
        (mine_ref, 0, 0),
        (left_ref, 1, 0),
        (right_ref, 3, 0),
        (top_ref, 2, 0),
        (bottom_ref, 2, pairs // 2),
    )

    def fetches(i):
        here = pl.ds(pl.multiple_of(i * block, block), block)
        copies = [
            pltpu.make_async_copy(rows_ref.at[:, here], near_ref.at[:, here], sem.at[i, 0])
        ]
        for half in range(2):
            here = pl.ds(pl.multiple_of(half * width + i * block, block), block)
            for k, (ref, shift, skip) in enumerate(shards):
                at = (amp_ref[0] + count - shift) % count
                there = pl.ds(pl.multiple_of(at * pairs + skip, pairs // 2), ref.shape[0])
                copies.append(
                    pltpu.make_async_copy(
                        ref.at[:, here],
                        amps_ref.at[there, here],
                        sem.at[i, 1 + half * len(shards) + k],
                    )
                )
        return copies

    for i in range(MULTIPLY_STEPS):
        for copy in fetches(i):
            copy.start()
    group = lax.broadcasted_iota(jnp.int32, (upper, block), 0) // CAP % 2
    low_ref[...] = jnp.zeros_like(low_ref)
    high_ref[...] = jnp.zeros_like(high_ref)

    @pl.loop(0, MULTIPLY_STEPS)
    def _(i):
        for copy in fetches(i):
            copy.wait()
        here = pl.ds(pl.multiple_of(i * block, block), block)
        first, second = near_ref[:upper, here], near_ref[upper:, here]
        for half, total_ref in enumerate((low_ref, high_ref)):
            there = pl.ds(pl.multiple_of(half * width + i * block, block), block)
            total_ref[...] += lax.dot_general(
                jnp.where(group == half, first, second),
                amps_ref[:, there],
                (((1,), (1,)), ((), ())),
                preferred_element_type=jnp.float32,
            )

    half_peers = upper // BLOCK
    for source in range(half_peers):
        start = source * BLOCK
        top, bottom = slice(start, start + CAP), slice(start + CAP, start + BLOCK)
        out_ref[source] = low_ref[top, :] + high_ref[bottom, :]
        out_ref[half_peers + source] = low_ref[bottom, :] + high_ref[top, :]


def multiply(amp, rows, shards, peers, amps):
    lines, width = rows.shape
    pairs = amps * shards[0].shape[0]
    return pl.pallas_call(
        multiply_kernel,
        in_specs=[whole_in(pltpu.SMEM)] + [whole_in(pl.ANY)] * (1 + len(shards)),
        out_specs=whole_in(pltpu.VMEM),
        out_shape=jax.ShapeDtypeStruct((peers, CAP, pairs), jnp.float32),
        scratch_shapes=[
            pltpu.VMEM((lines, width), jnp.bfloat16),
            pltpu.VMEM((pairs, 2 * width), jnp.bfloat16),
            pltpu.VMEM((lines // 2, pairs), jnp.float32),
            pltpu.VMEM((lines // 2, pairs), jnp.float32),
            pltpu.SemaphoreType.DMA((MULTIPLY_STEPS, 1 + 2 * len(shards))),
        ],
        compiler_params=pltpu.CompilerParams(vmem_limit_bytes=36 * 1024 * 1024),
        cost_estimate=pl.CostEstimate(
            flops=2 * lines * pairs * width,
            bytes_accessed=2 * (lines + 2 * pairs) * width,
            transcendentals=0,
        ),
        name="multiply",
    )(amp, *[pltpu.with_memory_space_constraint(x, pltpu.HBM) for x in (rows, *shards)])


def body(integrals, row_owner, lambda_amps):
    peers, amps = lax.axis_size("kblk"), lax.axis_size("amp")
    amp = lax.axis_index("amp").astype(jnp.int32)
    swap = (lax.axis_index("kblk") >= peers // 2).astype(jnp.int32)
    mine = lambda_amps[0]
    middle = mine.shape[0] // 2
    ahead = [(i, (i + 1) % amps) for i in range(amps)]
    back = [(i, (i - 1) % amps) for i in range(amps)]
    left, right = lax.ppermute(mine, "amp", ahead), lax.ppermute(mine, "amp", back)
    top = lax.ppermute(left[:middle], "amp", ahead)
    bottom = lax.ppermute(right[middle:], "amp", back)
    shards = (mine, left, right, top, bottom)

    rows_here = integrals.shape[0]
    owner = row_owner[:, 0]
    placed = place(swap[None], owner[None, :], integrals, peers)
    width = placed.shape[1]
    arrived = lax.all_to_all(
        placed.reshape(peers, BLOCK, width), "kblk", split_axis=0, concat_axis=0, tiled=True
    )
    values = multiply(amp[None], arrived.reshape(peers * BLOCK, width), shards, peers, amps)
    returned = lax.all_to_all(values, "kblk", split_axis=0, concat_axis=0, tiled=True)

    number = jnp.arange(rows_here, dtype=jnp.int32)
    earlier = (owner[:, None] == owner[None, :]) & (number[None, :] < number[:, None])
    slot = jnp.sum(earlier.astype(jnp.int32), axis=1)
    return returned.reshape(peers * CAP, values.shape[2])[owner * CAP + slot]


def solution(mesh):
    placed = (P(("kblk", "amp"), None), P(("kblk", "amp"), None), P("kblk", "amp", None))
    return jax.shard_map(
        body, mesh=mesh, in_specs=placed, out_specs=P(("kblk", "amp"), None), check_vma=False
    )
```

time: 309 us -> 241 us (0.78)
  blocking collectives: 198 us -> 0 us
  waiting for transfers between devices: 18 us -> 194 us
  local copies, waits for them, and re-layouts: 38.4 us -> 6.04 us
  matrix products: 25.7 us -> 0 us
  starting transfers between devices: 5.82 us -> 24.6 us
  Pallas kernels: 0 us -> 16.6 us
  between operations: 13.5 us -> 0.1 us
  other arithmetic: 8.41 us -> 0.18 us
    all_to_all x1 -> x0, blocking collectives: 198 us -> none  [body(): lax.all_to_all(outgoing, 'kblk', split_axis=0, concat_axis=0, tiled=True)]
    ppermute x0 -> x4, waiting for transfers between devices: none -> 134 us  [the longest x1 90.5 us: body(): lax.ppermute(mine, 'amp', ahead)]
    all_to_all x1 -> x2, waiting for transfers between devices: 17.3 us -> 59.6 us  [the longest x1 42.5 us: body(): lax.all_to_all(placed.reshape(peers, BLOCK, width), 'kblk', split_axis=0,...]
    gather x3 -> x1, local copies, waits for them, and re-layouts: 35 us -> 1.45 us  [body(): return returned.reshape(peers * CAP, values.shape[2])[owner * CAP + slot]]
    dot_general x1 -> x0, matrix products: 25.7 us -> none  [body(): lax.dot_general(flat, whole_lambda, (((1,), (1,)), ((), ())), preferred_e...]
    pallas_call x0 -> x2, Pallas kernels: none -> 16.6 us  [the longest x1 10.7 us: multiply(): pl.pallas_call(multiply_kernel, in_specs=[whole_in(pltpu.SMEM)] + [whole_...]
    all_to_all x1 -> x2, starting transfers between devices: 5.81 us -> 19.3 us  [the longest x1 13.4 us: body(): lax.all_to_all(placed.reshape(peers, BLOCK, width), 'kblk', split_axis=0,...]
    select_n x3 -> x1, other arithmetic: 6.66 us -> 0.01 us  [body(): return returned.reshape(peers * CAP, values.shape[2])[owner * CAP + slot]]
  transfers between devices with their start and end apart: 2 -> 6, of which waited for: 1 -> 5; matrix products, arithmetic and copies ran while one was open for 14% -> 1% of each run, Pallas kernels for 0% -> 0%
where the time goes in v3:
time: 241 us
  waiting for transfers between devices  194 us (80%)
  starting transfers between devices  24.6 us (10%)
  Pallas kernels  16.6 us (7%)
  local copies, waits for them, and re-layouts  6.04 us (3%)
    ppermute x1, waiting for transfers between devices, body(): lax.ppermute(mine, 'amp', ahead)  90.5 us
    all_to_all x1, waiting for transfers between devices, body(): lax.all_to_all(placed.reshape(peers, BLOCK, width), 'kblk', split_axis=0,...  42.5 us
    ppermute x1, waiting for transfers between devices, body(): top = lax.ppermute(left[:middle], 'amp', ahead)  41 us
    all_to_all x1, waiting for transfers between devices, body(): lax.all_to_all(values, 'kblk', split_axis=0, concat_axis=0, tiled=True)  17.1 us
    all_to_all x1, starting transfers between devices, body(): lax.all_to_all(placed.reshape(peers, BLOCK, width), 'kblk', split_axis=0,...  13.4 us
    pallas_call x1, Pallas kernels, multiply(): pl.pallas_call(multiply_kernel, in_specs=[whole_in(pltpu.SMEM)] + [whole_...  10.7 us
    all_to_all x1, starting transfers between devices, body(): lax.all_to_all(values, 'kblk', split_axis=0, concat_axis=0, tiled=True)  5.9 us
    pallas_call x1, Pallas kernels, place(): pl.pallas_call(place_kernel, in_specs=[whole_in(pltpu.SMEM), whole_in(plt...  5.83 us
  transfers between devices with their start and end apart: 6, of which 5 were waited for; matrix products, arithmetic and copies ran while one was open for 1% of the time, Pallas kernels for 0%

profile of v3, /device:TPU:1, one launch (start us, length us, event | category | flops | bytes accessed | tf_op | source)
XLA Modules:
  0.0 241.2 jit_solution(17612357948080413906)
XLA Ops:
  0.0 0.0 copy-start
  0.0 0.7 copy-done
  0.7 5.8 %place.1 = bf16[512,8192]{1,0:T(8,128)(2,1)} custom-call(s32[1]{0:T(128)} %bitcast.1.swap_ref, s32[1,128]{1,0:T(1,128)S(1)} %bitcast.13, bf16[128,16384]{1,0:T(8,128)(2,1)} %integrals_ref.1), custom_call_target="tpu_custom_call" | custom-call | flops 2147483648 | bytes 12582912 | tf_op jit(solution)/shard_map/place/pallas_call | solution.py:66
  6.5 13.4 %all-to-all-start = ((bf16[64,8,8192]{2,1,0:T(8,128)(2,1)}), bf16[64,8,8192]{2,1,0:T(8,128)(2,1)}, u32[]{:S(2)}, u32[]{:S(2)}) async-start(bf16[64,8,8192]{2,1,0:T(8,128)(2,1)} %bitcast.15), calls=%async_computation | async-start | bytes 16777216 | tf_op jit(solution)/shard_map/all_to_all | solution.py:195
  19.9 1.3 collective-permute-start
  21.1 1.5 collective-permute-start.1
  22.6 90.5 %collective-permute-done.left_ref = bf16[128,16384]{1,0:T(8,128)(2,1)S(1)} collective-permute-done((bf16[128,16384]{1,0:T(8,128)(2,1)}, bf16[128,16384]{1,0:T(8,128)(2,1)S(1)}, u32[]{:S(2)}, u32[]{:S(2)}) %collective-permute-start) | collective-permute-done | bytes 4194336 | tf_op jit(solution)/shard_map/ppermute | solution.py:186
  113.1 0.0 copy-start.2
  113.1 0.1 slice.10
  113.2 0.1 collective-permute-start.2
  113.3 0.0 collective-permute-done.1.right_ref
  113.3 0.0 copy-start.3
  113.3 2.1 copy-done.3
  115.5 1.5 slice.11
  116.9 0.0 copy-done.2
  116.9 2.5 %collective-permute-start.3 = (bf16[64,16384]{1,0:T(8,128)(2,1)}, bf16[64,16384]{1,0:T(8,128)(2,1)}, u32[]{:S(2)}, u32[]{:S(2)}) collective-permute-start(bf16[64,16384]{1,0:T(8,128)(2,1)} %slice.11), channel_id=1, source_target_pairs={{0,3},{1,0},{2,1},{3,2},{4,7},{5,4},{6,5},{7,6},{8,11},{9,8},{10,9... | collective-permute-start | bytes 6291464 | tf_op jit(solution)/shard_map/ppermute | solution.py:188
  119.4 41.0 %collective-permute-done.2.top_ref = bf16[64,16384]{1,0:T(8,128)(2,1)} collective-permute-done((bf16[64,16384]{1,0:T(8,128)(2,1)S(1)}, bf16[64,16384]{1,0:T(8,128)(2,1)}, u32[]{:S(2)}, u32[]{:S(2)}) %collective-permute-start.2) | collective-permute-done | bytes 2097184 | tf_op jit(solution)/shard_map/ppermute | solution.py:187
  160.5 2.6 %collective-permute-done.3.bottom_ref = bf16[64,16384]{1,0:T(8,128)(2,1)} collective-permute-done((bf16[64,16384]{1,0:T(8,128)(2,1)}, bf16[64,16384]{1,0:T(8,128)(2,1)}, u32[]{:S(2)}, u32[]{:S(2)}) %collective-permute-start.3) | collective-permute-done | bytes 2097184 | tf_op jit(solution)/shard_map/ppermute | solution.py:188
  163.1 42.5 %all-to-all-done = bf16[64,8,8192]{2,1,0:T(8,128)(2,1)} async-done(((bf16[64,8,8192]{2,1,0:T(8,128)(2,1)}), bf16[64,8,8192]{2,1,0:T(8,128)(2,1)}, u32[]{:S(2)}, u32[]{:S(2)}) %all-to-all-start) | async-done | bytes 8388640 | tf_op jit(solution)/shard_map/all_to_all | solution.py:195
  205.6 0.0 copy-start.1
  205.6 10.7 %multiply.1 = f32[64,4,512]{2,1,0:T(4,128)} custom-call(s32[1]{0:T(128)} %bitcast.amp_ref, bf16[512,8192]{1,0:T(8,128)(2,1)} %bitcast.4.rows_ref, bf16[128,16384]{1,0:T(8,128)(2,1)} %bitcast.18, bf16[128,16384]{1,0:T(8,128)(2,1)} %copy-done.2, bf16[128,16384]{1,0:T(8,128)(2,1)} %copy-done.3, bf16[64,16384]{1,0:T(8,128)(2,1)} %collective-permute-done.2.top_ref, ...), custom_call_target="tpu_custom_call" | custom-call | flops 4294967296 | bytes 25165824 | tf_op jit(solution)/shard_map/multiply/pallas_call | solution.py:156
  216.4 5.9 %all-to-all-start.1 = ((f32[64,4,512]{2,1,0:T(4,128)}), f32[64,4,512]{2,1,0:T(4,128)S(1)}, u32[]{:S(2)}, u32[]{:S(2)}) async-start(f32[64,4,512]{2,1,0:T(4,128)} %multiply.1), calls=%async_computation.1 | async-start | bytes 1048576 | tf_op jit(solution)/shard_map/all_to_all | solution.py:199
  222.3 0.0 copy-done.1
  222.3 0.2 convert_reduce_fusion
  222.5 17.1 %all-to-all-done.1 = f32[64,4,512]{2,1,0:T(4,128)S(1)} async-done(((f32[64,4,512]{2,1,0:T(4,128)}), f32[64,4,512]{2,1,0:T(4,128)S(1)}, u32[]{:S(2)}, u32[]{:S(2)}) %all-to-all-start.1) | async-done | bytes 524320 | tf_op jit(solution)/shard_map/all_to_all | solution.py:199
  239.6 0.2 reshape.13
  239.8 1.5 gather_fusion
  (2 shorter events, 0.0 us)
Async XLA Ops:
  0.0 0.7 copy-start
  6.5 199.1 %all-to-all-start = ((bf16[64,8,8192]{2,1,0:T(8,128)(2,1)}), bf16[64,8,8192]{2,1,0:T(8,128)(2,1)}, u32[]{:S(2)}, u32[]{:S(2)}) async-start(bf16[64,8,8192]{2,1,0:T(8,128)(2,1)} %bitcast.15), calls=%async_computation | async-start | bytes 16777216 | tf_op jit(solution)/shard_map/all_to_all | solution.py:195
  19.9 93.2 %collective-permute-start = (bf16[128,16384]{1,0:T(8,128)(2,1)}, bf16[128,16384]{1,0:T(8,128)(2,1)S(1)}, u32[]{:S(2)}, u32[]{:S(2)}) collective-permute-start(bf16[128,16384]{1,0:T(8,128)(2,1)} %bitcast.16), channel_id=1, source_target_pairs={{0,1},{1,2},{2,3},{3,0},{4,5},{5,6},{6,7},{7,4},{8,9},{9,10},{10,1... | collective-permute-start | bytes 12582920 | tf_op jit(solution)/shard_map/ppermute | solution.py:186
  21.1 92.2 %collective-permute-start.1 = (bf16[128,16384]{1,0:T(8,128)(2,1)}, bf16[128,16384]{1,0:T(8,128)(2,1)S(1)}, u32[]{:S(2)}, u32[]{:S(2)}) collective-permute-start(bf16[128,16384]{1,0:T(8,128)(2,1)} %bitcast.17), channel_id=1, source_target_pairs={{0,3},{1,0},{2,1},{3,2},{4,7},{5,4},{6,5},{7,6},{8,11},{9,8},{10,9... | collective-permute-start | bytes 12582920 | tf_op jit(solution)/shard_map/ppermute | solution.py:186
  113.1 3.9 %copy-start.2 = (bf16[128,16384]{1,0:T(8,128)(2,1)}, bf16[128,16384]{1,0:T(8,128)(2,1)S(1)}, u32[]{:S(2)}) copy-start(bf16[128,16384]{1,0:T(8,128)(2,1)S(1)} %collective-permute-done.left_ref) | copy-start | bytes 12582916
  113.2 47.2 %collective-permute-start.2 = (bf16[64,16384]{1,0:T(8,128)(2,1)S(1)}, bf16[64,16384]{1,0:T(8,128)(2,1)}, u32[]{:S(2)}, u32[]{:S(2)}) collective-permute-start(bf16[64,16384]{1,0:T(8,128)(2,1)S(1)} %slice.10), channel_id=1, source_target_pairs={{0,1},{1,2},{2,3},{3,0},{4,5},{5,6},{6,7},{7,4},{8,9},{9,10},{10,1... | collective-permute-start | bytes 6291464 | tf_op jit(solution)/shard_map/ppermute | solution.py:187
  113.3 2.1 copy-start.3
  116.9 46.2 %collective-permute-start.3 = (bf16[64,16384]{1,0:T(8,128)(2,1)}, bf16[64,16384]{1,0:T(8,128)(2,1)}, u32[]{:S(2)}, u32[]{:S(2)}) collective-permute-start(bf16[64,16384]{1,0:T(8,128)(2,1)} %slice.11), channel_id=1, source_target_pairs={{0,3},{1,0},{2,1},{3,2},{4,7},{5,4},{6,5},{7,6},{8,11},{9,8},{10,9... | collective-permute-start | bytes 6291464 | tf_op jit(solution)/shard_map/ppermute | solution.py:188
  205.6 16.6 %copy-start.1 = (s32[128,1]{0,1:T(1,128)S(1)}, s32[128,1]{0,1:T(1,128)}, u32[]{:S(2)}) copy-start(s32[128,1]{0,1:T(1,128)} %param.4) | copy-start | bytes 1540
  216.4 23.2 %all-to-all-start.1 = ((f32[64,4,512]{2,1,0:T(4,128)}), f32[64,4,512]{2,1,0:T(4,128)S(1)}, u32[]{:S(2)}, u32[]{:S(2)}) async-start(f32[64,4,512]{2,1,0:T(4,128)} %multiply.1), calls=%async_computation.1 | async-start | bytes 1048576 | tf_op jit(solution)/shard_map/all_to_all | solution.py:199

commit v4 on v3

v4 whole, which is shorter than its diff:
```python
import jax
import jax.numpy as jnp
from jax import lax
from jax.experimental import pallas as pl
from jax.experimental.pallas import tpu as pltpu
from jax.sharding import PartitionSpec as P

CAP = 4
LARGEST = 32767.0
STEPS = 64
LANES = 128
BLOCK = 2 * CAP
PLACE_STEPS = 8
MULTIPLY_BLOCKS = (512, 512, 1024, 1024, 1024, 1024, 1024, 1024, 512, 512)


def whole_in(space):
    return pl.BlockSpec(memory_space=space)


def slots_of(owner):
    rows = owner.shape[1]
    across = jnp.broadcast_to(owner.astype(jnp.float32), (rows, rows))
    down = across.T
    first = lax.broadcasted_iota(jnp.int32, (rows, rows), 0)
    second = lax.broadcasted_iota(jnp.int32, (rows, rows), 1)
    earlier = jnp.where((across == down) & (first < second), 1, 0)
    return jnp.sum(earlier, axis=0, keepdims=True)


def place_kernel(swap_ref, owner_ref, integrals_ref, out_ref, both_ref, placed_ref, pick_ref, sem):
    rows, (lines, width) = integrals_ref.shape[0], out_ref.shape
    block = width // PLACE_STEPS
    fetches = [
        [
            pltpu.make_async_copy(
                integrals_ref.at[:, pl.ds(half * width + i * block, block)],
                both_ref.at[pl.ds(half * rows, rows), pl.ds(i * block, block)],
                sem.at[i, half],
            )
            for half in range(2)
        ]
        for i in range(PLACE_STEPS)
    ]
    for pair in fetches:
        for copy in pair:
            copy.start()

    owner = owner_ref[...]
    line = owner * BLOCK + slots_of(owner)
    number = lax.broadcasted_iota(jnp.int32, (lines, rows), 0)
    swap = swap_ref[0] * CAP
    pick_ref[:, :rows] = jnp.where(number == line + swap, 1.0, 0.0).astype(jnp.bfloat16)
    pick_ref[:, rows:] = jnp.where(number == line + (CAP - swap), 1.0, 0.0).astype(jnp.bfloat16)

    writes = []
    for i, pair in enumerate(fetches):
        for copy in pair:
            copy.wait()
        here = pl.ds(i * block, block)
        placed_ref[:, here] = jnp.dot(
            pick_ref[...], both_ref[:, here], preferred_element_type=jnp.float32
        ).astype(jnp.bfloat16)
        write = pltpu.make_async_copy(placed_ref.at[:, here], out_ref.at[:, here], sem.at[i, 2])
        write.start()
        writes.append(write)
    for write in writes:
        write.wait()


def place(swap, owner, integrals, peers):
    rows, cols = integrals.shape
    lines, width = peers * BLOCK, cols // 2
    return pl.pallas_call(
        place_kernel,
        in_specs=[whole_in(pltpu.SMEM), whole_in(pltpu.VMEM), whole_in(pl.ANY)],
        out_specs=whole_in(pl.ANY),
        out_shape=pltpu.HBM((lines, width), jnp.bfloat16),
        scratch_shapes=[
            pltpu.VMEM((2 * rows, width), jnp.bfloat16),
            pltpu.VMEM((lines, width), jnp.bfloat16),
            pltpu.VMEM((lines, 2 * rows), jnp.bfloat16),
            pltpu.SemaphoreType.DMA((PLACE_STEPS, 3)),
        ],
        compiler_params=pltpu.CompilerParams(vmem_limit_bytes=24 * 1024 * 1024),
        cost_estimate=pl.CostEstimate(
            flops=4 * lines * rows * width,
            bytes_accessed=2 * (2 * rows + lines) * width,
            transcendentals=0,
        ),
        name="place",
    )(swap, owner, pltpu.with_memory_space_constraint(integrals, pltpu.HBM))


def collect_kernel(amp_ref, mine_ref, left_ref, right_ref, top_ref, bottom_ref, out_ref, held_ref, sem):
    pairs = mine_ref.shape[0]
    count = out_ref.shape[0] // pairs
    shards = (
        (mine_ref, 0, 0),
        (left_ref, 1, 0),
        (right_ref, 3, 0),
        (top_ref, 2, 0),
        (bottom_ref, 2, pairs // 2),
    )
    fetches, writes = [], []
    for i, (ref, shift, skip) in enumerate(shards):
        at = (amp_ref[0] + count - shift) % count
        there = pl.ds(pl.multiple_of(at * pairs + skip, pairs // 2), ref.shape[0])
        fetches.append(pltpu.make_async_copy(ref, held_ref.at[there, :], sem.at[i, 0]))
        writes.append(
            pltpu.make_async_copy(held_ref.at[there, :], out_ref.at[there, :], sem.at[i, 1])
        )
    for copy in fetches:
        copy.start()
    for fetch, write in zip(fetches, writes):
        fetch.wait()
        write.start()
    for copy in writes:
        copy.wait()


def collect(amp, shards, count):
    pairs, cols = shards[0].shape
    return pl.pallas_call(
        collect_kernel,
        in_specs=[whole_in(pltpu.SMEM)] + [whole_in(pl.ANY)] * len(shards),
        out_specs=whole_in(pl.ANY),
        out_shape=pltpu.HBM((count * pairs, cols), jnp.bfloat16),
        scratch_shapes=[
            pltpu.VMEM((count * pairs, cols), jnp.bfloat16),
            pltpu.SemaphoreType.DMA((len(shards), 2)),
        ],
        compiler_params=pltpu.CompilerParams(vmem_limit_bytes=24 * 1024 * 1024),
        cost_estimate=pl.CostEstimate(
            flops=0, bytes_accessed=4 * count * pairs * cols, transcendentals=0
        ),
        name="collect",
    )(amp, *[pltpu.with_memory_space_constraint(x, pltpu.HBM) for x in shards])


def exchange(x, group):
    lines = x.shape[0]
    return jnp.where(group == 0, pltpu.roll(x, lines - CAP, 0), pltpu.roll(x, CAP, 0))


def multiply_kernel(rows_ref, amps_ref, out_ref, near_ref, held_ref, low_ref, high_ref, sem):
    lines, width = rows_ref.shape
    upper = lines // 2
    fetches, start = [], 0
    for i, block in enumerate(MULTIPLY_BLOCKS):
        fetches.append(
            [
                pltpu.make_async_copy(
                    source.at[:, pl.ds(first, block)], target.at[:, pl.ds(first, block)], sem.at[i, k]
                )
                for k, (source, target, first) in enumerate(
                    (
                        (rows_ref, near_ref, start),
                        (amps_ref, held_ref, start),
                        (amps_ref, held_ref, width + start),
                    )
                )
            ]
        )
        start += block
    for trio in fetches:
        for copy in trio:
            copy.start()

    start = 0
    for block, trio in zip(MULTIPLY_BLOCKS, fetches):
        for copy in trio:
            copy.wait()
        group = lax.broadcasted_iota(jnp.int32, (upper, block), 0) // CAP % 2
        here = pl.ds(start, block)
        first, second = near_ref[:upper, here], near_ref[upper:, here]
        for half, total_ref in enumerate((low_ref, high_ref)):
            product = lax.dot_general(
                jnp.where(group == half, first, second),
                held_ref[:, pl.ds(half * width + start, block)],
                (((1,), (1,)), ((), ())),
                preferred_element_type=jnp.float32,
            )
            if start == 0:
                total_ref[...] = product
            else:
                total_ref[...] += product
        start += block

    group = lax.broadcasted_iota(jnp.int32, low_ref.shape, 0) // CAP % 2
    value = low_ref[...] + exchange(high_ref[...], group)
    power = jnp.log2(jnp.maximum(jnp.max(jnp.abs(value), axis=1, keepdims=True), 2.0**-110))
    code = jnp.ceil(power * STEPS + 0.01).astype(jnp.int32)
    whole = jnp.round(value * (LARGEST / jnp.exp2(code.astype(jnp.float32) / STEPS)))
    whole = jnp.clip(whole, -LARGEST, LARGEST).astype(jnp.int32)
    whole = jnp.concatenate([whole, jnp.broadcast_to(code, (upper, LANES))], axis=1)
    blocks = whole.reshape(upper // BLOCK, 2, CAP, whole.shape[1])
    for j in range(2):
        first = j * (upper // BLOCK)
        out_ref[first : first + upper // BLOCK] = blocks[:, j].astype(jnp.int16)


def multiply(rows, amps):
    lines, width = rows.shape
    pairs = amps.shape[0]
    return pl.pallas_call(
        multiply_kernel,
        in_specs=[whole_in(pl.ANY)] * 2,
        out_specs=whole_in(pltpu.VMEM),
        out_shape=jax.ShapeDtypeStruct((lines // BLOCK, CAP, pairs + LANES), jnp.int16),
        scratch_shapes=[
            pltpu.VMEM((lines, width), jnp.bfloat16),
            pltpu.VMEM((pairs, 2 * width), jnp.bfloat16),
            pltpu.VMEM((lines // 2, pairs), jnp.float32),
            pltpu.VMEM((lines // 2, pairs), jnp.float32),
            pltpu.SemaphoreType.DMA((len(MULTIPLY_BLOCKS), 3)),
        ],
        compiler_params=pltpu.CompilerParams(vmem_limit_bytes=40 * 1024 * 1024),
        cost_estimate=pl.CostEstimate(
            flops=2 * lines * pairs * width,
            bytes_accessed=2 * (lines + 2 * pairs) * width,
            transcendentals=0,
        ),
        name="multiply",
    )(*[pltpu.with_memory_space_constraint(x, pltpu.HBM) for x in (rows, amps)])


def pick_kernel(owner_ref, lines_ref, out_ref):
    rows, pairs = out_ref.shape
    owner = owner_ref[...]
    line = owner * CAP + slots_of(owner)
    lines = lines_ref.shape[0] * CAP
    number = lax.broadcasted_iota(jnp.int32, (lines, rows), 0)
    pick = jnp.where(number == line, 1.0, 0.0).astype(jnp.bfloat16)
    whole = lines_ref[...].astype(jnp.int32).reshape(lines, lines_ref.shape[2])
    upper = whole >> 8
    lower = whole - (upper << 8)
    got = [
        lax.dot_general(
            pick,
            part.astype(jnp.float32).astype(jnp.bfloat16),
            (((0,), (0,)), ((), ())),
            preferred_element_type=jnp.float32,
        )
        for part in (upper, lower)
    ]
    picked = got[0] * 256.0 + got[1]
    unit = jnp.exp2(picked[:, pairs : pairs + 1] / STEPS) / LARGEST
    out_ref[...] = picked[:, :pairs] * unit


def pick(owner, lines):
    rows, pairs = owner.shape[1], lines.shape[2] - LANES
    return pl.pallas_call(
        pick_kernel,
        in_specs=[whole_in(pltpu.VMEM)] * 2,
        out_specs=whole_in(pltpu.VMEM),
        out_shape=jax.ShapeDtypeStruct((rows, pairs), jnp.float32),
        cost_estimate=pl.CostEstimate(
            flops=4 * rows * lines.size,
            bytes_accessed=2 * lines.size + 4 * rows * pairs,
            transcendentals=rows,
        ),
        name="pick",
    )(owner, lines)


def body(integrals, row_owner, lambda_amps):
    peers, amps = lax.axis_size("kblk"), lax.axis_size("amp")
    amp = lax.axis_index("amp").astype(jnp.int32)
    swap = (lax.axis_index("kblk") >= peers // 2).astype(jnp.int32)
    mine = lambda_amps[0]
    middle = mine.shape[0] // 2
    ahead = [(i, (i + 1) % amps) for i in range(amps)]
    back = [(i, (i - 1) % amps) for i in range(amps)]
    left, right = lax.ppermute(mine, "amp", ahead), lax.ppermute(mine, "amp", back)
    top = lax.ppermute(left[:middle], "amp", ahead)
    bottom = lax.ppermute(right[middle:], "amp", back)
    whole_lambda = collect(amp[None], (mine, left, right, top, bottom), amps)

    owner = row_owner.reshape(1, -1)
    placed = place(swap[None], owner, integrals, peers)
    width = placed.shape[1]
    arrived = lax.all_to_all(
        placed.reshape(peers, BLOCK, width), "kblk", split_axis=0, concat_axis=0, tiled=True
    )
    values = multiply(arrived.reshape(peers * BLOCK, width), whole_lambda)
    returned = lax.all_to_all(values, "kblk", split_axis=0, concat_axis=0, tiled=True)
    return pick(owner, returned)


def solution(mesh):
    placed = (P(("kblk", "amp"), None), P(("kblk", "amp"), None), P("kblk", "amp", None))
    return jax.shard_map(
        body, mesh=mesh, in_specs=placed, out_specs=P(("kblk", "amp"), None), check_vma=False
    )
```

time: 241 us -> 237 us (0.983)
  waiting for transfers between devices: 194 us -> 164 us
  blocking collectives: 0 us -> 19.1 us
  Pallas kernels: 16.6 us -> 28.4 us
  starting transfers between devices: 24.6 us -> 19.3 us
    ppermute x1, waiting for transfers between devices: 90.5 us -> 0.01 us  [body(): lax.ppermute(mine, 'amp', ahead)]
    ppermute x1, waiting for transfers between devices: 0.01 us -> 89.7 us  [body(): lax.ppermute(mine, 'amp', back)]
    ppermute x1, waiting for transfers between devices: 2.65 us -> 40.5 us  [body(): bottom = lax.ppermute(right[middle:], 'amp', back)]
    ppermute x1, waiting for transfers between devices: 41 us -> 6.56 us  [body(): top = lax.ppermute(left[:middle], 'amp', ahead)]
    all_to_all x0 -> x1, blocking collectives: none -> 19.1 us  [body(): lax.all_to_all(values, 'kblk', split_axis=0, concat_axis=0, tiled=True)]
    all_to_all x1 -> x0, waiting for transfers between devices: 17.1 us -> none  [body(): lax.all_to_all(values, 'kblk', split_axis=0, concat_axis=0, tiled=True)]
    all_to_all x1, waiting for transfers between devices: 42.5 us -> 27.1 us  [body(): lax.all_to_all(placed.reshape(peers, BLOCK, width), 'kblk', split_axis=0,...]
    pallas_call x1 -> x3, Pallas kernels: 10.7 us -> 22.6 us  [the longest x1 10.9 us: collect(): pl.pallas_call(collect_kernel, in_specs=[whole_in(pltpu.SMEM)] + [whole_i...]
  transfers between devices with their start and end apart: 6 -> 5, of which waited for: 5 -> 4; matrix products, arithmetic and copies ran while one was open for 1% -> 1% of each run, Pallas kernels for 0% -> 5%
where the time goes in v4:
time: 237 us; the launch traced here: 236 us
  waiting for transfers between devices  164 us (69%)
  Pallas kernels  28.4 us (12%)
  starting transfers between devices  19.3 us (8%)
  blocking collectives  19.1 us (8%)
  local copies, waits for them, and re-layouts  5.64 us (2%)
    ppermute x1, waiting for transfers between devices, body(): lax.ppermute(mine, 'amp', back)  89.7 us
    ppermute x1, waiting for transfers between devices, body(): bottom = lax.ppermute(right[middle:], 'amp', back)  40.5 us
    all_to_all x1, waiting for transfers between devices, body(): lax.all_to_all(placed.reshape(peers, BLOCK, width), 'kblk', split_axis=0,...  27.1 us
    all_to_all x1, blocking collectives, body(): lax.all_to_all(values, 'kblk', split_axis=0, concat_axis=0, tiled=True)  19.1 us
    all_to_all x1, starting transfers between devices, body(): lax.all_to_all(placed.reshape(peers, BLOCK, width), 'kblk', split_axis=0,...  13.4 us
    pallas_call x1, Pallas kernels, collect(): pl.pallas_call(collect_kernel, in_specs=[whole_in(pltpu.SMEM)] + [whole_i...  10.9 us
    pallas_call x1, Pallas kernels, multiply(): pl.pallas_call(multiply_kernel, in_specs=[whole_in(pl.ANY)] * 2, out_spec...  9.36 us
    ppermute x1, waiting for transfers between devices, body(): top = lax.ppermute(left[:middle], 'amp', ahead)  6.56 us
  transfers between devices with their start and end apart: 5, of which 4 were waited for; matrix products, arithmetic and copies ran while one was open for 1% of the time, Pallas kernels for 5%

profile of v4, /device:TPU:1, one launch (start us, length us, event | category | flops | bytes accessed | tf_op | source)
XLA Modules:
  0.0 236.4 jit_solution(7593274675669384720)
XLA Ops:
  0.0 0.0 copy-start
  0.0 0.7 copy-done
  0.7 5.8 %place.1 = bf16[512,8192]{1,0:T(8,128)(2,1)} custom-call(s32[1]{0:T(128)} %bitcast.1.swap_ref, s32[1,128]{1,0:T(1,128)S(1)} %bitcast.7, bf16[128,16384]{1,0:T(8,128)(2,1)} %integrals_ref.1), custom_call_target="tpu_custom_call" | custom-call | flops 2147483648 | bytes 12582912 | tf_op jit(solution)/shard_map/place/pallas_call | solution.py:74
  6.5 13.4 %all-to-all-start = ((bf16[64,8,8192]{2,1,0:T(8,128)(2,1)}), bf16[64,8,8192]{2,1,0:T(8,128)(2,1)}, u32[]{:S(2)}, u32[]{:S(2)}) async-start(bf16[64,8,8192]{2,1,0:T(8,128)(2,1)} %bitcast.8), calls=%async_computation | async-start | bytes 16777216 | tf_op jit(solution)/shard_map/all_to_all | solution.py:284
  19.9 2.6 %collective-permute-start.1 = (bf16[128,16384]{1,0:T(8,128)(2,1)}, bf16[128,16384]{1,0:T(8,128)(2,1)S(1)}, u32[]{:S(2)}, u32[]{:S(2)}) collective-permute-start(bf16[128,16384]{1,0:T(8,128)(2,1)} %bitcast.9), channel_id=1, source_target_pairs={{0,3},{1,0},{2,1},{3,2},{4,7},{5,4},{6,5},{7,6},{8,11},{9,8},{10,9... | collective-permute-start | bytes 12582920 | tf_op jit(solution)/shard_map/ppermute | solution.py:276
  22.4 0.0 collective-permute-start
  22.4 89.7 %collective-permute-done.1.right_ref = bf16[128,16384]{1,0:T(8,128)(2,1)S(1)} collective-permute-done((bf16[128,16384]{1,0:T(8,128)(2,1)}, bf16[128,16384]{1,0:T(8,128)(2,1)S(1)}, u32[]{:S(2)}, u32[]{:S(2)}) %collective-permute-start.1) | collective-permute-done | bytes 4194336 | tf_op jit(solution)/shard_map/ppermute | solution.py:276
  112.2 0.0 copy-start.1
  112.2 1.6 slice.9
  113.7 3.4 %collective-permute-start.3 = (bf16[64,16384]{1,0:T(8,128)(2,1)}, bf16[64,16384]{1,0:T(8,128)(2,1)S(1)}, u32[]{:S(2)}, u32[]{:S(2)}) collective-permute-start(bf16[64,16384]{1,0:T(8,128)(2,1)} %slice.9), channel_id=1, source_target_pairs={{0,3},{1,0},{2,1},{3,2},{4,7},{5,4},{6,5},{7,6},{8,11},{9,8},{10,9... | collective-permute-start | bytes 6291464 | tf_op jit(solution)/shard_map/ppermute | solution.py:278
  117.1 0.0 collective-permute-done.left_ref
  117.1 0.0 copy-start.2
  117.1 1.9 copy-done.2
  119.1 1.5 slice.8
  120.6 0.0 copy-done.1
  120.6 0.0 collective-permute-start.2
  120.6 40.5 %collective-permute-done.3.bottom_ref = bf16[64,16384]{1,0:T(8,128)(2,1)S(1)} collective-permute-done((bf16[64,16384]{1,0:T(8,128)(2,1)}, bf16[64,16384]{1,0:T(8,128)(2,1)S(1)}, u32[]{:S(2)}, u32[]{:S(2)}) %collective-permute-start.3) | collective-permute-done | bytes 2097184 | tf_op jit(solution)/shard_map/ppermute | solution.py:278
  161.1 0.0 copy-start.3
  161.1 6.6 %collective-permute-done.2.top_ref = bf16[64,16384]{1,0:T(8,128)(2,1)} collective-permute-done((bf16[64,16384]{1,0:T(8,128)(2,1)}, bf16[64,16384]{1,0:T(8,128)(2,1)}, u32[]{:S(2)}, u32[]{:S(2)}) %collective-permute-start.2) | collective-permute-done | bytes 2097184 | tf_op jit(solution)/shard_map/ppermute | solution.py:277
  167.6 0.0 copy-done.3
  167.6 10.9 %collect.1.amps_ref = bf16[512,16384]{1,0:T(8,128)(2,1)} custom-call(s32[1]{0:T(128)} %bitcast.4.amp_ref, bf16[128,16384]{1,0:T(8,128)(2,1)} %bitcast.11, bf16[128,16384]{1,0:T(8,128)(2,1)} %copy-done.2, bf16[128,16384]{1,0:T(8,128)(2,1)} %copy-done.1, bf16[64,16384]{1,0:T(8,128)(2,1)} %collective-permute-done.2.top_ref, bf16[64,16384]{1,0:T(8,128)(2,1)} %copy-done.3), custom_call_target="tpu_custom_call" | custom-call | bytes 33554432 | tf_op jit(solution)/shard_map/collect/pallas_call | solution.py:124
  178.6 27.1 %all-to-all-done = bf16[64,8,8192]{2,1,0:T(8,128)(2,1)} async-done(((bf16[64,8,8192]{2,1,0:T(8,128)(2,1)}), bf16[64,8,8192]{2,1,0:T(8,128)(2,1)}, u32[]{:S(2)}, u32[]{:S(2)}) %all-to-all-start) | async-done | bytes 8388640 | tf_op jit(solution)/shard_map/all_to_all | solution.py:284
  205.6 9.4 %multiply.1 = s16[64,4,640]{2,1,0:T(4,128)(2,1)S(1)} custom-call(bf16[512,8192]{1,0:T(8,128)(2,1)} %bitcast.3.rows_ref, bf16[512,16384]{1,0:T(8,128)(2,1)} %collect.1.amps_ref), custom_call_target="tpu_custom_call" | custom-call | flops 4294967296 | bytes 25165824 | tf_op jit(solution)/shard_map/multiply/pallas_call | solution.py:206
  215.0 19.1 %all_to_all.10.lines_ref = s16[64,4,640]{2,1,0:T(4,128)(2,1)} all-to-all(s16[64,4,640]{2,1,0:T(4,128)(2,1)S(1)} %multiply.1), channel_id=1, replica_groups=mesh['kblk'=64,'amp'=4] {'kblk'}, dimensions={0} | all-to-all | bytes 655360 | tf_op jit(solution)/shard_map/all_to_all | solution.py:288
  234.1 2.3 pick.1
Async XLA Ops:
  0.0 0.7 copy-start
  6.5 199.1 %all-to-all-start = ((bf16[64,8,8192]{2,1,0:T(8,128)(2,1)}), bf16[64,8,8192]{2,1,0:T(8,128)(2,1)}, u32[]{:S(2)}, u32[]{:S(2)}) async-start(bf16[64,8,8192]{2,1,0:T(8,128)(2,1)} %bitcast.8), calls=%async_computation | async-start | bytes 16777216 | tf_op jit(solution)/shard_map/all_to_all | solution.py:284
  19.9 92.3 %collective-permute-start.1 = (bf16[128,16384]{1,0:T(8,128)(2,1)}, bf16[128,16384]{1,0:T(8,128)(2,1)S(1)}, u32[]{:S(2)}, u32[]{:S(2)}) collective-permute-start(bf16[128,16384]{1,0:T(8,128)(2,1)} %bitcast.9), channel_id=1, source_target_pairs={{0,3},{1,0},{2,1},{3,2},{4,7},{5,4},{6,5},{7,6},{8,11},{9,8},{10,9... | collective-permute-start | bytes 12582920 | tf_op jit(solution)/shard_map/ppermute | solution.py:276
  22.4 94.7 %collective-permute-start = (bf16[128,16384]{1,0:T(8,128)(2,1)}, bf16[128,16384]{1,0:T(8,128)(2,1)S(1)}, u32[]{:S(2)}, u32[]{:S(2)}) collective-permute-start(bf16[128,16384]{1,0:T(8,128)(2,1)} %bitcast.10), channel_id=1, source_target_pairs={{0,1},{1,2},{2,3},{3,0},{4,5},{5,6},{6,7},{7,4},{8,9},{9,10},{10,1... | collective-permute-start | bytes 12582920 | tf_op jit(solution)/shard_map/ppermute | solution.py:276
  112.2 8.4 %copy-start.1 = (bf16[128,16384]{1,0:T(8,128)(2,1)}, bf16[128,16384]{1,0:T(8,128)(2,1)S(1)}, u32[]{:S(2)}) copy-start(bf16[128,16384]{1,0:T(8,128)(2,1)S(1)} %collective-permute-done.1.right_ref) | copy-start | bytes 12582916
  113.7 47.4 %collective-permute-start.3 = (bf16[64,16384]{1,0:T(8,128)(2,1)}, bf16[64,16384]{1,0:T(8,128)(2,1)S(1)}, u32[]{:S(2)}, u32[]{:S(2)}) collective-permute-start(bf16[64,16384]{1,0:T(8,128)(2,1)} %slice.9), channel_id=1, source_target_pairs={{0,3},{1,0},{2,1},{3,2},{4,7},{5,4},{6,5},{7,6},{8,11},{9,8},{10,9... | collective-permute-start | bytes 6291464 | tf_op jit(solution)/shard_map/ppermute | solution.py:278
  117.1 1.9 copy-start.2
  120.6 47.1 %collective-permute-start.2 = (bf16[64,16384]{1,0:T(8,128)(2,1)}, bf16[64,16384]{1,0:T(8,128)(2,1)}, u32[]{:S(2)}, u32[]{:S(2)}) collective-permute-start(bf16[64,16384]{1,0:T(8,128)(2,1)} %slice.8), channel_id=1, source_target_pairs={{0,1},{1,2},{2,3},{3,0},{4,5},{5,6},{6,7},{7,4},{8,9},{9,10},{10,1... | collective-permute-start | bytes 6291464 | tf_op jit(solution)/shard_map/ppermute | solution.py:277
  161.1 6.6 %copy-start.3 = (bf16[64,16384]{1,0:T(8,128)(2,1)}, bf16[64,16384]{1,0:T(8,128)(2,1)S(1)}, u32[]{:S(2)}) copy-start(bf16[64,16384]{1,0:T(8,128)(2,1)S(1)} %collective-permute-done.3.bottom_ref) | copy-start | bytes 6291460

commit v5 on v4

--- a/solution.py
+++ b/solution.py
@@ -10,8 +10,9 @@
 STEPS = 64
 LANES = 128
 BLOCK = 2 * CAP
-PLACE_STEPS = 8
-MULTIPLY_BLOCKS = (512, 512, 1024, 1024, 1024, 1024, 1024, 1024, 512, 512)
+PLACE_BLOCKS = (512, 1024, 1024, 1024, 1024, 1024, 1024, 1024, 512)
+MULTIPLY_BLOCKS = (512, 1024, 1024, 1024, 1024, 1024, 1024, 1024, 512)
+KEPT = 2
 
 
 def whole_in(space):
@@ -30,17 +31,17 @@
 
 def place_kernel(swap_ref, owner_ref, integrals_ref, out_ref, both_ref, placed_ref, pick_ref, sem):
     rows, (lines, width) = integrals_ref.shape[0], out_ref.shape
-    block = width // PLACE_STEPS
+    starts = [sum(PLACE_BLOCKS[:i]) for i in range(len(PLACE_BLOCKS))]
     fetches = [
         [
             pltpu.make_async_copy(
-                integrals_ref.at[:, pl.ds(half * width + i * block, block)],
-                both_ref.at[pl.ds(half * rows, rows), pl.ds(i * block, block)],
+                integrals_ref.at[:, pl.ds(half * width + start, block)],
+                both_ref.at[pl.ds(half * rows, rows), pl.ds(start, block)],
                 sem.at[i, half],
             )
             for half in range(2)
         ]
-        for i in range(PLACE_STEPS)
+        for i, (start, block) in enumerate(zip(starts, PLACE_BLOCKS))
     ]
     for pair in fetches:
         for copy in pair:
@@ -57,7 +58,7 @@
     for i, pair in enumerate(fetches):
         for copy in pair:
             copy.wait()
-        here = pl.ds(i * block, block)
+        here = pl.ds(starts[i], PLACE_BLOCKS[i])
         placed_ref[:, here] = jnp.dot(
             pick_ref[...], both_ref[:, here], preferred_element_type=jnp.float32
         ).astype(jnp.bfloat16)
@@ -80,7 +81,7 @@
             pltpu.VMEM((2 * rows, width), jnp.bfloat16),
             pltpu.VMEM((lines, width), jnp.bfloat16),
             pltpu.VMEM((lines, 2 * rows), jnp.bfloat16),
-            pltpu.SemaphoreType.DMA((PLACE_STEPS, 3)),
+            pltpu.SemaphoreType.DMA((len(PLACE_BLOCKS), 3)),
         ],
         compiler_params=pltpu.CompilerParams(vmem_limit_bytes=24 * 1024 * 1024),
         cost_estimate=pl.CostEstimate(
@@ -92,7 +93,10 @@
     )(swap, owner, pltpu.with_memory_space_constraint(integrals, pltpu.HBM))
 
 
-def collect_kernel(amp_ref, mine_ref, left_ref, right_ref, top_ref, bottom_ref, out_ref, held_ref, sem):
+def collect_kernel(
+    amp_ref, owner_ref, mine_ref, left_ref, right_ref, top_ref, bottom_ref,
+    out_ref, kept_ref, pick_ref, held_ref, sem,
+):
     pairs = mine_ref.shape[0]
     count = out_ref.shape[0] // pairs
     shards = (
@@ -112,20 +116,32 @@
         )
     for copy in fetches:
         copy.start()
+    owner = owner_ref[...]
+    number = lax.broadcasted_iota(jnp.int32, pick_ref.shape, 0)
+    here = number == owner * CAP + slots_of(owner)
+    pick_ref[...] = jnp.where(here, 1.0, 0.0).astype(jnp.bfloat16)
     for fetch, write in zip(fetches, writes):
         fetch.wait()
         write.start()
+    kept, width = kept_ref.shape[1] // 2, out_ref.shape[1] // 2
+    kept_ref[:, :kept] = held_ref[:, :kept]
+    kept_ref[:, kept:] = held_ref[:, width : width + kept]
     for copy in writes:
         copy.wait()
 
 
-def collect(amp, shards, count):
+def collect(amp, owner, shards, count, peers):
     pairs, cols = shards[0].shape
+    kept = 2 * sum(MULTIPLY_BLOCKS[:KEPT])
     return pl.pallas_call(
         collect_kernel,
-        in_specs=[whole_in(pltpu.SMEM)] + [whole_in(pl.ANY)] * len(shards),
-        out_specs=whole_in(pl.ANY),
-        out_shape=pltpu.HBM((count * pairs, cols), jnp.bfloat16),
+        in_specs=[whole_in(pltpu.SMEM), whole_in(pltpu.VMEM)] + [whole_in(pl.ANY)] * len(shards),
+        out_specs=[whole_in(pl.ANY), whole_in(pltpu.VMEM), whole_in(pltpu.VMEM)],
+        out_shape=[
+            pltpu.HBM((count * pairs, cols), jnp.bfloat16),
+            pltpu.VMEM((count * pairs, kept), jnp.bfloat16),
+            jax.ShapeDtypeStruct((peers * CAP, owner.shape[1]), jnp.bfloat16),
+        ],
         scratch_shapes=[
             pltpu.VMEM((count * pairs, cols), jnp.bfloat16),
             pltpu.SemaphoreType.DMA((len(shards), 2)),
@@ -135,7 +151,7 @@
             flops=0, bytes_accessed=4 * count * pairs * cols, transcendentals=0
         ),
         name="collect",
-    )(amp, *[pltpu.with_memory_space_constraint(x, pltpu.HBM) for x in shards])
+    )(amp, owner, *[pltpu.with_memory_space_constraint(x, pltpu.HBM) for x in shards])
 
 
 def exchange(x, group):
@@ -143,7 +159,9 @@
     return jnp.where(group == 0, pltpu.roll(x, lines - CAP, 0), pltpu.roll(x, CAP, 0))
 
 
-def multiply_kernel(rows_ref, amps_ref, out_ref, near_ref, held_ref, low_ref, high_ref, sem):
+def multiply_kernel(
+    rows_ref, amps_ref, kept_ref, out_ref, near_ref, held_ref, low_ref, high_ref, sem
+):
     lines, width = rows_ref.shape
     upper = lines // 2
     fetches, start = [], 0
@@ -158,7 +176,7 @@
                         (rows_ref, near_ref, start),
                         (amps_ref, held_ref, start),
                         (amps_ref, held_ref, width + start),
-                    )
+                    )[: 1 if i < KEPT else 3]
                 )
             ]
         )
@@ -174,10 +192,12 @@
         group = lax.broadcasted_iota(jnp.int32, (upper, block), 0) // CAP % 2
         here = pl.ds(start, block)
         first, second = near_ref[:upper, here], near_ref[upper:, here]
+        kept = start < kept_ref.shape[1] // 2
         for half, total_ref in enumerate((low_ref, high_ref)):
+            skip = half * (kept_ref.shape[1] // 2 if kept else width)
             product = lax.dot_general(
                 jnp.where(group == half, first, second),
-                held_ref[:, pl.ds(half * width + start, block)],
+                (kept_ref if kept else held_ref)[:, pl.ds(skip + start, block)],
                 (((1,), (1,)), ((), ())),
                 preferred_element_type=jnp.float32,
             )
@@ -200,12 +220,12 @@
         out_ref[first : first + upper // BLOCK] = blocks[:, j].astype(jnp.int16)
 
 
-def multiply(rows, amps):
+def multiply(rows, amps, kept):
     lines, width = rows.shape
     pairs = amps.shape[0]
     return pl.pallas_call(
         multiply_kernel,
-        in_specs=[whole_in(pl.ANY)] * 2,
+        in_specs=[whole_in(pl.ANY), whole_in(pl.ANY), whole_in(pltpu.VMEM)],
         out_specs=whole_in(pltpu.VMEM),
         out_shape=jax.ShapeDtypeStruct((lines // BLOCK, CAP, pairs + LANES), jnp.int16),
         scratch_shapes=[
@@ -222,22 +242,21 @@
             transcendentals=0,
         ),
         name="multiply",
-    )(*[pltpu.with_memory_space_constraint(x, pltpu.HBM) for x in (rows, amps)])
-
-
-def pick_kernel(owner_ref, lines_ref, out_ref):
-    rows, pairs = out_ref.shape
-    owner = owner_ref[...]
-    line = owner * CAP + slots_of(owner)
-    lines = lines_ref.shape[0] * CAP
-    number = lax.broadcasted_iota(jnp.int32, (lines, rows), 0)
-    pick = jnp.where(number == line, 1.0, 0.0).astype(jnp.bfloat16)
+    )(
+        pltpu.with_memory_space_constraint(rows, pltpu.HBM),
+        pltpu.with_memory_space_constraint(amps, pltpu.HBM),
+        pltpu.with_memory_space_constraint(kept, pltpu.VMEM),
+    )
+
+
+def pick_kernel(pick_ref, lines_ref, out_ref):
+    lines, pairs = pick_ref.shape[0], out_ref.shape[1]
     whole = lines_ref[...].astype(jnp.int32).reshape(lines, lines_ref.shape[2])
     upper = whole >> 8
     lower = whole - (upper << 8)
     got = [
         lax.dot_general(
-            pick,
+            pick_ref[...],
             part.astype(jnp.float32).astype(jnp.bfloat16),
             (((0,), (0,)), ((), ())),
             preferred_element_type=jnp.float32,
@@ -249,8 +268,8 @@
     out_ref[...] = picked[:, :pairs] * unit
 
 
-def pick(owner, lines):
-    rows, pairs = owner.shape[1], lines.shape[2] - LANES
+def pick(matrix, lines):
+    rows, pairs = matrix.shape[1], lines.shape[2] - LANES
     return pl.pallas_call(
         pick_kernel,
         in_specs=[whole_in(pltpu.VMEM)] * 2,
@@ -262,7 +281,7 @@
             transcendentals=rows,
         ),
         name="pick",
-    )(owner, lines)
+    )(matrix, pltpu.with_memory_space_constraint(lines, pltpu.VMEM))
 
 
 def body(integrals, row_owner, lambda_amps):
@@ -276,17 +295,19 @@
     left, right = lax.ppermute(mine, "amp", ahead), lax.ppermute(mine, "amp", back)
     top = lax.ppermute(left[:middle], "amp", ahead)
     bottom = lax.ppermute(right[middle:], "amp", back)
-    whole_lambda = collect(amp[None], (mine, left, right, top, bottom), amps)
-
     owner = row_owner.reshape(1, -1)
+    whole_lambda, kept, matrix = collect(
+        amp[None], owner, (mine, left, right, top, bottom), amps, peers
+    )
+
     placed = place(swap[None], owner, integrals, peers)
     width = placed.shape[1]
     arrived = lax.all_to_all(
         placed.reshape(peers, BLOCK, width), "kblk", split_axis=0, concat_axis=0, tiled=True
     )
-    values = multiply(arrived.reshape(peers * BLOCK, width), whole_lambda)
+    values = multiply(arrived.reshape(peers * BLOCK, width), whole_lambda, kept)
     returned = lax.all_to_all(values, "kblk", split_axis=0, concat_axis=0, tiled=True)
-    return pick(owner, returned)
+    return pick(matrix, returned)
 
 
 def solution(mesh):

time: 237 us -> 235 us (level)
  no operation moved by 1% of the time
where the time goes in v5:
time: 235 us
  waiting for transfers between devices  163 us (69%)
  Pallas kernels  27.3 us (12%)
  starting transfers between devices  19.3 us (8%)
  blocking collectives  18.9 us (8%)
  local copies, waits for them, and re-layouts  6.26 us (3%)
    ppermute x1, waiting for transfers between devices, body(): lax.ppermute(mine, 'amp', back)  89.7 us
    ppermute x1, waiting for transfers between devices, body(): bottom = lax.ppermute(right[middle:], 'amp', back)  40.5 us
    all_to_all x1, waiting for transfers between devices, body(): lax.all_to_all(placed.reshape(peers, BLOCK, width), 'kblk', split_axis=0,...  26.4 us
    all_to_all x1, blocking collectives, body(): lax.all_to_all(values, 'kblk', split_axis=0, concat_axis=0, tiled=True)  18.9 us
    all_to_all x1, starting transfers between devices, body(): lax.all_to_all(placed.reshape(peers, BLOCK, width), 'kblk', split_axis=0,...  13.4 us
    pallas_call x1, Pallas kernels, collect(): pl.pallas_call(collect_kernel, in_specs=[whole_in(pltpu.SMEM), whole_in(p...  10.9 us
    pallas_call x1, Pallas kernels, multiply(): pl.pallas_call(multiply_kernel, in_specs=[whole_in(pl.ANY), whole_in(pl.A...  8.5 us
    ppermute x1, waiting for transfers between devices, body(): top = lax.ppermute(left[:middle], 'amp', ahead)  6.56 us
  transfers between devices with their start and end apart: 5, of which 4 were waited for; matrix products, arithmetic and copies ran while one was open for 1% of the time, Pallas kernels for 5%

profile of v5, /device:TPU:1, one launch (start us, length us, event | category | flops | bytes accessed | tf_op | source)
XLA Modules:
  0.0 235.1 jit_solution(18407274869106310468)
XLA Ops:
  0.0 0.0 copy-start.1
  0.0 0.7 copy-done.1
  0.7 5.8 %place.1 = bf16[512,8192]{1,0:T(8,128)(2,1)} custom-call(s32[1]{0:T(128)} %bitcast.3.swap_ref, s32[1,128]{1,0:T(1,128)S(1)} %bitcast.6, bf16[128,16384]{1,0:T(8,128)(2,1)} %integrals_ref.1), custom_call_target="tpu_custom_call" | custom-call | flops 2147483648 | bytes 12582912 | tf_op jit(solution)/shard_map/place/pallas_call | solution.py:75
  6.4 13.4 %all-to-all-start = ((bf16[64,8,8192]{2,1,0:T(8,128)(2,1)}), bf16[64,8,8192]{2,1,0:T(8,128)(2,1)}, u32[]{:S(2)}, u32[]{:S(2)}) async-start(bf16[64,8,8192]{2,1,0:T(8,128)(2,1)} %bitcast.8), calls=%async_computation | async-start | bytes 16777216 | tf_op jit(solution)/shard_map/all_to_all | solution.py:305
  19.8 0.0 copy-start.2
  19.8 2.6 %collective-permute-start.1 = (bf16[128,16384]{1,0:T(8,128)(2,1)}, bf16[128,16384]{1,0:T(8,128)(2,1)S(1)}, u32[]{:S(2)}, u32[]{:S(2)}) collective-permute-start(bf16[128,16384]{1,0:T(8,128)(2,1)} %bitcast.9), channel_id=1, source_target_pairs={{0,3},{1,0},{2,1},{3,2},{4,7},{5,4},{6,5},{7,6},{8,11},{9,8},{10,9... | collective-permute-start | bytes 12582920 | tf_op jit(solution)/shard_map/ppermute | solution.py:295
  22.4 0.0 collective-permute-start
  22.4 89.7 %collective-permute-done.1.right_ref = bf16[128,16384]{1,0:T(8,128)(2,1)S(1)} collective-permute-done((bf16[128,16384]{1,0:T(8,128)(2,1)}, bf16[128,16384]{1,0:T(8,128)(2,1)S(1)}, u32[]{:S(2)}, u32[]{:S(2)}) %collective-permute-start.1) | collective-permute-done | bytes 4194336 | tf_op jit(solution)/shard_map/ppermute | solution.py:295
  112.1 0.0 copy-start.3
  112.1 1.6 slice.9
  113.7 3.4 %collective-permute-start.3 = (bf16[64,16384]{1,0:T(8,128)(2,1)}, bf16[64,16384]{1,0:T(8,128)(2,1)S(1)}, u32[]{:S(2)}, u32[]{:S(2)}) collective-permute-start(bf16[64,16384]{1,0:T(8,128)(2,1)} %slice.9), channel_id=1, source_target_pairs={{0,3},{1,0},{2,1},{3,2},{4,7},{5,4},{6,5},{7,6},{8,11},{9,8},{10,9... | collective-permute-start | bytes 6291464 | tf_op jit(solution)/shard_map/ppermute | solution.py:297
  117.1 0.0 collective-permute-done.left_ref
  117.1 0.0 copy-start.4
  117.1 2.0 copy-done.4
  119.0 1.5 slice.8
  120.5 0.0 copy-done.3
  120.5 0.0 collective-permute-start.2
  120.5 40.5 %collective-permute-done.3.bottom_ref = bf16[64,16384]{1,0:T(8,128)(2,1)S(1)} collective-permute-done((bf16[64,16384]{1,0:T(8,128)(2,1)}, bf16[64,16384]{1,0:T(8,128)(2,1)S(1)}, u32[]{:S(2)}, u32[]{:S(2)}) %collective-permute-start.3) | collective-permute-done | bytes 2097184 | tf_op jit(solution)/shard_map/ppermute | solution.py:297
  161.0 0.0 copy-start.5
  161.0 6.6 %collective-permute-done.2.top_ref = bf16[64,16384]{1,0:T(8,128)(2,1)} collective-permute-done((bf16[64,16384]{1,0:T(8,128)(2,1)}, bf16[64,16384]{1,0:T(8,128)(2,1)}, u32[]{:S(2)}, u32[]{:S(2)}) %collective-permute-start.2) | collective-permute-done | bytes 2097184 | tf_op jit(solution)/shard_map/ppermute | solution.py:296
  167.6 0.0 copy-done.5
  167.6 0.0 copy-done.2
  167.6 10.9 %collect.1 = (bf16[512,16384]{1,0:T(8,128)(2,1)}, bf16[512,3072]{1,0:T(8,128)(2,1)S(1)}, bf16[256,128]{1,0:T(8,128)(2,1)S(1)}) custom-call(s32[1]{0:T(128)} %bitcast.amp_ref, s32[1,128]{1,0:T(1,128)S(1)} %bitcast.7, bf16[128,16384]{1,0:T(8,128)(2,1)} %bitcast.11, bf16[128,16384]{1,0:T(8,128)(2,1)} %copy-done.4, bf16[128,16384]{1,0:T(8,128)(2,1)} %copy-done.3, ...), custom_call_target="tpu_custom_call" | custom-call | bytes 33554432 | tf_op jit(solution)/shard_map/collect/pallas_call | solution.py:136
  178.5 0.0 copy-start
  178.5 0.6 copy-done
  179.2 26.4 %all-to-all-done = bf16[64,8,8192]{2,1,0:T(8,128)(2,1)} async-done(((bf16[64,8,8192]{2,1,0:T(8,128)(2,1)}), bf16[64,8,8192]{2,1,0:T(8,128)(2,1)}, u32[]{:S(2)}, u32[]{:S(2)}) %all-to-all-start) | async-done | bytes 8388640 | tf_op jit(solution)/shard_map/all_to_all | solution.py:305
  205.6 8.5 %multiply.1 = s16[64,4,640]{2,1,0:T(4,128)(2,1)S(1)} custom-call(bf16[512,8192]{1,0:T(8,128)(2,1)} %bitcast.5.rows_ref, bf16[512,16384]{1,0:T(8,128)(2,1)} %get-tuple-element.9.amps_ref, bf16[512,3072]{1,0:T(8,128)(2,1)S(1)} %get-tuple-element.10.kept_ref), custom_call_target="tpu_custom_call" | custom-call | flops 4294967296 | bytes 25165824 | tf_op jit(solution)/shard_map/multiply/pallas_call | solution.py:226
  214.1 18.9 %all_to_all.10.lines_ref = s16[64,4,640]{2,1,0:T(4,128)(2,1)S(1)} all-to-all(s16[64,4,640]{2,1,0:T(4,128)(2,1)S(1)} %multiply.1), channel_id=1, replica_groups=mesh['kblk'=64,'amp'=4] {'kblk'}, dimensions={0} | all-to-all | bytes 655360 | tf_op jit(solution)/shard_map/all_to_all | solution.py:309
  233.0 2.1 pick.1
Async XLA Ops:
  0.0 0.7 copy-start.1
  6.4 199.1 %all-to-all-start = ((bf16[64,8,8192]{2,1,0:T(8,128)(2,1)}), bf16[64,8,8192]{2,1,0:T(8,128)(2,1)}, u32[]{:S(2)}, u32[]{:S(2)}) async-start(bf16[64,8,8192]{2,1,0:T(8,128)(2,1)} %bitcast.8), calls=%async_computation | async-start | bytes 16777216 | tf_op jit(solution)/shard_map/all_to_all | solution.py:305
  19.8 147.8 %copy-start.2 = (s32[128,1]{0,1:T(1,128)S(1)}, s32[128,1]{0,1:T(1,128)}, u32[]{:S(2)}) copy-start(s32[128,1]{0,1:T(1,128)} %param.4) | copy-start | bytes 1540
  19.8 92.3 %collective-permute-start.1 = (bf16[128,16384]{1,0:T(8,128)(2,1)}, bf16[128,16384]{1,0:T(8,128)(2,1)S(1)}, u32[]{:S(2)}, u32[]{:S(2)}) collective-permute-start(bf16[128,16384]{1,0:T(8,128)(2,1)} %bitcast.9), channel_id=1, source_target_pairs={{0,3},{1,0},{2,1},{3,2},{4,7},{5,4},{6,5},{7,6},{8,11},{9,8},{10,9... | collective-permute-start | bytes 12582920 | tf_op jit(solution)/shard_map/ppermute | solution.py:295
  22.4 94.7 %collective-permute-start = (bf16[128,16384]{1,0:T(8,128)(2,1)}, bf16[128,16384]{1,0:T(8,128)(2,1)S(1)}, u32[]{:S(2)}, u32[]{:S(2)}) collective-permute-start(bf16[128,16384]{1,0:T(8,128)(2,1)} %bitcast.10), channel_id=1, source_target_pairs={{0,1},{1,2},{2,3},{3,0},{4,5},{5,6},{6,7},{7,4},{8,9},{9,10},{10,1... | collective-permute-start | bytes 12582920 | tf_op jit(solution)/shard_map/ppermute | solution.py:295
  112.1 8.4 %copy-start.3 = (bf16[128,16384]{1,0:T(8,128)(2,1)}, bf16[128,16384]{1,0:T(8,128)(2,1)S(1)}, u32[]{:S(2)}) copy-start(bf16[128,16384]{1,0:T(8,128)(2,1)S(1)} %collective-permute-done.1.right_ref) | copy-start | bytes 12582916
  113.7 47.4 %collective-permute-start.3 = (bf16[64,16384]{1,0:T(8,128)(2,1)}, bf16[64,16384]{1,0:T(8,128)(2,1)S(1)}, u32[]{:S(2)}, u32[]{:S(2)}) collective-permute-start(bf16[64,16384]{1,0:T(8,128)(2,1)} %slice.9), channel_id=1, source_target_pairs={{0,3},{1,0},{2,1},{3,2},{4,7},{5,4},{6,5},{7,6},{8,11},{9,8},{10,9... | collective-permute-start | bytes 6291464 | tf_op jit(solution)/shard_map/ppermute | solution.py:297
  117.1 2.0 copy-start.4
  120.5 47.1 %collective-permute-start.2 = (bf16[64,16384]{1,0:T(8,128)(2,1)}, bf16[64,16384]{1,0:T(8,128)(2,1)}, u32[]{:S(2)}, u32[]{:S(2)}) collective-permute-start(bf16[64,16384]{1,0:T(8,128)(2,1)} %slice.8), channel_id=1, source_target_pairs={{0,1},{1,2},{2,3},{3,0},{4,5},{5,6},{6,7},{7,4},{8,9},{9,10},{10,1... | collective-permute-start | bytes 6291464 | tf_op jit(solution)/shard_map/ppermute | solution.py:296
  161.0 6.6 %copy-start.5 = (bf16[64,16384]{1,0:T(8,128)(2,1)}, bf16[64,16384]{1,0:T(8,128)(2,1)S(1)}, u32[]{:S(2)}) copy-start(bf16[64,16384]{1,0:T(8,128)(2,1)S(1)} %collective-permute-done.3.bottom_ref) | copy-start | bytes 6291460
  178.5 0.6 copy-start

commit v6 on v5

--- a/solution.py
+++ b/solution.py
@@ -11,7 +11,7 @@
 LANES = 128
 BLOCK = 2 * CAP
 PLACE_BLOCKS = (512, 1024, 1024, 1024, 1024, 1024, 1024, 1024, 512)
-MULTIPLY_BLOCKS = (512, 1024, 1024, 1024, 1024, 1024, 1024, 1024, 512)
+MULTIPLY_BLOCKS = (512, 1024, 1024, 1024, 1024, 1024, 1024, 1024, 256, 256)
 KEPT = 2
 
 
@@ -19,12 +19,15 @@
     return pl.BlockSpec(memory_space=space)
 
 
-def slots_of(owner):
+def slots_of(owner, upright=False):
     rows = owner.shape[1]
     across = jnp.broadcast_to(owner.astype(jnp.float32), (rows, rows))
     down = across.T
     first = lax.broadcasted_iota(jnp.int32, (rows, rows), 0)
     second = lax.broadcasted_iota(jnp.int32, (rows, rows), 1)
+    if upright:
+        earlier = jnp.where((across == down) & (second < first), 1, 0)
+        return down[:, :1].astype(jnp.int32), jnp.sum(earlier, axis=1, keepdims=True)
     earlier = jnp.where((across == down) & (first < second), 1, 0)
     return jnp.sum(earlier, axis=0, keepdims=True)
 
@@ -116,10 +119,12 @@
         )
     for copy in fetches:
         copy.start()
-    owner = owner_ref[...]
-    number = lax.broadcasted_iota(jnp.int32, pick_ref.shape, 0)
-    here = number == owner * CAP + slots_of(owner)
-    pick_ref[...] = jnp.where(here, 1.0, 0.0).astype(jnp.bfloat16)
+    owner, slot = slots_of(owner_ref[...], upright=True)
+    lines = pick_ref.shape[1] // 2
+    number = lax.broadcasted_iota(jnp.int32, (pick_ref.shape[0], lines), 1)
+    here = jnp.where(number == owner * CAP + slot, 1.0, 0.0)
+    pick_ref[:, :lines] = (here * 256.0).astype(jnp.bfloat16)
+    pick_ref[:, lines:] = here.astype(jnp.bfloat16)
     for fetch, write in zip(fetches, writes):
         fetch.wait()
         write.start()
@@ -140,7 +145,7 @@
         out_shape=[
             pltpu.HBM((count * pairs, cols), jnp.bfloat16),
             pltpu.VMEM((count * pairs, kept), jnp.bfloat16),
-            jax.ShapeDtypeStruct((peers * CAP, owner.shape[1]), jnp.bfloat16),
+            jax.ShapeDtypeStruct((owner.shape[1], 2 * peers * CAP), jnp.bfloat16),
         ],
         scratch_shapes=[
             pltpu.VMEM((count * pairs, cols), jnp.bfloat16),
@@ -250,26 +255,21 @@
 
 
 def pick_kernel(pick_ref, lines_ref, out_ref):
-    lines, pairs = pick_ref.shape[0], out_ref.shape[1]
+    lines, pairs = pick_ref.shape[1] // 2, out_ref.shape[1]
     whole = lines_ref[...].astype(jnp.int32).reshape(lines, lines_ref.shape[2])
     upper = whole >> 8
-    lower = whole - (upper << 8)
-    got = [
-        lax.dot_general(
-            pick_ref[...],
-            part.astype(jnp.float32).astype(jnp.bfloat16),
-            (((0,), (0,)), ((), ())),
-            preferred_element_type=jnp.float32,
-        )
-        for part in (upper, lower)
-    ]
-    picked = got[0] * 256.0 + got[1]
+    parts = jnp.concatenate([upper, whole - (upper << 8)], axis=0)
+    picked = jnp.dot(
+        pick_ref[...],
+        parts.astype(jnp.float32).astype(jnp.bfloat16),
+        preferred_element_type=jnp.float32,
+    )
     unit = jnp.exp2(picked[:, pairs : pairs + 1] / STEPS) / LARGEST
     out_ref[...] = picked[:, :pairs] * unit
 
 
 def pick(matrix, lines):
-    rows, pairs = matrix.shape[1], lines.shape[2] - LANES
+    rows, pairs = matrix.shape[0], lines.shape[2] - LANES
     return pl.pallas_call(
         pick_kernel,
         in_specs=[whole_in(pltpu.VMEM)] * 2,

time: 235 us -> 235 us (level)
  no operation moved by 1% of the time
where the time goes in v6:
time: 235 us
  waiting for transfers between devices  163 us (69%)
  Pallas kernels  27.4 us (12%)
  starting transfers between devices  19.3 us (8%)
  blocking collectives  18.9 us (8%)
  local copies, waits for them, and re-layouts  6.28 us (3%)
    ppermute x1, waiting for transfers between devices, body(): lax.ppermute(mine, 'amp', back)  89.7 us
    ppermute x1, waiting for transfers between devices, body(): bottom = lax.ppermute(right[middle:], 'amp', back)  40.5 us
    all_to_all x1, waiting for transfers between devices, body(): lax.all_to_all(placed.reshape(peers, BLOCK, width), 'kblk', split_axis=0,...  26.4 us
    all_to_all x1, blocking collectives, body(): lax.all_to_all(values, 'kblk', split_axis=0, concat_axis=0, tiled=True)  18.9 us
    all_to_all x1, starting transfers between devices, body(): lax.all_to_all(placed.reshape(peers, BLOCK, width), 'kblk', split_axis=0,...  13.4 us
    pallas_call x1, Pallas kernels, collect(): pl.pallas_call(collect_kernel, in_specs=[whole_in(pltpu.SMEM), whole_in(p...  10.9 us
    pallas_call x1, Pallas kernels, multiply(): pl.pallas_call(multiply_kernel, in_specs=[whole_in(pl.ANY), whole_in(pl.A...  8.63 us
    ppermute x1, waiting for transfers between devices, body(): top = lax.ppermute(left[:middle], 'amp', ahead)  6.56 us
  transfers between devices with their start and end apart: 5, of which 4 were waited for; matrix products, arithmetic and copies ran while one was open for 1% of the time, Pallas kernels for 5%

profile of v6, /device:TPU:1, one launch (start us, length us, event | category | flops | bytes accessed | tf_op | source)
XLA Modules:
  0.0 235.3 jit_solution(14563150984539208491)
XLA Ops:
  0.0 0.0 copy-start.1
  0.0 0.7 copy-done.1
  0.7 5.8 %place.1 = bf16[512,8192]{1,0:T(8,128)(2,1)} custom-call(s32[1]{0:T(128)} %bitcast.3.swap_ref, s32[1,128]{1,0:T(1,128)S(1)} %bitcast.6, bf16[128,16384]{1,0:T(8,128)(2,1)} %integrals_ref.1), custom_call_target="tpu_custom_call" | custom-call | flops 2147483648 | bytes 12582912 | tf_op jit(solution)/shard_map/place/pallas_call | solution.py:78
  6.4 13.4 %all-to-all-start = ((bf16[64,8,8192]{2,1,0:T(8,128)(2,1)}), bf16[64,8,8192]{2,1,0:T(8,128)(2,1)}, u32[]{:S(2)}, u32[]{:S(2)}) async-start(bf16[64,8,8192]{2,1,0:T(8,128)(2,1)} %bitcast.8), calls=%async_computation | async-start | bytes 16777216 | tf_op jit(solution)/shard_map/all_to_all | solution.py:305
  19.8 0.0 copy-start.2
  19.8 2.6 %collective-permute-start.1 = (bf16[128,16384]{1,0:T(8,128)(2,1)}, bf16[128,16384]{1,0:T(8,128)(2,1)S(1)}, u32[]{:S(2)}, u32[]{:S(2)}) collective-permute-start(bf16[128,16384]{1,0:T(8,128)(2,1)} %bitcast.9), channel_id=1, source_target_pairs={{0,3},{1,0},{2,1},{3,2},{4,7},{5,4},{6,5},{7,6},{8,11},{9,8},{10,9... | collective-permute-start | bytes 12582920 | tf_op jit(solution)/shard_map/ppermute | solution.py:295
  22.4 0.0 collective-permute-start
  22.4 89.7 %collective-permute-done.1.right_ref = bf16[128,16384]{1,0:T(8,128)(2,1)S(1)} collective-permute-done((bf16[128,16384]{1,0:T(8,128)(2,1)}, bf16[128,16384]{1,0:T(8,128)(2,1)S(1)}, u32[]{:S(2)}, u32[]{:S(2)}) %collective-permute-start.1) | collective-permute-done | bytes 4194336 | tf_op jit(solution)/shard_map/ppermute | solution.py:295
  112.1 0.0 copy-start.3
  112.1 1.6 slice.9
  113.7 3.4 %collective-permute-start.3 = (bf16[64,16384]{1,0:T(8,128)(2,1)}, bf16[64,16384]{1,0:T(8,128)(2,1)S(1)}, u32[]{:S(2)}, u32[]{:S(2)}) collective-permute-start(bf16[64,16384]{1,0:T(8,128)(2,1)} %slice.9), channel_id=1, source_target_pairs={{0,3},{1,0},{2,1},{3,2},{4,7},{5,4},{6,5},{7,6},{8,11},{9,8},{10,9... | collective-permute-start | bytes 6291464 | tf_op jit(solution)/shard_map/ppermute | solution.py:297
  117.1 0.0 collective-permute-done.left_ref
  117.1 0.0 copy-start.4
  117.1 2.0 copy-done.4
  119.0 1.5 slice.8
  120.5 0.0 copy-done.3
  120.5 0.0 collective-permute-start.2
  120.5 40.5 %collective-permute-done.3.bottom_ref = bf16[64,16384]{1,0:T(8,128)(2,1)S(1)} collective-permute-done((bf16[64,16384]{1,0:T(8,128)(2,1)}, bf16[64,16384]{1,0:T(8,128)(2,1)S(1)}, u32[]{:S(2)}, u32[]{:S(2)}) %collective-permute-start.3) | collective-permute-done | bytes 2097184 | tf_op jit(solution)/shard_map/ppermute | solution.py:297
  161.0 0.0 copy-start.5
  161.0 6.6 %collective-permute-done.2.top_ref = bf16[64,16384]{1,0:T(8,128)(2,1)} collective-permute-done((bf16[64,16384]{1,0:T(8,128)(2,1)}, bf16[64,16384]{1,0:T(8,128)(2,1)}, u32[]{:S(2)}, u32[]{:S(2)}) %collective-permute-start.2) | collective-permute-done | bytes 2097184 | tf_op jit(solution)/shard_map/ppermute | solution.py:296
  167.6 0.0 copy-done.5
  167.6 0.0 copy-done.2
  167.6 10.9 %collect.1 = (bf16[512,16384]{1,0:T(8,128)(2,1)}, bf16[512,3072]{1,0:T(8,128)(2,1)S(1)}, bf16[128,512]{1,0:T(8,128)(2,1)S(1)}) custom-call(s32[1]{0:T(128)} %bitcast.amp_ref, s32[1,128]{1,0:T(1,128)S(1)} %bitcast.7, bf16[128,16384]{1,0:T(8,128)(2,1)} %bitcast.11, bf16[128,16384]{1,0:T(8,128)(2,1)} %copy-done.4, bf16[128,16384]{1,0:T(8,128)(2,1)} %copy-done.3, ...), custom_call_target="tpu_custom_call" | custom-call | bytes 33554432 | tf_op jit(solution)/shard_map/collect/pallas_call | solution.py:141
  178.5 0.0 copy-start
  178.5 0.6 copy-done
  179.2 26.4 %all-to-all-done = bf16[64,8,8192]{2,1,0:T(8,128)(2,1)} async-done(((bf16[64,8,8192]{2,1,0:T(8,128)(2,1)}), bf16[64,8,8192]{2,1,0:T(8,128)(2,1)}, u32[]{:S(2)}, u32[]{:S(2)}) %all-to-all-start) | async-done | bytes 8388640 | tf_op jit(solution)/shard_map/all_to_all | solution.py:305
  205.6 8.6 %multiply.1 = s16[64,4,640]{2,1,0:T(4,128)(2,1)S(1)} custom-call(bf16[512,8192]{1,0:T(8,128)(2,1)} %bitcast.5.rows_ref, bf16[512,16384]{1,0:T(8,128)(2,1)} %get-tuple-element.9.amps_ref, bf16[512,3072]{1,0:T(8,128)(2,1)S(1)} %get-tuple-element.10.kept_ref), custom_call_target="tpu_custom_call" | custom-call | flops 4294967296 | bytes 25165824 | tf_op jit(solution)/shard_map/multiply/pallas_call | solution.py:231
  214.2 18.9 %all_to_all.10.lines_ref = s16[64,4,640]{2,1,0:T(4,128)(2,1)S(1)} all-to-all(s16[64,4,640]{2,1,0:T(4,128)(2,1)S(1)} %multiply.1), channel_id=1, replica_groups=mesh['kblk'=64,'amp'=4] {'kblk'}, dimensions={0} | all-to-all | bytes 655360 | tf_op jit(solution)/shard_map/all_to_all | solution.py:309
  233.2 2.1 pick.1
Async XLA Ops:
  0.0 0.7 copy-start.1
  6.4 199.1 %all-to-all-start = ((bf16[64,8,8192]{2,1,0:T(8,128)(2,1)}), bf16[64,8,8192]{2,1,0:T(8,128)(2,1)}, u32[]{:S(2)}, u32[]{:S(2)}) async-start(bf16[64,8,8192]{2,1,0:T(8,128)(2,1)} %bitcast.8), calls=%async_computation | async-start | bytes 16777216 | tf_op jit(solution)/shard_map/all_to_all | solution.py:305
  19.8 147.8 %copy-start.2 = (s32[128,1]{0,1:T(1,128)S(1)}, s32[128,1]{0,1:T(1,128)}, u32[]{:S(2)}) copy-start(s32[128,1]{0,1:T(1,128)} %param.4) | copy-start | bytes 1540
  19.8 92.3 %collective-permute-start.1 = (bf16[128,16384]{1,0:T(8,128)(2,1)}, bf16[128,16384]{1,0:T(8,128)(2,1)S(1)}, u32[]{:S(2)}, u32[]{:S(2)}) collective-permute-start(bf16[128,16384]{1,0:T(8,128)(2,1)} %bitcast.9), channel_id=1, source_target_pairs={{0,3},{1,0},{2,1},{3,2},{4,7},{5,4},{6,5},{7,6},{8,11},{9,8},{10,9... | collective-permute-start | bytes 12582920 | tf_op jit(solution)/shard_map/ppermute | solution.py:295
  22.4 94.7 %collective-permute-start = (bf16[128,16384]{1,0:T(8,128)(2,1)}, bf16[128,16384]{1,0:T(8,128)(2,1)S(1)}, u32[]{:S(2)}, u32[]{:S(2)}) collective-permute-start(bf16[128,16384]{1,0:T(8,128)(2,1)} %bitcast.10), channel_id=1, source_target_pairs={{0,1},{1,2},{2,3},{3,0},{4,5},{5,6},{6,7},{7,4},{8,9},{9,10},{10,1... | collective-permute-start | bytes 12582920 | tf_op jit(solution)/shard_map/ppermute | solution.py:295
  112.1 8.4 %copy-start.3 = (bf16[128,16384]{1,0:T(8,128)(2,1)}, bf16[128,16384]{1,0:T(8,128)(2,1)S(1)}, u32[]{:S(2)}) copy-start(bf16[128,16384]{1,0:T(8,128)(2,1)S(1)} %collective-permute-done.1.right_ref) | copy-start | bytes 12582916
  113.7 47.4 %collective-permute-start.3 = (bf16[64,16384]{1,0:T(8,128)(2,1)}, bf16[64,16384]{1,0:T(8,128)(2,1)S(1)}, u32[]{:S(2)}, u32[]{:S(2)}) collective-permute-start(bf16[64,16384]{1,0:T(8,128)(2,1)} %slice.9), channel_id=1, source_target_pairs={{0,3},{1,0},{2,1},{3,2},{4,7},{5,4},{6,5},{7,6},{8,11},{9,8},{10,9... | collective-permute-start | bytes 6291464 | tf_op jit(solution)/shard_map/ppermute | solution.py:297
  117.1 2.0 copy-start.4
  120.5 47.1 %collective-permute-start.2 = (bf16[64,16384]{1,0:T(8,128)(2,1)}, bf16[64,16384]{1,0:T(8,128)(2,1)}, u32[]{:S(2)}, u32[]{:S(2)}) collective-permute-start(bf16[64,16384]{1,0:T(8,128)(2,1)} %slice.8), channel_id=1, source_target_pairs={{0,1},{1,2},{2,3},{3,0},{4,5},{5,6},{6,7},{7,4},{8,9},{9,10},{10,1... | collective-permute-start | bytes 6291464 | tf_op jit(solution)/shard_map/ppermute | solution.py:296
  161.0 6.6 %copy-start.5 = (bf16[64,16384]{1,0:T(8,128)(2,1)}, bf16[64,16384]{1,0:T(8,128)(2,1)S(1)}, u32[]{:S(2)}) copy-start(bf16[64,16384]{1,0:T(8,128)(2,1)S(1)} %collective-permute-done.3.bottom_ref) | copy-start | bytes 6291460
  178.5 0.6 copy-start

commit v7 on v6

--- a/solution.py
+++ b/solution.py
@@ -201,8 +201,8 @@
         for half, total_ref in enumerate((low_ref, high_ref)):
             skip = half * (kept_ref.shape[1] // 2 if kept else width)
             product = lax.dot_general(
+                (kept_ref if kept else held_ref)[:, pl.ds(skip + start, block)],
                 jnp.where(group == half, first, second),
-                (kept_ref if kept else held_ref)[:, pl.ds(skip + start, block)],
                 (((1,), (1,)), ((), ())),
                 preferred_element_type=jnp.float32,
             )
@@ -212,8 +212,9 @@
                 total_ref[...] += product
         start += block
 
-    group = lax.broadcasted_iota(jnp.int32, low_ref.shape, 0) // CAP % 2
-    value = low_ref[...] + exchange(high_ref[...], group)
+    low, high = low_ref[...].T, high_ref[...].T
+    group = lax.broadcasted_iota(jnp.int32, low.shape, 0) // CAP % 2
+    value = low + exchange(high, group)
     power = jnp.log2(jnp.maximum(jnp.max(jnp.abs(value), axis=1, keepdims=True), 2.0**-110))
     code = jnp.ceil(power * STEPS + 0.01).astype(jnp.int32)
     whole = jnp.round(value * (LARGEST / jnp.exp2(code.astype(jnp.float32) / STEPS)))
@@ -236,8 +237,8 @@
         scratch_shapes=[
             pltpu.VMEM((lines, width), jnp.bfloat16),
             pltpu.VMEM((pairs, 2 * width), jnp.bfloat16),
-            pltpu.VMEM((lines // 2, pairs), jnp.float32),
-            pltpu.VMEM((lines // 2, pairs), jnp.float32),
+            pltpu.VMEM((pairs, lines // 2), jnp.float32),
+            pltpu.VMEM((pairs, lines // 2), jnp.float32),
             pltpu.SemaphoreType.DMA((len(MULTIPLY_BLOCKS), 3)),
         ],
         compiler_params=pltpu.CompilerParams(vmem_limit_bytes=40 * 1024 * 1024),

time: 235 us -> 236 us (level)
  no operation moved by 1% of the time
where the time goes in v7:
time: 236 us
  waiting for transfers between devices  163 us (69%)
  Pallas kernels  27.7 us (12%)
  starting transfers between devices  19.3 us (8%)
  blocking collectives  19 us (8%)
  local copies, waits for them, and re-layouts  6.28 us (3%)
    ppermute x1, waiting for transfers between devices, body(): lax.ppermute(mine, 'amp', back)  89.7 us
    ppermute x1, waiting for transfers between devices, body(): bottom = lax.ppermute(right[middle:], 'amp', back)  40.5 us
    all_to_all x1, waiting for transfers between devices, body(): lax.all_to_all(placed.reshape(peers, BLOCK, width), 'kblk', split_axis=0,...  26.4 us
    all_to_all x1, blocking collectives, body(): lax.all_to_all(values, 'kblk', split_axis=0, concat_axis=0, tiled=True)  19 us
    all_to_all x1, starting transfers between devices, body(): lax.all_to_all(placed.reshape(peers, BLOCK, width), 'kblk', split_axis=0,...  13.4 us
    pallas_call x1, Pallas kernels, collect(): pl.pallas_call(collect_kernel, in_specs=[whole_in(pltpu.SMEM), whole_in(p...  10.9 us
    pallas_call x1, Pallas kernels, multiply(): pl.pallas_call(multiply_kernel, in_specs=[whole_in(pl.ANY), whole_in(pl.A...  8.86 us
    ppermute x1, waiting for transfers between devices, body(): top = lax.ppermute(left[:middle], 'amp', ahead)  6.56 us
  transfers between devices with their start and end apart: 5, of which 4 were waited for; matrix products, arithmetic and copies ran while one was open for 1% of the time, Pallas kernels for 5%

profile of v7, /device:TPU:1, one launch (start us, length us, event | category | flops | bytes accessed | tf_op | source)
XLA Modules:
  0.0 235.5 jit_solution(12992625637059705730)
XLA Ops:
  0.0 0.0 copy-start.1
  0.0 0.7 copy-done.1
  0.7 5.8 %place.1 = bf16[512,8192]{1,0:T(8,128)(2,1)} custom-call(s32[1]{0:T(128)} %bitcast.3.swap_ref, s32[1,128]{1,0:T(1,128)S(1)} %bitcast.6, bf16[128,16384]{1,0:T(8,128)(2,1)} %integrals_ref.1), custom_call_target="tpu_custom_call" | custom-call | flops 2147483648 | bytes 12582912 | tf_op jit(solution)/shard_map/place/pallas_call | solution.py:78
  6.4 13.4 %all-to-all-start = ((bf16[64,8,8192]{2,1,0:T(8,128)(2,1)}), bf16[64,8,8192]{2,1,0:T(8,128)(2,1)}, u32[]{:S(2)}, u32[]{:S(2)}) async-start(bf16[64,8,8192]{2,1,0:T(8,128)(2,1)} %bitcast.8), calls=%async_computation | async-start | bytes 16777216 | tf_op jit(solution)/shard_map/all_to_all | solution.py:306
  19.8 0.0 copy-start.2
  19.8 2.6 %collective-permute-start.1 = (bf16[128,16384]{1,0:T(8,128)(2,1)}, bf16[128,16384]{1,0:T(8,128)(2,1)S(1)}, u32[]{:S(2)}, u32[]{:S(2)}) collective-permute-start(bf16[128,16384]{1,0:T(8,128)(2,1)} %bitcast.9), channel_id=1, source_target_pairs={{0,3},{1,0},{2,1},{3,2},{4,7},{5,4},{6,5},{7,6},{8,11},{9,8},{10,9... | collective-permute-start | bytes 12582920 | tf_op jit(solution)/shard_map/ppermute | solution.py:296
  22.4 0.0 collective-permute-start
  22.4 89.7 %collective-permute-done.1.right_ref = bf16[128,16384]{1,0:T(8,128)(2,1)S(1)} collective-permute-done((bf16[128,16384]{1,0:T(8,128)(2,1)}, bf16[128,16384]{1,0:T(8,128)(2,1)S(1)}, u32[]{:S(2)}, u32[]{:S(2)}) %collective-permute-start.1) | collective-permute-done | bytes 4194336 | tf_op jit(solution)/shard_map/ppermute | solution.py:296
  112.1 0.0 copy-start.3
  112.1 1.6 slice.9
  113.7 3.4 %collective-permute-start.3 = (bf16[64,16384]{1,0:T(8,128)(2,1)}, bf16[64,16384]{1,0:T(8,128)(2,1)S(1)}, u32[]{:S(2)}, u32[]{:S(2)}) collective-permute-start(bf16[64,16384]{1,0:T(8,128)(2,1)} %slice.9), channel_id=1, source_target_pairs={{0,3},{1,0},{2,1},{3,2},{4,7},{5,4},{6,5},{7,6},{8,11},{9,8},{10,9... | collective-permute-start | bytes 6291464 | tf_op jit(solution)/shard_map/ppermute | solution.py:298
  117.1 0.0 collective-permute-done.left_ref
  117.1 0.0 copy-start.4
  117.1 2.0 copy-done.4
  119.0 1.5 slice.8
  120.5 0.0 copy-done.3
  120.5 0.0 collective-permute-start.2
  120.5 40.5 %collective-permute-done.3.bottom_ref = bf16[64,16384]{1,0:T(8,128)(2,1)S(1)} collective-permute-done((bf16[64,16384]{1,0:T(8,128)(2,1)}, bf16[64,16384]{1,0:T(8,128)(2,1)S(1)}, u32[]{:S(2)}, u32[]{:S(2)}) %collective-permute-start.3) | collective-permute-done | bytes 2097184 | tf_op jit(solution)/shard_map/ppermute | solution.py:298
  161.0 0.0 copy-start.5
  161.0 6.6 %collective-permute-done.2.top_ref = bf16[64,16384]{1,0:T(8,128)(2,1)} collective-permute-done((bf16[64,16384]{1,0:T(8,128)(2,1)}, bf16[64,16384]{1,0:T(8,128)(2,1)}, u32[]{:S(2)}, u32[]{:S(2)}) %collective-permute-start.2) | collective-permute-done | bytes 2097184 | tf_op jit(solution)/shard_map/ppermute | solution.py:297
  167.6 0.0 copy-done.5
  167.6 0.0 copy-done.2
  167.6 10.9 %collect.1 = (bf16[512,16384]{1,0:T(8,128)(2,1)}, bf16[512,3072]{1,0:T(8,128)(2,1)S(1)}, bf16[128,512]{1,0:T(8,128)(2,1)S(1)}) custom-call(s32[1]{0:T(128)} %bitcast.amp_ref, s32[1,128]{1,0:T(1,128)S(1)} %bitcast.7, bf16[128,16384]{1,0:T(8,128)(2,1)} %bitcast.11, bf16[128,16384]{1,0:T(8,128)(2,1)} %copy-done.4, bf16[128,16384]{1,0:T(8,128)(2,1)} %copy-done.3, ...), custom_call_target="tpu_custom_call" | custom-call | bytes 33554432 | tf_op jit(solution)/shard_map/collect/pallas_call | solution.py:141
  178.5 0.0 copy-start
  178.5 0.6 copy-done
  179.2 26.4 %all-to-all-done = bf16[64,8,8192]{2,1,0:T(8,128)(2,1)} async-done(((bf16[64,8,8192]{2,1,0:T(8,128)(2,1)}), bf16[64,8,8192]{2,1,0:T(8,128)(2,1)}, u32[]{:S(2)}, u32[]{:S(2)}) %all-to-all-start) | async-done | bytes 8388640 | tf_op jit(solution)/shard_map/all_to_all | solution.py:306
  205.6 8.9 %multiply.1 = s16[64,4,640]{2,1,0:T(4,128)(2,1)S(1)} custom-call(bf16[512,8192]{1,0:T(8,128)(2,1)} %bitcast.5.rows_ref, bf16[512,16384]{1,0:T(8,128)(2,1)} %get-tuple-element.9.amps_ref, bf16[512,3072]{1,0:T(8,128)(2,1)S(1)} %get-tuple-element.10.kept_ref), custom_call_target="tpu_custom_call" | custom-call | flops 4294967296 | bytes 25165824 | tf_op jit(solution)/shard_map/multiply/pallas_call | solution.py:232
  214.4 19.0 %all_to_all.10.lines_ref = s16[64,4,640]{2,1,0:T(4,128)(2,1)S(1)} all-to-all(s16[64,4,640]{2,1,0:T(4,128)(2,1)S(1)} %multiply.1), channel_id=1, replica_groups=mesh['kblk'=64,'amp'=4] {'kblk'}, dimensions={0} | all-to-all | bytes 655360 | tf_op jit(solution)/shard_map/all_to_all | solution.py:310
  233.4 2.1 pick.1
Async XLA Ops:
  0.0 0.7 copy-start.1
  6.4 199.1 %all-to-all-start = ((bf16[64,8,8192]{2,1,0:T(8,128)(2,1)}), bf16[64,8,8192]{2,1,0:T(8,128)(2,1)}, u32[]{:S(2)}, u32[]{:S(2)}) async-start(bf16[64,8,8192]{2,1,0:T(8,128)(2,1)} %bitcast.8), calls=%async_computation | async-start | bytes 16777216 | tf_op jit(solution)/shard_map/all_to_all | solution.py:306
  19.8 147.8 %copy-start.2 = (s32[128,1]{0,1:T(1,128)S(1)}, s32[128,1]{0,1:T(1,128)}, u32[]{:S(2)}) copy-start(s32[128,1]{0,1:T(1,128)} %param.4) | copy-start | bytes 1540
  19.8 92.3 %collective-permute-start.1 = (bf16[128,16384]{1,0:T(8,128)(2,1)}, bf16[128,16384]{1,0:T(8,128)(2,1)S(1)}, u32[]{:S(2)}, u32[]{:S(2)}) collective-permute-start(bf16[128,16384]{1,0:T(8,128)(2,1)} %bitcast.9), channel_id=1, source_target_pairs={{0,3},{1,0},{2,1},{3,2},{4,7},{5,4},{6,5},{7,6},{8,11},{9,8},{10,9... | collective-permute-start | bytes 12582920 | tf_op jit(solution)/shard_map/ppermute | solution.py:296
  22.4 94.7 %collective-permute-start = (bf16[128,16384]{1,0:T(8,128)(2,1)}, bf16[128,16384]{1,0:T(8,128)(2,1)S(1)}, u32[]{:S(2)}, u32[]{:S(2)}) collective-permute-start(bf16[128,16384]{1,0:T(8,128)(2,1)} %bitcast.10), channel_id=1, source_target_pairs={{0,1},{1,2},{2,3},{3,0},{4,5},{5,6},{6,7},{7,4},{8,9},{9,10},{10,1... | collective-permute-start | bytes 12582920 | tf_op jit(solution)/shard_map/ppermute | solution.py:296
  112.1 8.4 %copy-start.3 = (bf16[128,16384]{1,0:T(8,128)(2,1)}, bf16[128,16384]{1,0:T(8,128)(2,1)S(1)}, u32[]{:S(2)}) copy-start(bf16[128,16384]{1,0:T(8,128)(2,1)S(1)} %collective-permute-done.1.right_ref) | copy-start | bytes 12582916
  113.7 47.4 %collective-permute-start.3 = (bf16[64,16384]{1,0:T(8,128)(2,1)}, bf16[64,16384]{1,0:T(8,128)(2,1)S(1)}, u32[]{:S(2)}, u32[]{:S(2)}) collective-permute-start(bf16[64,16384]{1,0:T(8,128)(2,1)} %slice.9), channel_id=1, source_target_pairs={{0,3},{1,0},{2,1},{3,2},{4,7},{5,4},{6,5},{7,6},{8,11},{9,8},{10,9... | collective-permute-start | bytes 6291464 | tf_op jit(solution)/shard_map/ppermute | solution.py:298
  117.1 2.0 copy-start.4
  120.5 47.1 %collective-permute-start.2 = (bf16[64,16384]{1,0:T(8,128)(2,1)}, bf16[64,16384]{1,0:T(8,128)(2,1)}, u32[]{:S(2)}, u32[]{:S(2)}) collective-permute-start(bf16[64,16384]{1,0:T(8,128)(2,1)} %slice.8), channel_id=1, source_target_pairs={{0,1},{1,2},{2,3},{3,0},{4,5},{5,6},{6,7},{7,4},{8,9},{9,10},{10,1... | collective-permute-start | bytes 6291464 | tf_op jit(solution)/shard_map/ppermute | solution.py:297
  161.0 6.6 %copy-start.5 = (bf16[64,16384]{1,0:T(8,128)(2,1)}, bf16[64,16384]{1,0:T(8,128)(2,1)S(1)}, u32[]{:S(2)}) copy-start(bf16[64,16384]{1,0:T(8,128)(2,1)S(1)} %collective-permute-done.3.bottom_ref) | copy-start | bytes 6291460
  178.5 0.6 copy-start

commit v8 on v6

--- a/solution.py
+++ b/solution.py
@@ -10,9 +10,9 @@
 STEPS = 64
 LANES = 128
 BLOCK = 2 * CAP
-PLACE_BLOCKS = (512, 1024, 1024, 1024, 1024, 1024, 1024, 1024, 512)
-MULTIPLY_BLOCKS = (512, 1024, 1024, 1024, 1024, 1024, 1024, 1024, 256, 256)
-KEPT = 2
+PLACE_STEPS = 8
+MULTIPLY_BLOCK = 1024
+HEAD = 1536
 
 
 def whole_in(space):
@@ -34,21 +34,27 @@
 
 def place_kernel(swap_ref, owner_ref, integrals_ref, out_ref, both_ref, placed_ref, pick_ref, sem):
     rows, (lines, width) = integrals_ref.shape[0], out_ref.shape
-    starts = [sum(PLACE_BLOCKS[:i]) for i in range(len(PLACE_BLOCKS))]
-    fetches = [
-        [
-            pltpu.make_async_copy(
-                integrals_ref.at[:, pl.ds(half * width + start, block)],
-                both_ref.at[pl.ds(half * rows, rows), pl.ds(start, block)],
-                sem.at[i, half],
-            )
-            for half in range(2)
-        ]
-        for i, (start, block) in enumerate(zip(starts, PLACE_BLOCKS))
-    ]
-    for pair in fetches:
-        for copy in pair:
-            copy.start()
+    block = width // PLACE_STEPS
+
+    def columns(i, half=0):
+        return pl.ds(pl.multiple_of(half * width + i * block, block), block)
+
+    def fetch(i, half):
+        return pltpu.make_async_copy(
+            integrals_ref.at[:, columns(i, half)],
+            both_ref.at[pl.ds(half * rows, rows), columns(i)],
+            sem.at[i, half],
+        )
+
+    def write(i):
+        return pltpu.make_async_copy(
+            placed_ref.at[:, columns(i)], out_ref.at[:, columns(i)], sem.at[i, 2]
+        )
+
+    @pl.loop(0, PLACE_STEPS)
+    def _(i):
+        fetch(i, 0).start()
+        fetch(i, 1).start()
 
     owner = owner_ref[...]
     line = owner * BLOCK + slots_of(owner)
@@ -57,19 +63,18 @@
     pick_ref[:, :rows] = jnp.where(number == line + swap, 1.0, 0.0).astype(jnp.bfloat16)
     pick_ref[:, rows:] = jnp.where(number == line + (CAP - swap), 1.0, 0.0).astype(jnp.bfloat16)
 
-    writes = []
-    for i, pair in enumerate(fetches):
-        for copy in pair:
-            copy.wait()
-        here = pl.ds(starts[i], PLACE_BLOCKS[i])
-        placed_ref[:, here] = jnp.dot(
-            pick_ref[...], both_ref[:, here], preferred_element_type=jnp.float32
+    @pl.loop(0, PLACE_STEPS)
+    def _(i):
+        fetch(i, 0).wait()
+        fetch(i, 1).wait()
+        placed_ref[:, columns(i)] = jnp.dot(
+            pick_ref[...], both_ref[:, columns(i)], preferred_element_type=jnp.float32
         ).astype(jnp.bfloat16)
-        write = pltpu.make_async_copy(placed_ref.at[:, here], out_ref.at[:, here], sem.at[i, 2])
-        write.start()
-        writes.append(write)
-    for write in writes:
-        write.wait()
+        write(i).start()
+
+    @pl.loop(0, PLACE_STEPS)
+    def _(i):
+        write(i).wait()
 
 
 def place(swap, owner, integrals, peers):
@@ -84,7 +89,7 @@
             pltpu.VMEM((2 * rows, width), jnp.bfloat16),
             pltpu.VMEM((lines, width), jnp.bfloat16),
             pltpu.VMEM((lines, 2 * rows), jnp.bfloat16),
-            pltpu.SemaphoreType.DMA((len(PLACE_BLOCKS), 3)),
+            pltpu.SemaphoreType.DMA((PLACE_STEPS, 3)),
         ],
         compiler_params=pltpu.CompilerParams(vmem_limit_bytes=24 * 1024 * 1024),
         cost_estimate=pl.CostEstimate(
@@ -137,7 +142,7 @@
 
 def collect(amp, owner, shards, count, peers):
     pairs, cols = shards[0].shape
-    kept = 2 * sum(MULTIPLY_BLOCKS[:KEPT])
+    kept = 2 * HEAD
     return pl.pallas_call(
         collect_kernel,
         in_specs=[whole_in(pltpu.SMEM), whole_in(pltpu.VMEM)] + [whole_in(pl.ANY)] * len(shards),
@@ -169,48 +174,61 @@
 ):
     lines, width = rows_ref.shape
     upper = lines // 2
-    fetches, start = [], 0
-    for i, block in enumerate(MULTIPLY_BLOCKS):
-        fetches.append(
-            [
+    steps = (width - HEAD) // MULTIPLY_BLOCK
+    tail = HEAD + steps * MULTIPLY_BLOCK
+
+    def fetches(i, start, block, halves=2):
+        at = [pl.ds(half * width + start, block) for half in range(2)]
+        copies = [pltpu.make_async_copy(rows_ref.at[:, at[0]], near_ref.at[:, at[0]], sem.at[i, 0])]
+        for half in range(halves):
+            copies.append(
                 pltpu.make_async_copy(
-                    source.at[:, pl.ds(first, block)], target.at[:, pl.ds(first, block)], sem.at[i, k]
+                    amps_ref.at[:, at[half]], held_ref.at[:, at[half]], sem.at[i, 1 + half]
                 )
-                for k, (source, target, first) in enumerate(
-                    (
-                        (rows_ref, near_ref, start),
-                        (amps_ref, held_ref, start),
-                        (amps_ref, held_ref, width + start),
-                    )[: 1 if i < KEPT else 3]
-                )
-            ]
-        )
-        start += block
-    for trio in fetches:
-        for copy in trio:
-            copy.start()
-
-    start = 0
-    for block, trio in zip(MULTIPLY_BLOCKS, fetches):
-        for copy in trio:
-            copy.wait()
+            )
+        return copies
+
+    def middle(i):
+        start = pl.multiple_of(HEAD + i * MULTIPLY_BLOCK, 512)
+        return fetches(1 + i, start, MULTIPLY_BLOCK), start
+
+    def work(start, block, table_ref, half_width):
         group = lax.broadcasted_iota(jnp.int32, (upper, block), 0) // CAP % 2
-        here = pl.ds(start, block)
-        first, second = near_ref[:upper, here], near_ref[upper:, here]
-        kept = start < kept_ref.shape[1] // 2
+        first, second = near_ref[:upper, pl.ds(start, block)], near_ref[upper:, pl.ds(start, block)]
         for half, total_ref in enumerate((low_ref, high_ref)):
-            skip = half * (kept_ref.shape[1] // 2 if kept else width)
-            product = lax.dot_general(
+            total_ref[...] += lax.dot_general(
                 jnp.where(group == half, first, second),
-                (kept_ref if kept else held_ref)[:, pl.ds(skip + start, block)],
+                table_ref[:, pl.ds(half * half_width + start, block)],
                 (((1,), (1,)), ((), ())),
                 preferred_element_type=jnp.float32,
             )
-            if start == 0:
-                total_ref[...] = product
-            else:
-                total_ref[...] += product
-        start += block
+
+    head = fetches(0, 0, HEAD, 0)[0]
+    head.start()
+
+    @pl.loop(0, steps)
+    def _(i):
+        for copy in middle(i)[0]:
+            copy.start()
+
+    rest = fetches(1 + steps, tail, width - tail)
+    for copy in rest:
+        copy.start()
+    low_ref[...] = jnp.zeros_like(low_ref)
+    high_ref[...] = jnp.zeros_like(high_ref)
+    head.wait()
+    work(0, HEAD, kept_ref, HEAD)
+
+    @pl.loop(0, steps)
+    def _(i):
+        copies, start = middle(i)
+        for copy in copies:
+            copy.wait()
+        work(start, MULTIPLY_BLOCK, held_ref, width)
+
+    for copy in rest:
+        copy.wait()
+    work(tail, width - tail, held_ref, width)
 
     group = lax.broadcasted_iota(jnp.int32, low_ref.shape, 0) // CAP % 2
     value = low_ref[...] + exchange(high_ref[...], group)
@@ -238,7 +256,7 @@
             pltpu.VMEM((pairs, 2 * width), jnp.bfloat16),
             pltpu.VMEM((lines // 2, pairs), jnp.float32),
             pltpu.VMEM((lines // 2, pairs), jnp.float32),
-            pltpu.SemaphoreType.DMA((len(MULTIPLY_BLOCKS), 3)),
+            pltpu.SemaphoreType.DMA((2 + (width - HEAD) // MULTIPLY_BLOCK, 3)),
         ],
         compiler_params=pltpu.CompilerParams(vmem_limit_bytes=40 * 1024 * 1024),
         cost_estimate=pl.CostEstimate(

time: 235 us -> 235 us (level)
  no operation moved by 1% of the time
where the time goes in v8:
time: 235 us
  waiting for transfers between devices  163 us (69%)
  Pallas kernels  27.5 us (12%)
  starting transfers between devices  19.3 us (8%)
  blocking collectives  18.9 us (8%)
  local copies, waits for them, and re-layouts  6.28 us (3%)
    ppermute x1, waiting for transfers between devices, body(): lax.ppermute(mine, 'amp', back)  89.7 us
    ppermute x1, waiting for transfers between devices, body(): bottom = lax.ppermute(right[middle:], 'amp', back)  40.5 us
    all_to_all x1, waiting for transfers between devices, body(): lax.all_to_all(placed.reshape(peers, BLOCK, width), 'kblk', split_axis=0,...  26.4 us
    all_to_all x1, blocking collectives, body(): lax.all_to_all(values, 'kblk', split_axis=0, concat_axis=0, tiled=True)  18.9 us
    all_to_all x1, starting transfers between devices, body(): lax.all_to_all(placed.reshape(peers, BLOCK, width), 'kblk', split_axis=0,...  13.4 us
    pallas_call x1, Pallas kernels, collect(): pl.pallas_call(collect_kernel, in_specs=[whole_in(pltpu.SMEM), whole_in(p...  10.9 us
    pallas_call x1, Pallas kernels, multiply(): pl.pallas_call(multiply_kernel, in_specs=[whole_in(pl.ANY), whole_in(pl.A...  8.62 us
    ppermute x1, waiting for transfers between devices, body(): top = lax.ppermute(left[:middle], 'amp', ahead)  6.56 us
  transfers between devices with their start and end apart: 5, of which 4 were waited for; matrix products, arithmetic and copies ran while one was open for 1% of the time, Pallas kernels for 5%

profile of v8, /device:TPU:1, one launch (start us, length us, event | category | flops | bytes accessed | tf_op | source)
XLA Modules:
  0.0 235.3 jit_solution(10572439479252575785)
XLA Ops:
  0.0 0.0 copy-start.1
  0.0 0.7 copy-done.1
  0.7 5.8 %place.1 = bf16[512,8192]{1,0:T(8,128)(2,1)} custom-call(s32[1]{0:T(128)} %bitcast.3.swap_ref, s32[1,128]{1,0:T(1,128)S(1)} %bitcast.6, bf16[128,16384]{1,0:T(8,128)(2,1)} %integrals_ref.1), custom_call_target="tpu_custom_call" | custom-call | flops 2147483648 | bytes 12582912 | tf_op jit(solution)/shard_map/place/pallas_call | solution.py:83
  6.5 13.4 %all-to-all-start = ((bf16[64,8,8192]{2,1,0:T(8,128)(2,1)}), bf16[64,8,8192]{2,1,0:T(8,128)(2,1)}, u32[]{:S(2)}, u32[]{:S(2)}) async-start(bf16[64,8,8192]{2,1,0:T(8,128)(2,1)} %bitcast.8), calls=%async_computation | async-start | bytes 16777216 | tf_op jit(solution)/shard_map/all_to_all | solution.py:323
  19.8 0.0 copy-start.2
  19.8 2.6 %collective-permute-start.1 = (bf16[128,16384]{1,0:T(8,128)(2,1)}, bf16[128,16384]{1,0:T(8,128)(2,1)S(1)}, u32[]{:S(2)}, u32[]{:S(2)}) collective-permute-start(bf16[128,16384]{1,0:T(8,128)(2,1)} %bitcast.9), channel_id=1, source_target_pairs={{0,3},{1,0},{2,1},{3,2},{4,7},{5,4},{6,5},{7,6},{8,11},{9,8},{10,9... | collective-permute-start | bytes 12582920 | tf_op jit(solution)/shard_map/ppermute | solution.py:313
  22.4 0.0 collective-permute-start
  22.4 89.7 %collective-permute-done.1.right_ref = bf16[128,16384]{1,0:T(8,128)(2,1)S(1)} collective-permute-done((bf16[128,16384]{1,0:T(8,128)(2,1)}, bf16[128,16384]{1,0:T(8,128)(2,1)S(1)}, u32[]{:S(2)}, u32[]{:S(2)}) %collective-permute-start.1) | collective-permute-done | bytes 4194336 | tf_op jit(solution)/shard_map/ppermute | solution.py:313
  112.1 0.0 copy-start.3
  112.1 1.6 slice.9
  113.7 3.4 %collective-permute-start.3 = (bf16[64,16384]{1,0:T(8,128)(2,1)}, bf16[64,16384]{1,0:T(8,128)(2,1)S(1)}, u32[]{:S(2)}, u32[]{:S(2)}) collective-permute-start(bf16[64,16384]{1,0:T(8,128)(2,1)} %slice.9), channel_id=1, source_target_pairs={{0,3},{1,0},{2,1},{3,2},{4,7},{5,4},{6,5},{7,6},{8,11},{9,8},{10,9... | collective-permute-start | bytes 6291464 | tf_op jit(solution)/shard_map/ppermute | solution.py:315
  117.1 0.0 collective-permute-done.left_ref
  117.1 0.0 copy-start.4
  117.1 2.0 copy-done.4
  119.0 1.5 slice.8
  120.5 0.0 copy-done.3
  120.5 0.0 collective-permute-start.2
  120.5 40.5 %collective-permute-done.3.bottom_ref = bf16[64,16384]{1,0:T(8,128)(2,1)S(1)} collective-permute-done((bf16[64,16384]{1,0:T(8,128)(2,1)}, bf16[64,16384]{1,0:T(8,128)(2,1)S(1)}, u32[]{:S(2)}, u32[]{:S(2)}) %collective-permute-start.3) | collective-permute-done | bytes 2097184 | tf_op jit(solution)/shard_map/ppermute | solution.py:315
  161.0 0.0 copy-start.5
  161.0 6.6 %collective-permute-done.2.top_ref = bf16[64,16384]{1,0:T(8,128)(2,1)} collective-permute-done((bf16[64,16384]{1,0:T(8,128)(2,1)}, bf16[64,16384]{1,0:T(8,128)(2,1)}, u32[]{:S(2)}, u32[]{:S(2)}) %collective-permute-start.2) | collective-permute-done | bytes 2097184 | tf_op jit(solution)/shard_map/ppermute | solution.py:314
  167.6 0.0 copy-done.5
  167.6 0.0 copy-done.2
  167.6 10.9 %collect.1 = (bf16[512,16384]{1,0:T(8,128)(2,1)}, bf16[512,3072]{1,0:T(8,128)(2,1)S(1)}, bf16[128,512]{1,0:T(8,128)(2,1)S(1)}) custom-call(s32[1]{0:T(128)} %bitcast.amp_ref, s32[1,128]{1,0:T(1,128)S(1)} %bitcast.7, bf16[128,16384]{1,0:T(8,128)(2,1)} %bitcast.11, bf16[128,16384]{1,0:T(8,128)(2,1)} %copy-done.4, bf16[128,16384]{1,0:T(8,128)(2,1)} %copy-done.3, ...), custom_call_target="tpu_custom_call" | custom-call | bytes 33554432 | tf_op jit(solution)/shard_map/collect/pallas_call | solution.py:146
  178.5 0.0 copy-start
  178.6 0.6 copy-done
  179.2 26.4 %all-to-all-done = bf16[64,8,8192]{2,1,0:T(8,128)(2,1)} async-done(((bf16[64,8,8192]{2,1,0:T(8,128)(2,1)}), bf16[64,8,8192]{2,1,0:T(8,128)(2,1)}, u32[]{:S(2)}, u32[]{:S(2)}) %all-to-all-start) | async-done | bytes 8388640 | tf_op jit(solution)/shard_map/all_to_all | solution.py:323
  205.6 8.6 %multiply.1 = s16[64,4,640]{2,1,0:T(4,128)(2,1)S(1)} custom-call(bf16[512,8192]{1,0:T(8,128)(2,1)} %bitcast.5.rows_ref, bf16[512,16384]{1,0:T(8,128)(2,1)} %get-tuple-element.9.amps_ref, bf16[512,3072]{1,0:T(8,128)(2,1)S(1)} %get-tuple-element.10.kept_ref), custom_call_target="tpu_custom_call" | custom-call | flops 4294967296 | bytes 25165824 | tf_op jit(solution)/shard_map/multiply/pallas_call | solution.py:249
  214.2 18.9 %all_to_all.10.lines_ref = s16[64,4,640]{2,1,0:T(4,128)(2,1)S(1)} all-to-all(s16[64,4,640]{2,1,0:T(4,128)(2,1)S(1)} %multiply.1), channel_id=1, replica_groups=mesh['kblk'=64,'amp'=4] {'kblk'}, dimensions={0} | all-to-all | bytes 655360 | tf_op jit(solution)/shard_map/all_to_all | solution.py:327
  233.2 2.1 pick.1
Async XLA Ops:
  0.0 0.7 copy-start.1
  6.5 199.1 %all-to-all-start = ((bf16[64,8,8192]{2,1,0:T(8,128)(2,1)}), bf16[64,8,8192]{2,1,0:T(8,128)(2,1)}, u32[]{:S(2)}, u32[]{:S(2)}) async-start(bf16[64,8,8192]{2,1,0:T(8,128)(2,1)} %bitcast.8), calls=%async_computation | async-start | bytes 16777216 | tf_op jit(solution)/shard_map/all_to_all | solution.py:323
  19.8 147.8 %copy-start.2 = (s32[128,1]{0,1:T(1,128)S(1)}, s32[128,1]{0,1:T(1,128)}, u32[]{:S(2)}) copy-start(s32[128,1]{0,1:T(1,128)} %param.4) | copy-start | bytes 1540
  19.8 92.3 %collective-permute-start.1 = (bf16[128,16384]{1,0:T(8,128)(2,1)}, bf16[128,16384]{1,0:T(8,128)(2,1)S(1)}, u32[]{:S(2)}, u32[]{:S(2)}) collective-permute-start(bf16[128,16384]{1,0:T(8,128)(2,1)} %bitcast.9), channel_id=1, source_target_pairs={{0,3},{1,0},{2,1},{3,2},{4,7},{5,4},{6,5},{7,6},{8,11},{9,8},{10,9... | collective-permute-start | bytes 12582920 | tf_op jit(solution)/shard_map/ppermute | solution.py:313
  22.4 94.7 %collective-permute-start = (bf16[128,16384]{1,0:T(8,128)(2,1)}, bf16[128,16384]{1,0:T(8,128)(2,1)S(1)}, u32[]{:S(2)}, u32[]{:S(2)}) collective-permute-start(bf16[128,16384]{1,0:T(8,128)(2,1)} %bitcast.10), channel_id=1, source_target_pairs={{0,1},{1,2},{2,3},{3,0},{4,5},{5,6},{6,7},{7,4},{8,9},{9,10},{10,1... | collective-permute-start | bytes 12582920 | tf_op jit(solution)/shard_map/ppermute | solution.py:313
  112.1 8.4 %copy-start.3 = (bf16[128,16384]{1,0:T(8,128)(2,1)}, bf16[128,16384]{1,0:T(8,128)(2,1)S(1)}, u32[]{:S(2)}) copy-start(bf16[128,16384]{1,0:T(8,128)(2,1)S(1)} %collective-permute-done.1.right_ref) | copy-start | bytes 12582916
  113.7 47.4 %collective-permute-start.3 = (bf16[64,16384]{1,0:T(8,128)(2,1)}, bf16[64,16384]{1,0:T(8,128)(2,1)S(1)}, u32[]{:S(2)}, u32[]{:S(2)}) collective-permute-start(bf16[64,16384]{1,0:T(8,128)(2,1)} %slice.9), channel_id=1, source_target_pairs={{0,3},{1,0},{2,1},{3,2},{4,7},{5,4},{6,5},{7,6},{8,11},{9,8},{10,9... | collective-permute-start | bytes 6291464 | tf_op jit(solution)/shard_map/ppermute | solution.py:315
  117.1 2.0 copy-start.4
  120.5 47.1 %collective-permute-start.2 = (bf16[64,16384]{1,0:T(8,128)(2,1)}, bf16[64,16384]{1,0:T(8,128)(2,1)}, u32[]{:S(2)}, u32[]{:S(2)}) collective-permute-start(bf16[64,16384]{1,0:T(8,128)(2,1)} %slice.8), channel_id=1, source_target_pairs={{0,1},{1,2},{2,3},{3,0},{4,5},{5,6},{6,7},{7,4},{8,9},{9,10},{10,1... | collective-permute-start | bytes 6291464 | tf_op jit(solution)/shard_map/ppermute | solution.py:314
  161.0 6.6 %copy-start.5 = (bf16[64,16384]{1,0:T(8,128)(2,1)}, bf16[64,16384]{1,0:T(8,128)(2,1)S(1)}, u32[]{:S(2)}) copy-start(bf16[64,16384]{1,0:T(8,128)(2,1)S(1)} %collective-permute-done.3.bottom_ref) | copy-start | bytes 6291460
  178.5 0.6 copy-start

commit v9 on v8

--- a/solution.py
+++ b/solution.py
@@ -11,6 +11,7 @@
 LANES = 128
 BLOCK = 2 * CAP
 PLACE_STEPS = 8
+PLACE_AHEAD = 3
 MULTIPLY_BLOCK = 1024
 HEAD = 1536
 
@@ -32,7 +33,9 @@
     return jnp.sum(earlier, axis=0, keepdims=True)
 
 
-def place_kernel(swap_ref, owner_ref, integrals_ref, out_ref, both_ref, placed_ref, pick_ref, sem):
+def place_kernel(
+    swap_ref, named_ref, integrals_ref, out_ref, owner_ref, both_ref, placed_ref, pick_ref, sem, named_sem
+):
     rows, (lines, width) = integrals_ref.shape[0], out_ref.shape
     block = width // PLACE_STEPS
 
@@ -51,11 +54,13 @@
             placed_ref.at[:, columns(i)], out_ref.at[:, columns(i)], sem.at[i, 2]
         )
 
-    @pl.loop(0, PLACE_STEPS)
-    def _(i):
+    names = pltpu.make_async_copy(named_ref, owner_ref, named_sem)
+    names.start()
+    for i in range(PLACE_AHEAD):
         fetch(i, 0).start()
         fetch(i, 1).start()
 
+    names.wait()
     owner = owner_ref[...]
     line = owner * BLOCK + slots_of(owner)
     number = lax.broadcasted_iota(jnp.int32, (lines, rows), 0)
@@ -65,6 +70,11 @@
 
     @pl.loop(0, PLACE_STEPS)
     def _(i):
+        @pl.when(i + PLACE_AHEAD < PLACE_STEPS)
+        def _():
+            fetch(i + PLACE_AHEAD, 0).start()
+            fetch(i + PLACE_AHEAD, 1).start()
+
         fetch(i, 0).wait()
         fetch(i, 1).wait()
         placed_ref[:, columns(i)] = jnp.dot(
@@ -82,14 +92,16 @@
     lines, width = peers * BLOCK, cols // 2
     return pl.pallas_call(
         place_kernel,
-        in_specs=[whole_in(pltpu.SMEM), whole_in(pltpu.VMEM), whole_in(pl.ANY)],
+        in_specs=[whole_in(pltpu.SMEM), whole_in(pl.ANY), whole_in(pl.ANY)],
         out_specs=whole_in(pl.ANY),
         out_shape=pltpu.HBM((lines, width), jnp.bfloat16),
         scratch_shapes=[
+            pltpu.VMEM((1, rows), jnp.int32),
             pltpu.VMEM((2 * rows, width), jnp.bfloat16),
             pltpu.VMEM((lines, width), jnp.bfloat16),
             pltpu.VMEM((lines, 2 * rows), jnp.bfloat16),
             pltpu.SemaphoreType.DMA((PLACE_STEPS, 3)),
+            pltpu.SemaphoreType.DMA,
         ],
         compiler_params=pltpu.CompilerParams(vmem_limit_bytes=24 * 1024 * 1024),
         cost_estimate=pl.CostEstimate(
@@ -98,7 +110,7 @@
             transcendentals=0,
         ),
         name="place",
-    )(swap, owner, pltpu.with_memory_space_constraint(integrals, pltpu.HBM))
+    )(swap, *[pltpu.with_memory_space_constraint(x, pltpu.HBM) for x in (owner, integrals)])
 
 
 def collect_kernel(

time: 235 us -> 236 us (level)
  no operation moved by 1% of the time
where the time goes in v9:
time: 236 us; the launch traced here: 235 us
  waiting for transfers between devices  163 us (69%)
  Pallas kernels  28.1 us (12%)
  starting transfers between devices  19.3 us (8%)
  blocking collectives  18.9 us (8%)
  local copies, waits for them, and re-layouts  5.64 us (2%)
    ppermute x1, waiting for transfers between devices, body(): lax.ppermute(mine, 'amp', back)  89.7 us
    ppermute x1, waiting for transfers between devices, body(): bottom = lax.ppermute(right[middle:], 'amp', back)  40.5 us
    all_to_all x1, waiting for transfers between devices, body(): lax.all_to_all(placed.reshape(peers, BLOCK, width), 'kblk', split_axis=0,...  26.4 us
    all_to_all x1, blocking collectives, body(): lax.all_to_all(values, 'kblk', split_axis=0, concat_axis=0, tiled=True)  18.9 us
    all_to_all x1, starting transfers between devices, body(): lax.all_to_all(placed.reshape(peers, BLOCK, width), 'kblk', split_axis=0,...  13.4 us
    pallas_call x1, Pallas kernels, collect(): pl.pallas_call(collect_kernel, in_specs=[whole_in(pltpu.SMEM), whole_in(p...  10.9 us
    pallas_call x1, Pallas kernels, multiply(): pl.pallas_call(multiply_kernel, in_specs=[whole_in(pl.ANY), whole_in(pl.A...  8.62 us
    ppermute x1, waiting for transfers between devices, body(): top = lax.ppermute(left[:middle], 'amp', ahead)  6.56 us
  transfers between devices with their start and end apart: 5, of which 4 were waited for; matrix products, arithmetic and copies ran while one was open for 1% of the time, Pallas kernels for 5%

profile of v9, /device:TPU:1, one launch (start us, length us, event | category | flops | bytes accessed | tf_op | source)
XLA Modules:
  0.0 235.3 jit_solution(4264351149328607776)
XLA Ops:
  0.0 6.5 %place.1 = bf16[512,8192]{1,0:T(8,128)(2,1)} custom-call(s32[1]{0:T(128)} %bitcast.3.swap_ref, s32[1,128]{1,0:T(1,128)} %bitcast.6, bf16[128,16384]{1,0:T(8,128)(2,1)} %integrals_ref.1), custom_call_target="tpu_custom_call" | custom-call | flops 2147483648 | bytes 12582912 | tf_op jit(solution)/shard_map/place/pallas_call | solution.py:93
  6.5 13.4 %all-to-all-start = ((bf16[64,8,8192]{2,1,0:T(8,128)(2,1)}), bf16[64,8,8192]{2,1,0:T(8,128)(2,1)}, u32[]{:S(2)}, u32[]{:S(2)}) async-start(bf16[64,8,8192]{2,1,0:T(8,128)(2,1)} %bitcast.8), calls=%async_computation | async-start | bytes 16777216 | tf_op jit(solution)/shard_map/all_to_all | solution.py:335
  19.8 0.0 copy-start.1
  19.9 2.6 %collective-permute-start.1 = (bf16[128,16384]{1,0:T(8,128)(2,1)}, bf16[128,16384]{1,0:T(8,128)(2,1)S(1)}, u32[]{:S(2)}, u32[]{:S(2)}) collective-permute-start(bf16[128,16384]{1,0:T(8,128)(2,1)} %bitcast.9), channel_id=1, source_target_pairs={{0,3},{1,0},{2,1},{3,2},{4,7},{5,4},{6,5},{7,6},{8,11},{9,8},{10,9... | collective-permute-start | bytes 12582920 | tf_op jit(solution)/shard_map/ppermute | solution.py:325
  22.4 0.0 collective-permute-start
  22.4 89.7 %collective-permute-done.1.right_ref = bf16[128,16384]{1,0:T(8,128)(2,1)S(1)} collective-permute-done((bf16[128,16384]{1,0:T(8,128)(2,1)}, bf16[128,16384]{1,0:T(8,128)(2,1)S(1)}, u32[]{:S(2)}, u32[]{:S(2)}) %collective-permute-start.1) | collective-permute-done | bytes 4194336 | tf_op jit(solution)/shard_map/ppermute | solution.py:325
  112.1 0.0 copy-start.2
  112.1 1.6 slice.9
  113.7 3.4 %collective-permute-start.3 = (bf16[64,16384]{1,0:T(8,128)(2,1)}, bf16[64,16384]{1,0:T(8,128)(2,1)S(1)}, u32[]{:S(2)}, u32[]{:S(2)}) collective-permute-start(bf16[64,16384]{1,0:T(8,128)(2,1)} %slice.9), channel_id=1, source_target_pairs={{0,3},{1,0},{2,1},{3,2},{4,7},{5,4},{6,5},{7,6},{8,11},{9,8},{10,9... | collective-permute-start | bytes 6291464 | tf_op jit(solution)/shard_map/ppermute | solution.py:327
  117.1 0.0 collective-permute-done.left_ref
  117.1 0.0 copy-start.3
  117.1 2.0 copy-done.3
  119.1 1.5 slice.8
  120.5 0.0 copy-done.2
  120.5 0.0 collective-permute-start.2
  120.5 40.5 %collective-permute-done.3.bottom_ref = bf16[64,16384]{1,0:T(8,128)(2,1)S(1)} collective-permute-done((bf16[64,16384]{1,0:T(8,128)(2,1)}, bf16[64,16384]{1,0:T(8,128)(2,1)S(1)}, u32[]{:S(2)}, u32[]{:S(2)}) %collective-permute-start.3) | collective-permute-done | bytes 2097184 | tf_op jit(solution)/shard_map/ppermute | solution.py:327
  161.1 0.0 copy-start.4
  161.1 6.6 %collective-permute-done.2.top_ref = bf16[64,16384]{1,0:T(8,128)(2,1)} collective-permute-done((bf16[64,16384]{1,0:T(8,128)(2,1)}, bf16[64,16384]{1,0:T(8,128)(2,1)}, u32[]{:S(2)}, u32[]{:S(2)}) %collective-permute-start.2) | collective-permute-done | bytes 2097184 | tf_op jit(solution)/shard_map/ppermute | solution.py:326
  167.6 0.0 copy-done.4
  167.6 0.0 copy-done.1
  167.6 10.9 %collect.1 = (bf16[512,16384]{1,0:T(8,128)(2,1)}, bf16[512,3072]{1,0:T(8,128)(2,1)S(1)}, bf16[128,512]{1,0:T(8,128)(2,1)S(1)}) custom-call(s32[1]{0:T(128)} %bitcast.amp_ref, s32[1,128]{1,0:T(1,128)S(1)} %bitcast.7, bf16[128,16384]{1,0:T(8,128)(2,1)} %bitcast.11, bf16[128,16384]{1,0:T(8,128)(2,1)} %copy-done.3, bf16[128,16384]{1,0:T(8,128)(2,1)} %copy-done.2, ...), custom_call_target="tpu_custom_call" | custom-call | bytes 33554432 | tf_op jit(solution)/shard_map/collect/pallas_call | solution.py:158
  178.6 0.0 copy-start
  178.6 0.6 copy-done
  179.2 26.4 %all-to-all-done = bf16[64,8,8192]{2,1,0:T(8,128)(2,1)} async-done(((bf16[64,8,8192]{2,1,0:T(8,128)(2,1)}), bf16[64,8,8192]{2,1,0:T(8,128)(2,1)}, u32[]{:S(2)}, u32[]{:S(2)}) %all-to-all-start) | async-done | bytes 8388640 | tf_op jit(solution)/shard_map/all_to_all | solution.py:335
  205.6 8.6 %multiply.1 = s16[64,4,640]{2,1,0:T(4,128)(2,1)S(1)} custom-call(bf16[512,8192]{1,0:T(8,128)(2,1)} %bitcast.5.rows_ref, bf16[512,16384]{1,0:T(8,128)(2,1)} %get-tuple-element.9.amps_ref, bf16[512,3072]{1,0:T(8,128)(2,1)S(1)} %get-tuple-element.10.kept_ref), custom_call_target="tpu_custom_call" | custom-call | flops 4294967296 | bytes 25165824 | tf_op jit(solution)/shard_map/multiply/pallas_call | solution.py:261
  214.2 18.9 %all_to_all.10.lines_ref = s16[64,4,640]{2,1,0:T(4,128)(2,1)S(1)} all-to-all(s16[64,4,640]{2,1,0:T(4,128)(2,1)S(1)} %multiply.1), channel_id=1, replica_groups=mesh['kblk'=64,'amp'=4] {'kblk'}, dimensions={0} | all-to-all | bytes 655360 | tf_op jit(solution)/shard_map/all_to_all | solution.py:339
  233.2 2.1 pick.1
Async XLA Ops:
  6.5 199.1 %all-to-all-start = ((bf16[64,8,8192]{2,1,0:T(8,128)(2,1)}), bf16[64,8,8192]{2,1,0:T(8,128)(2,1)}, u32[]{:S(2)}, u32[]{:S(2)}) async-start(bf16[64,8,8192]{2,1,0:T(8,128)(2,1)} %bitcast.8), calls=%async_computation | async-start | bytes 16777216 | tf_op jit(solution)/shard_map/all_to_all | solution.py:335
  19.8 147.8 %copy-start.1 = (s32[128,1]{0,1:T(1,128)S(1)}, s32[128,1]{0,1:T(1,128)}, u32[]{:S(2)}) copy-start(s32[128,1]{0,1:T(1,128)} %param.4) | copy-start | bytes 1540
  19.9 92.3 %collective-permute-start.1 = (bf16[128,16384]{1,0:T(8,128)(2,1)}, bf16[128,16384]{1,0:T(8,128)(2,1)S(1)}, u32[]{:S(2)}, u32[]{:S(2)}) collective-permute-start(bf16[128,16384]{1,0:T(8,128)(2,1)} %bitcast.9), channel_id=1, source_target_pairs={{0,3},{1,0},{2,1},{3,2},{4,7},{5,4},{6,5},{7,6},{8,11},{9,8},{10,9... | collective-permute-start | bytes 12582920 | tf_op jit(solution)/shard_map/ppermute | solution.py:325
  22.4 94.7 %collective-permute-start = (bf16[128,16384]{1,0:T(8,128)(2,1)}, bf16[128,16384]{1,0:T(8,128)(2,1)S(1)}, u32[]{:S(2)}, u32[]{:S(2)}) collective-permute-start(bf16[128,16384]{1,0:T(8,128)(2,1)} %bitcast.10), channel_id=1, source_target_pairs={{0,1},{1,2},{2,3},{3,0},{4,5},{5,6},{6,7},{7,4},{8,9},{9,10},{10,1... | collective-permute-start | bytes 12582920 | tf_op jit(solution)/shard_map/ppermute | solution.py:325
  112.1 8.4 %copy-start.2 = (bf16[128,16384]{1,0:T(8,128)(2,1)}, bf16[128,16384]{1,0:T(8,128)(2,1)S(1)}, u32[]{:S(2)}) copy-start(bf16[128,16384]{1,0:T(8,128)(2,1)S(1)} %collective-permute-done.1.right_ref) | copy-start | bytes 12582916
  113.7 47.4 %collective-permute-start.3 = (bf16[64,16384]{1,0:T(8,128)(2,1)}, bf16[64,16384]{1,0:T(8,128)(2,1)S(1)}, u32[]{:S(2)}, u32[]{:S(2)}) collective-permute-start(bf16[64,16384]{1,0:T(8,128)(2,1)} %slice.9), channel_id=1, source_target_pairs={{0,3},{1,0},{2,1},{3,2},{4,7},{5,4},{6,5},{7,6},{8,11},{9,8},{10,9... | collective-permute-start | bytes 6291464 | tf_op jit(solution)/shard_map/ppermute | solution.py:327
  117.1 2.0 copy-start.3
  120.5 47.1 %collective-permute-start.2 = (bf16[64,16384]{1,0:T(8,128)(2,1)}, bf16[64,16384]{1,0:T(8,128)(2,1)}, u32[]{:S(2)}, u32[]{:S(2)}) collective-permute-start(bf16[64,16384]{1,0:T(8,128)(2,1)} %slice.8), channel_id=1, source_target_pairs={{0,1},{1,2},{2,3},{3,0},{4,5},{5,6},{6,7},{7,4},{8,9},{9,10},{10,1... | collective-permute-start | bytes 6291464 | tf_op jit(solution)/shard_map/ppermute | solution.py:326
  161.1 6.6 %copy-start.4 = (bf16[64,16384]{1,0:T(8,128)(2,1)}, bf16[64,16384]{1,0:T(8,128)(2,1)S(1)}, u32[]{:S(2)}) copy-start(bf16[64,16384]{1,0:T(8,128)(2,1)S(1)} %collective-permute-done.3.bottom_ref) | copy-start | bytes 6291460
  178.6 0.7 copy-start

commit v10 on v8

--- a/solution.py
+++ b/solution.py
@@ -250,7 +250,7 @@
         multiply_kernel,
         in_specs=[whole_in(pl.ANY), whole_in(pl.ANY), whole_in(pltpu.VMEM)],
         out_specs=whole_in(pltpu.VMEM),
-        out_shape=jax.ShapeDtypeStruct((lines // BLOCK, CAP, pairs + LANES), jnp.int16),
+        out_shape=pltpu.VMEM((lines // BLOCK, CAP, pairs + LANES), jnp.int16),
         scratch_shapes=[
             pltpu.VMEM((lines, width), jnp.bfloat16),
             pltpu.VMEM((pairs, 2 * width), jnp.bfloat16),
@@ -272,34 +272,58 @@
     )
 
 
-def pick_kernel(pick_ref, lines_ref, out_ref):
+def pick_kernel(matrix_ref, lines_ref, out_ref, pick_ref, parts_ref, held_ref, sem):
     lines, pairs = pick_ref.shape[1] // 2, out_ref.shape[1]
+    fetch = pltpu.make_async_copy(matrix_ref, pick_ref, sem.at[0])
+    fetch.start()
     whole = lines_ref[...].astype(jnp.int32).reshape(lines, lines_ref.shape[2])
     upper = whole >> 8
-    parts = jnp.concatenate([upper, whole - (upper << 8)], axis=0)
-    picked = jnp.dot(
-        pick_ref[...],
-        parts.astype(jnp.float32).astype(jnp.bfloat16),
-        preferred_element_type=jnp.float32,
-    )
-    unit = jnp.exp2(picked[:, pairs : pairs + 1] / STEPS) / LARGEST
-    out_ref[...] = picked[:, :pairs] * unit
+    parts_ref[:lines, :] = upper.astype(jnp.float32).astype(jnp.bfloat16)
+    parts_ref[lines:, :] = (whole - (upper << 8)).astype(jnp.float32).astype(jnp.bfloat16)
+    fetch.wait()
+
+    def picked(first, count):
+        return jnp.dot(
+            pick_ref[...],
+            parts_ref[:, first : first + count],
+            preferred_element_type=jnp.float32,
+        )
+
+    unit = jnp.exp2(picked(pairs, LANES)[:, :1] / STEPS) / LARGEST
+    writes = []
+    for i in range(2):
+        first, count = i * (pairs // 2), pairs // 2
+        held_ref[:, first : first + count] = picked(first, count) * unit
+        here = pl.ds(first, count)
+        writes.append(pltpu.make_async_copy(held_ref.at[:, here], out_ref.at[:, here], sem.at[1 + i]))
+        writes[-1].start()
+    for write in writes:
+        write.wait()
 
 
 def pick(matrix, lines):
     rows, pairs = matrix.shape[0], lines.shape[2] - LANES
     return pl.pallas_call(
         pick_kernel,
-        in_specs=[whole_in(pltpu.VMEM)] * 2,
-        out_specs=whole_in(pltpu.VMEM),
+        in_specs=[whole_in(pl.ANY), whole_in(pltpu.VMEM)],
+        out_specs=whole_in(pl.ANY),
         out_shape=jax.ShapeDtypeStruct((rows, pairs), jnp.float32),
+        scratch_shapes=[
+            pltpu.VMEM(matrix.shape, jnp.bfloat16),
+            pltpu.VMEM((matrix.shape[1], lines.shape[2]), jnp.bfloat16),
+            pltpu.VMEM((rows, pairs), jnp.float32),
+            pltpu.SemaphoreType.DMA((3,)),
+        ],
         cost_estimate=pl.CostEstimate(
             flops=4 * rows * lines.size,
             bytes_accessed=2 * lines.size + 4 * rows * pairs,
             transcendentals=rows,
         ),
         name="pick",
-    )(matrix, pltpu.with_memory_space_constraint(lines, pltpu.VMEM))
+    )(
+        pltpu.with_memory_space_constraint(matrix, pltpu.HBM),
+        pltpu.with_memory_space_constraint(lines, pltpu.VMEM),
+    )
 
 
 def body(integrals, row_owner, lambda_amps):

time: 235 us -> 235 us (level)
  no operation moved by 1% of the time
where the time goes in v10:
time: 235 us
  waiting for transfers between devices  163 us (69%)
  Pallas kernels  27.2 us (12%)
  starting transfers between devices  19.3 us (8%)
  blocking collectives  18.9 us (8%)
  local copies, waits for them, and re-layouts  6.28 us (3%)
    ppermute x1, waiting for transfers between devices, body(): lax.ppermute(mine, 'amp', back)  89.7 us
    ppermute x1, waiting for transfers between devices, body(): bottom = lax.ppermute(right[middle:], 'amp', back)  40.5 us
    all_to_all x1, waiting for transfers between devices, body(): lax.all_to_all(placed.reshape(peers, BLOCK, width), 'kblk', split_axis=0,...  26.4 us
    all_to_all x1, blocking collectives, body(): lax.all_to_all(values, 'kblk', split_axis=0, concat_axis=0, tiled=True)  18.9 us
    all_to_all x1, starting transfers between devices, body(): lax.all_to_all(placed.reshape(peers, BLOCK, width), 'kblk', split_axis=0,...  13.4 us
    pallas_call x1, Pallas kernels, collect(): pl.pallas_call(collect_kernel, in_specs=[whole_in(pltpu.SMEM), whole_in(p...  10.9 us
    pallas_call x1, Pallas kernels, multiply(): pl.pallas_call(multiply_kernel, in_specs=[whole_in(pl.ANY), whole_in(pl.A...  8.62 us
    ppermute x1, waiting for transfers between devices, body(): top = lax.ppermute(left[:middle], 'amp', ahead)  6.56 us
  transfers between devices with their start and end apart: 5, of which 4 were waited for; matrix products, arithmetic and copies ran while one was open for 1% of the time, Pallas kernels for 5%

profile of v10, /device:TPU:1, one launch (start us, length us, event | category | flops | bytes accessed | tf_op | source)
XLA Modules:
  0.0 235.1 jit_solution(10653517746527043212)
XLA Ops:
  0.0 0.0 copy-start.1
  0.0 0.7 copy-done.1
  0.7 5.8 %place.1 = bf16[512,8192]{1,0:T(8,128)(2,1)} custom-call(s32[1]{0:T(128)} %bitcast.3.swap_ref, s32[1,128]{1,0:T(1,128)S(1)} %bitcast.6, bf16[128,16384]{1,0:T(8,128)(2,1)} %integrals_ref.1), custom_call_target="tpu_custom_call" | custom-call | flops 2147483648 | bytes 12582912 | tf_op jit(solution)/shard_map/place/pallas_call | solution.py:83
  6.5 13.4 %all-to-all-start = ((bf16[64,8,8192]{2,1,0:T(8,128)(2,1)}), bf16[64,8,8192]{2,1,0:T(8,128)(2,1)}, u32[]{:S(2)}, u32[]{:S(2)}) async-start(bf16[64,8,8192]{2,1,0:T(8,128)(2,1)} %bitcast.8), calls=%async_computation | async-start | bytes 16777216 | tf_op jit(solution)/shard_map/all_to_all | solution.py:347
  19.8 0.0 copy-start.2
  19.8 2.6 %collective-permute-start.1 = (bf16[128,16384]{1,0:T(8,128)(2,1)}, bf16[128,16384]{1,0:T(8,128)(2,1)S(1)}, u32[]{:S(2)}, u32[]{:S(2)}) collective-permute-start(bf16[128,16384]{1,0:T(8,128)(2,1)} %bitcast.9), channel_id=1, source_target_pairs={{0,3},{1,0},{2,1},{3,2},{4,7},{5,4},{6,5},{7,6},{8,11},{9,8},{10,9... | collective-permute-start | bytes 12582920 | tf_op jit(solution)/shard_map/ppermute | solution.py:337
  22.4 0.0 collective-permute-start
  22.4 89.7 %collective-permute-done.1.right_ref = bf16[128,16384]{1,0:T(8,128)(2,1)S(1)} collective-permute-done((bf16[128,16384]{1,0:T(8,128)(2,1)}, bf16[128,16384]{1,0:T(8,128)(2,1)S(1)}, u32[]{:S(2)}, u32[]{:S(2)}) %collective-permute-start.1) | collective-permute-done | bytes 4194336 | tf_op jit(solution)/shard_map/ppermute | solution.py:337
  112.1 0.0 copy-start.3
  112.1 1.6 slice.9
  113.7 3.4 %collective-permute-start.3 = (bf16[64,16384]{1,0:T(8,128)(2,1)}, bf16[64,16384]{1,0:T(8,128)(2,1)S(1)}, u32[]{:S(2)}, u32[]{:S(2)}) collective-permute-start(bf16[64,16384]{1,0:T(8,128)(2,1)} %slice.9), channel_id=1, source_target_pairs={{0,3},{1,0},{2,1},{3,2},{4,7},{5,4},{6,5},{7,6},{8,11},{9,8},{10,9... | collective-permute-start | bytes 6291464 | tf_op jit(solution)/shard_map/ppermute | solution.py:339
  117.1 0.0 collective-permute-done.left_ref
  117.1 0.0 copy-start.4
  117.1 2.0 copy-done.4
  119.0 1.5 slice.8
  120.5 0.0 copy-done.3
  120.5 0.0 collective-permute-start.2
  120.5 40.5 %collective-permute-done.3.bottom_ref = bf16[64,16384]{1,0:T(8,128)(2,1)S(1)} collective-permute-done((bf16[64,16384]{1,0:T(8,128)(2,1)}, bf16[64,16384]{1,0:T(8,128)(2,1)S(1)}, u32[]{:S(2)}, u32[]{:S(2)}) %collective-permute-start.3) | collective-permute-done | bytes 2097184 | tf_op jit(solution)/shard_map/ppermute | solution.py:339
  161.0 0.0 copy-start.5
  161.0 6.6 %collective-permute-done.2.top_ref = bf16[64,16384]{1,0:T(8,128)(2,1)} collective-permute-done((bf16[64,16384]{1,0:T(8,128)(2,1)}, bf16[64,16384]{1,0:T(8,128)(2,1)}, u32[]{:S(2)}, u32[]{:S(2)}) %collective-permute-start.2) | collective-permute-done | bytes 2097184 | tf_op jit(solution)/shard_map/ppermute | solution.py:338
  167.6 0.0 copy-done.5
  167.6 0.0 copy-done.2
  167.6 10.9 %collect.1 = (bf16[512,16384]{1,0:T(8,128)(2,1)}, bf16[512,3072]{1,0:T(8,128)(2,1)S(1)}, bf16[128,512]{1,0:T(8,128)(2,1)S(1)}) custom-call(s32[1]{0:T(128)} %bitcast.amp_ref, s32[1,128]{1,0:T(1,128)S(1)} %bitcast.7, bf16[128,16384]{1,0:T(8,128)(2,1)} %bitcast.11, bf16[128,16384]{1,0:T(8,128)(2,1)} %copy-done.4, bf16[128,16384]{1,0:T(8,128)(2,1)} %copy-done.3, ...), custom_call_target="tpu_custom_call" | custom-call | bytes 33554432 | tf_op jit(solution)/shard_map/collect/pallas_call | solution.py:146
  178.5 0.0 copy-start
  178.6 0.6 copy-done
  179.2 26.4 %all-to-all-done = bf16[64,8,8192]{2,1,0:T(8,128)(2,1)} async-done(((bf16[64,8,8192]{2,1,0:T(8,128)(2,1)}), bf16[64,8,8192]{2,1,0:T(8,128)(2,1)}, u32[]{:S(2)}, u32[]{:S(2)}) %all-to-all-start) | async-done | bytes 8388640 | tf_op jit(solution)/shard_map/all_to_all | solution.py:347
  205.6 8.6 %multiply.1 = s16[64,4,640]{2,1,0:T(4,128)(2,1)S(1)} custom-call(bf16[512,8192]{1,0:T(8,128)(2,1)} %bitcast.5.rows_ref, bf16[512,16384]{1,0:T(8,128)(2,1)} %get-tuple-element.9.amps_ref, bf16[512,3072]{1,0:T(8,128)(2,1)S(1)} %get-tuple-element.10.kept_ref), custom_call_target="tpu_custom_call" | custom-call | flops 4294967296 | bytes 25165824 | tf_op jit(solution)/shard_map/multiply/pallas_call | solution.py:249
  214.2 18.9 %all_to_all.10.lines_ref = s16[64,4,640]{2,1,0:T(4,128)(2,1)S(1)} all-to-all(s16[64,4,640]{2,1,0:T(4,128)(2,1)S(1)} %multiply.1), channel_id=1, replica_groups=mesh['kblk'=64,'amp'=4] {'kblk'}, dimensions={0} | all-to-all | bytes 655360 | tf_op jit(solution)/shard_map/all_to_all | solution.py:351
  233.2 1.9 pick.1
Async XLA Ops:
  0.0 0.7 copy-start.1
  6.5 199.1 %all-to-all-start = ((bf16[64,8,8192]{2,1,0:T(8,128)(2,1)}), bf16[64,8,8192]{2,1,0:T(8,128)(2,1)}, u32[]{:S(2)}, u32[]{:S(2)}) async-start(bf16[64,8,8192]{2,1,0:T(8,128)(2,1)} %bitcast.8), calls=%async_computation | async-start | bytes 16777216 | tf_op jit(solution)/shard_map/all_to_all | solution.py:347
  19.8 147.8 %copy-start.2 = (s32[128,1]{0,1:T(1,128)S(1)}, s32[128,1]{0,1:T(1,128)}, u32[]{:S(2)}) copy-start(s32[128,1]{0,1:T(1,128)} %param.4) | copy-start | bytes 1540
  19.8 92.3 %collective-permute-start.1 = (bf16[128,16384]{1,0:T(8,128)(2,1)}, bf16[128,16384]{1,0:T(8,128)(2,1)S(1)}, u32[]{:S(2)}, u32[]{:S(2)}) collective-permute-start(bf16[128,16384]{1,0:T(8,128)(2,1)} %bitcast.9), channel_id=1, source_target_pairs={{0,3},{1,0},{2,1},{3,2},{4,7},{5,4},{6,5},{7,6},{8,11},{9,8},{10,9... | collective-permute-start | bytes 12582920 | tf_op jit(solution)/shard_map/ppermute | solution.py:337
  22.4 94.7 %collective-permute-start = (bf16[128,16384]{1,0:T(8,128)(2,1)}, bf16[128,16384]{1,0:T(8,128)(2,1)S(1)}, u32[]{:S(2)}, u32[]{:S(2)}) collective-permute-start(bf16[128,16384]{1,0:T(8,128)(2,1)} %bitcast.10), channel_id=1, source_target_pairs={{0,1},{1,2},{2,3},{3,0},{4,5},{5,6},{6,7},{7,4},{8,9},{9,10},{10,1... | collective-permute-start | bytes 12582920 | tf_op jit(solution)/shard_map/ppermute | solution.py:337
  112.1 8.4 %copy-start.3 = (bf16[128,16384]{1,0:T(8,128)(2,1)}, bf16[128,16384]{1,0:T(8,128)(2,1)S(1)}, u32[]{:S(2)}) copy-start(bf16[128,16384]{1,0:T(8,128)(2,1)S(1)} %collective-permute-done.1.right_ref) | copy-start | bytes 12582916
  113.7 47.4 %collective-permute-start.3 = (bf16[64,16384]{1,0:T(8,128)(2,1)}, bf16[64,16384]{1,0:T(8,128)(2,1)S(1)}, u32[]{:S(2)}, u32[]{:S(2)}) collective-permute-start(bf16[64,16384]{1,0:T(8,128)(2,1)} %slice.9), channel_id=1, source_target_pairs={{0,3},{1,0},{2,1},{3,2},{4,7},{5,4},{6,5},{7,6},{8,11},{9,8},{10,9... | collective-permute-start | bytes 6291464 | tf_op jit(solution)/shard_map/ppermute | solution.py:339
  117.1 2.0 copy-start.4
  120.5 47.1 %collective-permute-start.2 = (bf16[64,16384]{1,0:T(8,128)(2,1)}, bf16[64,16384]{1,0:T(8,128)(2,1)}, u32[]{:S(2)}, u32[]{:S(2)}) collective-permute-start(bf16[64,16384]{1,0:T(8,128)(2,1)} %slice.8), channel_id=1, source_target_pairs={{0,1},{1,2},{2,3},{3,0},{4,5},{5,6},{6,7},{7,4},{8,9},{9,10},{10,1... | collective-permute-start | bytes 6291464 | tf_op jit(solution)/shard_map/ppermute | solution.py:338
  161.0 6.6 %copy-start.5 = (bf16[64,16384]{1,0:T(8,128)(2,1)}, bf16[64,16384]{1,0:T(8,128)(2,1)S(1)}, u32[]{:S(2)}) copy-start(bf16[64,16384]{1,0:T(8,128)(2,1)S(1)} %collective-permute-done.3.bottom_ref) | copy-start | bytes 6291460
  178.5 0.6 copy-start

commit v11 on v10

--- a/solution.py
+++ b/solution.py
@@ -10,7 +10,7 @@
 STEPS = 64
 LANES = 128
 BLOCK = 2 * CAP
-PLACE_STEPS = 8
+PLACE_BLOCKS = (1024, 2048, 2048, 2048, 1024)
 MULTIPLY_BLOCK = 1024
 HEAD = 1536
 
@@ -34,27 +34,20 @@
 
 def place_kernel(swap_ref, owner_ref, integrals_ref, out_ref, both_ref, placed_ref, pick_ref, sem):
     rows, (lines, width) = integrals_ref.shape[0], out_ref.shape
-    block = width // PLACE_STEPS
-
-    def columns(i, half=0):
-        return pl.ds(pl.multiple_of(half * width + i * block, block), block)
+    starts = [sum(PLACE_BLOCKS[:i]) for i in range(len(PLACE_BLOCKS))]
 
     def fetch(i, half):
+        start, block = starts[i], PLACE_BLOCKS[i]
         return pltpu.make_async_copy(
-            integrals_ref.at[:, columns(i, half)],
-            both_ref.at[pl.ds(half * rows, rows), columns(i)],
+            integrals_ref.at[:, pl.ds(half * width + start, block)],
+            both_ref.at[pl.ds(half * rows, rows), pl.ds(start, block)],
             sem.at[i, half],
         )
 
-    def write(i):
-        return pltpu.make_async_copy(
-            placed_ref.at[:, columns(i)], out_ref.at[:, columns(i)], sem.at[i, 2]
-        )
-
-    @pl.loop(0, PLACE_STEPS)
-    def _(i):
-        fetch(i, 0).start()
-        fetch(i, 1).start()
+    fetches = [[fetch(i, half) for half in range(2)] for i in range(len(PLACE_BLOCKS))]
+    for pair in fetches:
+        for copy in pair:
+            copy.start()
 
     owner = owner_ref[...]
     line = owner * BLOCK + slots_of(owner)
@@ -63,18 +56,18 @@
     pick_ref[:, :rows] = jnp.where(number == line + swap, 1.0, 0.0).astype(jnp.bfloat16)
     pick_ref[:, rows:] = jnp.where(number == line + (CAP - swap), 1.0, 0.0).astype(jnp.bfloat16)
 
-    @pl.loop(0, PLACE_STEPS)
-    def _(i):
-        fetch(i, 0).wait()
-        fetch(i, 1).wait()
-        placed_ref[:, columns(i)] = jnp.dot(
-            pick_ref[...], both_ref[:, columns(i)], preferred_element_type=jnp.float32
+    writes = []
+    for i, pair in enumerate(fetches):
+        for copy in pair:
+            copy.wait()
+        here = pl.ds(starts[i], PLACE_BLOCKS[i])
+        placed_ref[:, here] = jnp.dot(
+            pick_ref[...], both_ref[:, here], preferred_element_type=jnp.float32
         ).astype(jnp.bfloat16)
-        write(i).start()
-
-    @pl.loop(0, PLACE_STEPS)
-    def _(i):
-        write(i).wait()
+        writes.append(pltpu.make_async_copy(placed_ref.at[:, here], out_ref.at[:, here], sem.at[i, 2]))
+        writes[-1].start()
+    for write in writes:
+        write.wait()
 
 
 def place(swap, owner, integrals, peers):
@@ -89,7 +82,7 @@
             pltpu.VMEM((2 * rows, width), jnp.bfloat16),
             pltpu.VMEM((lines, width), jnp.bfloat16),
             pltpu.VMEM((lines, 2 * rows), jnp.bfloat16),
-            pltpu.SemaphoreType.DMA((PLACE_STEPS, 3)),
+            pltpu.SemaphoreType.DMA((len(PLACE_BLOCKS), 3)),
         ],
         compiler_params=pltpu.CompilerParams(vmem_limit_bytes=24 * 1024 * 1024),
         cost_estimate=pl.CostEstimate(

time: 235 us -> 235 us (level)
  no operation moved by 1% of the time
where the time goes in v11:
time: 235 us
  waiting for transfers between devices  163 us (69%)
  Pallas kernels  26.8 us (11%)
  starting transfers between devices  19.3 us (8%)
  blocking collectives  18.9 us (8%)
  local copies, waits for them, and re-layouts  6.28 us (3%)
    ppermute x1, waiting for transfers between devices, body(): lax.ppermute(mine, 'amp', back)  89.7 us
    ppermute x1, waiting for transfers between devices, body(): bottom = lax.ppermute(right[middle:], 'amp', back)  40.5 us
    all_to_all x1, waiting for transfers between devices, body(): lax.all_to_all(placed.reshape(peers, BLOCK, width), 'kblk', split_axis=0,...  26.4 us
    all_to_all x1, blocking collectives, body(): lax.all_to_all(values, 'kblk', split_axis=0, concat_axis=0, tiled=True)  18.9 us
    all_to_all x1, starting transfers between devices, body(): lax.all_to_all(placed.reshape(peers, BLOCK, width), 'kblk', split_axis=0,...  13.4 us
    pallas_call x1, Pallas kernels, collect(): pl.pallas_call(collect_kernel, in_specs=[whole_in(pltpu.SMEM), whole_in(p...  10.9 us
    pallas_call x1, Pallas kernels, multiply(): pl.pallas_call(multiply_kernel, in_specs=[whole_in(pl.ANY), whole_in(pl.A...  8.63 us
    ppermute x1, waiting for transfers between devices, body(): top = lax.ppermute(left[:middle], 'amp', ahead)  6.56 us
  transfers between devices with their start and end apart: 5, of which 4 were waited for; matrix products, arithmetic and copies ran while one was open for 1% of the time, Pallas kernels for 5%

profile of v11, /device:TPU:1, one launch (start us, length us, event | category | flops | bytes accessed | tf_op | source)
XLA Modules:
  0.0 234.7 jit_solution(18442036362696671235)
XLA Ops:
  0.0 0.0 copy-start.1
  0.0 0.7 copy-done.1
  0.7 5.4 %place.1 = bf16[512,8192]{1,0:T(8,128)(2,1)} custom-call(s32[1]{0:T(128)} %bitcast.3.swap_ref, s32[1,128]{1,0:T(1,128)S(1)} %bitcast.6, bf16[128,16384]{1,0:T(8,128)(2,1)} %integrals_ref.1), custom_call_target="tpu_custom_call" | custom-call | flops 2147483648 | bytes 12582912 | tf_op jit(solution)/shard_map/place/pallas_call | solution.py:76
  6.0 13.4 %all-to-all-start = ((bf16[64,8,8192]{2,1,0:T(8,128)(2,1)}), bf16[64,8,8192]{2,1,0:T(8,128)(2,1)}, u32[]{:S(2)}, u32[]{:S(2)}) async-start(bf16[64,8,8192]{2,1,0:T(8,128)(2,1)} %bitcast.8), calls=%async_computation | async-start | bytes 16777216 | tf_op jit(solution)/shard_map/all_to_all | solution.py:340
  19.4 0.0 copy-start.2
  19.4 2.6 %collective-permute-start.1 = (bf16[128,16384]{1,0:T(8,128)(2,1)}, bf16[128,16384]{1,0:T(8,128)(2,1)S(1)}, u32[]{:S(2)}, u32[]{:S(2)}) collective-permute-start(bf16[128,16384]{1,0:T(8,128)(2,1)} %bitcast.9), channel_id=1, source_target_pairs={{0,3},{1,0},{2,1},{3,2},{4,7},{5,4},{6,5},{7,6},{8,11},{9,8},{10,9... | collective-permute-start | bytes 12582920 | tf_op jit(solution)/shard_map/ppermute | solution.py:330
  22.0 0.0 collective-permute-start
  22.0 89.7 %collective-permute-done.1.right_ref = bf16[128,16384]{1,0:T(8,128)(2,1)S(1)} collective-permute-done((bf16[128,16384]{1,0:T(8,128)(2,1)}, bf16[128,16384]{1,0:T(8,128)(2,1)S(1)}, u32[]{:S(2)}, u32[]{:S(2)}) %collective-permute-start.1) | collective-permute-done | bytes 4194336 | tf_op jit(solution)/shard_map/ppermute | solution.py:330
  111.7 0.0 copy-start.3
  111.7 1.6 slice.9
  113.3 3.4 %collective-permute-start.3 = (bf16[64,16384]{1,0:T(8,128)(2,1)}, bf16[64,16384]{1,0:T(8,128)(2,1)S(1)}, u32[]{:S(2)}, u32[]{:S(2)}) collective-permute-start(bf16[64,16384]{1,0:T(8,128)(2,1)} %slice.9), channel_id=1, source_target_pairs={{0,3},{1,0},{2,1},{3,2},{4,7},{5,4},{6,5},{7,6},{8,11},{9,8},{10,9... | collective-permute-start | bytes 6291464 | tf_op jit(solution)/shard_map/ppermute | solution.py:332
  116.7 0.0 collective-permute-done.left_ref
  116.7 0.0 copy-start.4
  116.7 2.0 copy-done.4
  118.6 1.5 slice.8
  120.1 0.0 copy-done.3
  120.1 0.0 collective-permute-start.2
  120.1 40.5 %collective-permute-done.3.bottom_ref = bf16[64,16384]{1,0:T(8,128)(2,1)S(1)} collective-permute-done((bf16[64,16384]{1,0:T(8,128)(2,1)}, bf16[64,16384]{1,0:T(8,128)(2,1)S(1)}, u32[]{:S(2)}, u32[]{:S(2)}) %collective-permute-start.3) | collective-permute-done | bytes 2097184 | tf_op jit(solution)/shard_map/ppermute | solution.py:332
  160.6 0.0 copy-start.5
  160.6 6.6 %collective-permute-done.2.top_ref = bf16[64,16384]{1,0:T(8,128)(2,1)} collective-permute-done((bf16[64,16384]{1,0:T(8,128)(2,1)}, bf16[64,16384]{1,0:T(8,128)(2,1)}, u32[]{:S(2)}, u32[]{:S(2)}) %collective-permute-start.2) | collective-permute-done | bytes 2097184 | tf_op jit(solution)/shard_map/ppermute | solution.py:331
  167.2 0.0 copy-done.5
  167.2 0.0 copy-done.2
  167.2 10.9 %collect.1 = (bf16[512,16384]{1,0:T(8,128)(2,1)}, bf16[512,3072]{1,0:T(8,128)(2,1)S(1)}, bf16[128,512]{1,0:T(8,128)(2,1)S(1)}) custom-call(s32[1]{0:T(128)} %bitcast.amp_ref, s32[1,128]{1,0:T(1,128)S(1)} %bitcast.7, bf16[128,16384]{1,0:T(8,128)(2,1)} %bitcast.11, bf16[128,16384]{1,0:T(8,128)(2,1)} %copy-done.4, bf16[128,16384]{1,0:T(8,128)(2,1)} %copy-done.3, ...), custom_call_target="tpu_custom_call" | custom-call | bytes 33554432 | tf_op jit(solution)/shard_map/collect/pallas_call | solution.py:139
  178.1 0.0 copy-start
  178.1 0.6 copy-done
  178.8 26.4 %all-to-all-done = bf16[64,8,8192]{2,1,0:T(8,128)(2,1)} async-done(((bf16[64,8,8192]{2,1,0:T(8,128)(2,1)}), bf16[64,8,8192]{2,1,0:T(8,128)(2,1)}, u32[]{:S(2)}, u32[]{:S(2)}) %all-to-all-start) | async-done | bytes 8388640 | tf_op jit(solution)/shard_map/all_to_all | solution.py:340
  205.2 8.6 %multiply.1 = s16[64,4,640]{2,1,0:T(4,128)(2,1)S(1)} custom-call(bf16[512,8192]{1,0:T(8,128)(2,1)} %bitcast.5.rows_ref, bf16[512,16384]{1,0:T(8,128)(2,1)} %get-tuple-element.9.amps_ref, bf16[512,3072]{1,0:T(8,128)(2,1)S(1)} %get-tuple-element.10.kept_ref), custom_call_target="tpu_custom_call" | custom-call | flops 4294967296 | bytes 25165824 | tf_op jit(solution)/shard_map/multiply/pallas_call | solution.py:242
  213.8 18.9 %all_to_all.10.lines_ref = s16[64,4,640]{2,1,0:T(4,128)(2,1)S(1)} all-to-all(s16[64,4,640]{2,1,0:T(4,128)(2,1)S(1)} %multiply.1), channel_id=1, replica_groups=mesh['kblk'=64,'amp'=4] {'kblk'}, dimensions={0} | all-to-all | bytes 655360 | tf_op jit(solution)/shard_map/all_to_all | solution.py:344
  232.8 1.9 pick.1
Async XLA Ops:
  0.0 0.7 copy-start.1
  6.0 199.1 %all-to-all-start = ((bf16[64,8,8192]{2,1,0:T(8,128)(2,1)}), bf16[64,8,8192]{2,1,0:T(8,128)(2,1)}, u32[]{:S(2)}, u32[]{:S(2)}) async-start(bf16[64,8,8192]{2,1,0:T(8,128)(2,1)} %bitcast.8), calls=%async_computation | async-start | bytes 16777216 | tf_op jit(solution)/shard_map/all_to_all | solution.py:340
  19.4 147.8 %copy-start.2 = (s32[128,1]{0,1:T(1,128)S(1)}, s32[128,1]{0,1:T(1,128)}, u32[]{:S(2)}) copy-start(s32[128,1]{0,1:T(1,128)} %param.4) | copy-start | bytes 1540
  19.4 92.3 %collective-permute-start.1 = (bf16[128,16384]{1,0:T(8,128)(2,1)}, bf16[128,16384]{1,0:T(8,128)(2,1)S(1)}, u32[]{:S(2)}, u32[]{:S(2)}) collective-permute-start(bf16[128,16384]{1,0:T(8,128)(2,1)} %bitcast.9), channel_id=1, source_target_pairs={{0,3},{1,0},{2,1},{3,2},{4,7},{5,4},{6,5},{7,6},{8,11},{9,8},{10,9... | collective-permute-start | bytes 12582920 | tf_op jit(solution)/shard_map/ppermute | solution.py:330
  22.0 94.7 %collective-permute-start = (bf16[128,16384]{1,0:T(8,128)(2,1)}, bf16[128,16384]{1,0:T(8,128)(2,1)S(1)}, u32[]{:S(2)}, u32[]{:S(2)}) collective-permute-start(bf16[128,16384]{1,0:T(8,128)(2,1)} %bitcast.10), channel_id=1, source_target_pairs={{0,1},{1,2},{2,3},{3,0},{4,5},{5,6},{6,7},{7,4},{8,9},{9,10},{10,1... | collective-permute-start | bytes 12582920 | tf_op jit(solution)/shard_map/ppermute | solution.py:330
  111.7 8.4 %copy-start.3 = (bf16[128,16384]{1,0:T(8,128)(2,1)}, bf16[128,16384]{1,0:T(8,128)(2,1)S(1)}, u32[]{:S(2)}) copy-start(bf16[128,16384]{1,0:T(8,128)(2,1)S(1)} %collective-permute-done.1.right_ref) | copy-start | bytes 12582916
  113.3 47.4 %collective-permute-start.3 = (bf16[64,16384]{1,0:T(8,128)(2,1)}, bf16[64,16384]{1,0:T(8,128)(2,1)S(1)}, u32[]{:S(2)}, u32[]{:S(2)}) collective-permute-start(bf16[64,16384]{1,0:T(8,128)(2,1)} %slice.9), channel_id=1, source_target_pairs={{0,3},{1,0},{2,1},{3,2},{4,7},{5,4},{6,5},{7,6},{8,11},{9,8},{10,9... | collective-permute-start | bytes 6291464 | tf_op jit(solution)/shard_map/ppermute | solution.py:332
  116.7 2.0 copy-start.4
  120.1 47.1 %collective-permute-start.2 = (bf16[64,16384]{1,0:T(8,128)(2,1)}, bf16[64,16384]{1,0:T(8,128)(2,1)}, u32[]{:S(2)}, u32[]{:S(2)}) collective-permute-start(bf16[64,16384]{1,0:T(8,128)(2,1)} %slice.8), channel_id=1, source_target_pairs={{0,1},{1,2},{2,3},{3,0},{4,5},{5,6},{6,7},{7,4},{8,9},{9,10},{10,1... | collective-permute-start | bytes 6291464 | tf_op jit(solution)/shard_map/ppermute | solution.py:331
  160.6 6.6 %copy-start.5 = (bf16[64,16384]{1,0:T(8,128)(2,1)}, bf16[64,16384]{1,0:T(8,128)(2,1)S(1)}, u32[]{:S(2)}) copy-start(bf16[64,16384]{1,0:T(8,128)(2,1)S(1)} %collective-permute-done.3.bottom_ref) | copy-start | bytes 6291460
  178.1 0.6 copy-start

commit v12 on v11

--- a/solution.py
+++ b/solution.py
@@ -11,7 +11,7 @@
 LANES = 128
 BLOCK = 2 * CAP
 PLACE_BLOCKS = (1024, 2048, 2048, 2048, 1024)
-MULTIPLY_BLOCK = 1024
+MULTIPLY_BLOCK = 2048
 HEAD = 1536
 
 

time: 235 us -> 235 us (level)
  no operation moved by 1% of the time
where the time goes in v12:
time: 235 us
  waiting for transfers between devices  163 us (69%)
  Pallas kernels  27.3 us (12%)
  starting transfers between devices  19.3 us (8%)
  blocking collectives  19 us (8%)
  local copies, waits for them, and re-layouts  6.28 us (3%)
    ppermute x1, waiting for transfers between devices, body(): lax.ppermute(mine, 'amp', back)  89.7 us
    ppermute x1, waiting for transfers between devices, body(): bottom = lax.ppermute(right[middle:], 'amp', back)  40.5 us
    all_to_all x1, waiting for transfers between devices, body(): lax.all_to_all(placed.reshape(peers, BLOCK, width), 'kblk', split_axis=0,...  26.4 us
    all_to_all x1, blocking collectives, body(): lax.all_to_all(values, 'kblk', split_axis=0, concat_axis=0, tiled=True)  19 us
    all_to_all x1, starting transfers between devices, body(): lax.all_to_all(placed.reshape(peers, BLOCK, width), 'kblk', split_axis=0,...  13.4 us
    pallas_call x1, Pallas kernels, collect(): pl.pallas_call(collect_kernel, in_specs=[whole_in(pltpu.SMEM), whole_in(p...  10.9 us
    pallas_call x1, Pallas kernels, multiply(): pl.pallas_call(multiply_kernel, in_specs=[whole_in(pl.ANY), whole_in(pl.A...  9.12 us
    ppermute x1, waiting for transfers between devices, body(): top = lax.ppermute(left[:middle], 'amp', ahead)  6.56 us
  transfers between devices with their start and end apart: 5, of which 4 were waited for; matrix products, arithmetic and copies ran while one was open for 1% of the time, Pallas kernels for 5%

profile of v12, /device:TPU:1, one launch (start us, length us, event | category | flops | bytes accessed | tf_op | source)
XLA Modules:
  0.0 235.2 jit_solution(8653228511378663377)
XLA Ops:
  0.0 0.0 copy-start.1
  0.0 0.7 copy-done.1
  0.7 5.4 %place.1 = bf16[512,8192]{1,0:T(8,128)(2,1)} custom-call(s32[1]{0:T(128)} %bitcast.3.swap_ref, s32[1,128]{1,0:T(1,128)S(1)} %bitcast.6, bf16[128,16384]{1,0:T(8,128)(2,1)} %integrals_ref.1), custom_call_target="tpu_custom_call" | custom-call | flops 2147483648 | bytes 12582912 | tf_op jit(solution)/shard_map/place/pallas_call | solution.py:76
  6.0 13.4 %all-to-all-start = ((bf16[64,8,8192]{2,1,0:T(8,128)(2,1)}), bf16[64,8,8192]{2,1,0:T(8,128)(2,1)}, u32[]{:S(2)}, u32[]{:S(2)}) async-start(bf16[64,8,8192]{2,1,0:T(8,128)(2,1)} %bitcast.8), calls=%async_computation | async-start | bytes 16777216 | tf_op jit(solution)/shard_map/all_to_all | solution.py:340
  19.4 0.0 copy-start.2
  19.4 2.6 %collective-permute-start.1 = (bf16[128,16384]{1,0:T(8,128)(2,1)}, bf16[128,16384]{1,0:T(8,128)(2,1)S(1)}, u32[]{:S(2)}, u32[]{:S(2)}) collective-permute-start(bf16[128,16384]{1,0:T(8,128)(2,1)} %bitcast.9), channel_id=1, source_target_pairs={{0,3},{1,0},{2,1},{3,2},{4,7},{5,4},{6,5},{7,6},{8,11},{9,8},{10,9... | collective-permute-start | bytes 12582920 | tf_op jit(solution)/shard_map/ppermute | solution.py:330
  22.0 0.0 collective-permute-start
  22.0 89.7 %collective-permute-done.1.right_ref = bf16[128,16384]{1,0:T(8,128)(2,1)S(1)} collective-permute-done((bf16[128,16384]{1,0:T(8,128)(2,1)}, bf16[128,16384]{1,0:T(8,128)(2,1)S(1)}, u32[]{:S(2)}, u32[]{:S(2)}) %collective-permute-start.1) | collective-permute-done | bytes 4194336 | tf_op jit(solution)/shard_map/ppermute | solution.py:330
  111.7 0.0 copy-start.3
  111.7 1.6 slice.9
  113.3 3.4 %collective-permute-start.3 = (bf16[64,16384]{1,0:T(8,128)(2,1)}, bf16[64,16384]{1,0:T(8,128)(2,1)S(1)}, u32[]{:S(2)}, u32[]{:S(2)}) collective-permute-start(bf16[64,16384]{1,0:T(8,128)(2,1)} %slice.9), channel_id=1, source_target_pairs={{0,3},{1,0},{2,1},{3,2},{4,7},{5,4},{6,5},{7,6},{8,11},{9,8},{10,9... | collective-permute-start | bytes 6291464 | tf_op jit(solution)/shard_map/ppermute | solution.py:332
  116.7 0.0 collective-permute-done.left_ref
  116.7 0.0 copy-start.4
  116.7 2.0 copy-done.4
  118.6 1.5 slice.8
  120.1 0.0 copy-done.3
  120.1 0.0 collective-permute-start.2
  120.1 40.5 %collective-permute-done.3.bottom_ref = bf16[64,16384]{1,0:T(8,128)(2,1)S(1)} collective-permute-done((bf16[64,16384]{1,0:T(8,128)(2,1)}, bf16[64,16384]{1,0:T(8,128)(2,1)S(1)}, u32[]{:S(2)}, u32[]{:S(2)}) %collective-permute-start.3) | collective-permute-done | bytes 2097184 | tf_op jit(solution)/shard_map/ppermute | solution.py:332
  160.6 0.0 copy-start.5
  160.6 6.6 %collective-permute-done.2.top_ref = bf16[64,16384]{1,0:T(8,128)(2,1)} collective-permute-done((bf16[64,16384]{1,0:T(8,128)(2,1)}, bf16[64,16384]{1,0:T(8,128)(2,1)}, u32[]{:S(2)}, u32[]{:S(2)}) %collective-permute-start.2) | collective-permute-done | bytes 2097184 | tf_op jit(solution)/shard_map/ppermute | solution.py:331
  167.2 0.0 copy-done.5
  167.2 0.0 copy-done.2
  167.2 10.9 %collect.1 = (bf16[512,16384]{1,0:T(8,128)(2,1)}, bf16[512,3072]{1,0:T(8,128)(2,1)S(1)}, bf16[128,512]{1,0:T(8,128)(2,1)S(1)}) custom-call(s32[1]{0:T(128)} %bitcast.amp_ref, s32[1,128]{1,0:T(1,128)S(1)} %bitcast.7, bf16[128,16384]{1,0:T(8,128)(2,1)} %bitcast.11, bf16[128,16384]{1,0:T(8,128)(2,1)} %copy-done.4, bf16[128,16384]{1,0:T(8,128)(2,1)} %copy-done.3, ...), custom_call_target="tpu_custom_call" | custom-call | bytes 33554432 | tf_op jit(solution)/shard_map/collect/pallas_call | solution.py:139
  178.1 0.0 copy-start
  178.1 0.6 copy-done
  178.8 26.4 %all-to-all-done = bf16[64,8,8192]{2,1,0:T(8,128)(2,1)} async-done(((bf16[64,8,8192]{2,1,0:T(8,128)(2,1)}), bf16[64,8,8192]{2,1,0:T(8,128)(2,1)}, u32[]{:S(2)}, u32[]{:S(2)}) %all-to-all-start) | async-done | bytes 8388640 | tf_op jit(solution)/shard_map/all_to_all | solution.py:340
  205.2 9.1 %multiply.1 = s16[64,4,640]{2,1,0:T(4,128)(2,1)S(1)} custom-call(bf16[512,8192]{1,0:T(8,128)(2,1)} %bitcast.5.rows_ref, bf16[512,16384]{1,0:T(8,128)(2,1)} %get-tuple-element.9.amps_ref, bf16[512,3072]{1,0:T(8,128)(2,1)S(1)} %get-tuple-element.10.kept_ref), custom_call_target="tpu_custom_call" | custom-call | flops 4294967296 | bytes 25165824 | tf_op jit(solution)/shard_map/multiply/pallas_call | solution.py:242
  214.3 19.0 %all_to_all.10.lines_ref = s16[64,4,640]{2,1,0:T(4,128)(2,1)S(1)} all-to-all(s16[64,4,640]{2,1,0:T(4,128)(2,1)S(1)} %multiply.1), channel_id=1, replica_groups=mesh['kblk'=64,'amp'=4] {'kblk'}, dimensions={0} | all-to-all | bytes 655360 | tf_op jit(solution)/shard_map/all_to_all | solution.py:344
  233.3 1.9 pick.1
Async XLA Ops:
  0.0 0.7 copy-start.1
  6.0 199.1 %all-to-all-start = ((bf16[64,8,8192]{2,1,0:T(8,128)(2,1)}), bf16[64,8,8192]{2,1,0:T(8,128)(2,1)}, u32[]{:S(2)}, u32[]{:S(2)}) async-start(bf16[64,8,8192]{2,1,0:T(8,128)(2,1)} %bitcast.8), calls=%async_computation | async-start | bytes 16777216 | tf_op jit(solution)/shard_map/all_to_all | solution.py:340
  19.4 147.8 %copy-start.2 = (s32[128,1]{0,1:T(1,128)S(1)}, s32[128,1]{0,1:T(1,128)}, u32[]{:S(2)}) copy-start(s32[128,1]{0,1:T(1,128)} %param.4) | copy-start | bytes 1540
  19.4 92.3 %collective-permute-start.1 = (bf16[128,16384]{1,0:T(8,128)(2,1)}, bf16[128,16384]{1,0:T(8,128)(2,1)S(1)}, u32[]{:S(2)}, u32[]{:S(2)}) collective-permute-start(bf16[128,16384]{1,0:T(8,128)(2,1)} %bitcast.9), channel_id=1, source_target_pairs={{0,3},{1,0},{2,1},{3,2},{4,7},{5,4},{6,5},{7,6},{8,11},{9,8},{10,9... | collective-permute-start | bytes 12582920 | tf_op jit(solution)/shard_map/ppermute | solution.py:330
  22.0 94.7 %collective-permute-start = (bf16[128,16384]{1,0:T(8,128)(2,1)}, bf16[128,16384]{1,0:T(8,128)(2,1)S(1)}, u32[]{:S(2)}, u32[]{:S(2)}) collective-permute-start(bf16[128,16384]{1,0:T(8,128)(2,1)} %bitcast.10), channel_id=1, source_target_pairs={{0,1},{1,2},{2,3},{3,0},{4,5},{5,6},{6,7},{7,4},{8,9},{9,10},{10,1... | collective-permute-start | bytes 12582920 | tf_op jit(solution)/shard_map/ppermute | solution.py:330
  111.7 8.4 %copy-start.3 = (bf16[128,16384]{1,0:T(8,128)(2,1)}, bf16[128,16384]{1,0:T(8,128)(2,1)S(1)}, u32[]{:S(2)}) copy-start(bf16[128,16384]{1,0:T(8,128)(2,1)S(1)} %collective-permute-done.1.right_ref) | copy-start | bytes 12582916
  113.3 47.4 %collective-permute-start.3 = (bf16[64,16384]{1,0:T(8,128)(2,1)}, bf16[64,16384]{1,0:T(8,128)(2,1)S(1)}, u32[]{:S(2)}, u32[]{:S(2)}) collective-permute-start(bf16[64,16384]{1,0:T(8,128)(2,1)} %slice.9), channel_id=1, source_target_pairs={{0,3},{1,0},{2,1},{3,2},{4,7},{5,4},{6,5},{7,6},{8,11},{9,8},{10,9... | collective-permute-start | bytes 6291464 | tf_op jit(solution)/shard_map/ppermute | solution.py:332
  116.7 2.0 copy-start.4
  120.1 47.1 %collective-permute-start.2 = (bf16[64,16384]{1,0:T(8,128)(2,1)}, bf16[64,16384]{1,0:T(8,128)(2,1)}, u32[]{:S(2)}, u32[]{:S(2)}) collective-permute-start(bf16[64,16384]{1,0:T(8,128)(2,1)} %slice.8), channel_id=1, source_target_pairs={{0,1},{1,2},{2,3},{3,0},{4,5},{5,6},{6,7},{7,4},{8,9},{9,10},{10,1... | collective-permute-start | bytes 6291464 | tf_op jit(solution)/shard_map/ppermute | solution.py:331
  160.6 6.6 %copy-start.5 = (bf16[64,16384]{1,0:T(8,128)(2,1)}, bf16[64,16384]{1,0:T(8,128)(2,1)S(1)}, u32[]{:S(2)}) copy-start(bf16[64,16384]{1,0:T(8,128)(2,1)S(1)} %collective-permute-done.3.bottom_ref) | copy-start | bytes 6291460
  178.1 0.6 copy-start
